TPU v7x, 512 devices: a whole 4x4x16 slice. The times are simulated.
512 devices in a mesh: seq: 32 (over y, x, core), section: 16 (over z).
Axes of the slice: x: 4, y: 4, z: 16, core: 2. Of those that a mesh axis runs over, the one named last changes fastest.
Arguments:
- slabs: bfloat16 [16, 6144, 2048], P('section', 'seq'), may hold values from -6 to 6
- fresh: bfloat16 [1, 6144, 2048], P(None, 'seq'), may hold values from -6 to 6
- norm_gain: bfloat16 [16, 2048], P('section'), may hold values from 0.099609375 to 1.8984375
- qkv_proj: bfloat16 [16, 3, 16, 128, 128], P('section'), may hold values from -8 to 8
- o_proj: bfloat16 [16, 16, 128, 128], P('section'), may hold values from -0.5 to 0.5
- offsets: int32 [16, 16], P('section'), may hold values from 0 to 15
Outputs:
- result: bfloat16 [16, 6144, 2048], P('section', 'seq')
All inputs are finite; a program needn't handle non-finite values.
Results may differ from a plain program's by a relative error of at most 0.023.
The roundings to bfloat16 on the way count: a program that leaves them out, or rounds other values in their place, can miss the bound.
Values may be sent and summed in bfloat16 or wider, within the bound.
No kernel may reach another device: no remote copies, remote signals or barrier semaphores. Data moves between devices by JAX's collectives and lax.ppermute only.
A program may use at most 64 MiB of HBM per device.

v0:
```python
import math

import jax
import jax.numpy as jnp
from jax import lax
from jax.sharding import PartitionSpec as P

RATE = 16
TICKS = 2


eps = 1e-06
neg_big = -1e30


def from_behind(value, axis, steps):
    count = lax.axis_size(axis)
    initial, last = (max(0, -steps), min(count, count - steps))
    return lax.ppermute(value, axis, [(source, source + steps) for source in range(initial, last)])


def prepare(state, gain, qkv_weights):
    rows = state.shape[0]
    heads, depth = (qkv_weights.shape[1], qkv_weights.shape[2])
    widened = state.astype(jnp.float32)
    scaled = widened * lax.rsqrt(jnp.mean(widened * widened, axis=-1, keepdims=True) + eps)
    normed = (scaled * gain.astype(jnp.float32)).astype(jnp.bfloat16).reshape(rows, heads, depth)
    stacked = jnp.einsum(
        "shd,chde->cshe", normed, qkv_weights, preferred_element_type=jnp.float32
    ).astype(jnp.bfloat16)
    return (stacked[0], stacked[1], stacked[2])


def dilate(field, offsets, rate):
    rows, heads, depth = field.shape
    grouped = field.reshape(rows // rate, rate, heads, depth)
    phase = (lax.broadcasted_iota(jnp.int32, (rate, heads), 0) == offsets[None, :]).astype(
        field.dtype
    )
    return jnp.sum(grouped * phase[None, :, :, None], axis=1)


def attend(queries, keys, values, mask):
    scale = 1.0 / math.sqrt(queries.shape[-1])
    scores = jnp.einsum("qhd,khd->qhk", queries, keys, preferred_element_type=jnp.float32) * scale
    scores = jnp.where(mask[:, None, :], scores, neg_big)
    top = jnp.max(scores, axis=-1, keepdims=True)
    expo = jnp.exp(scores - top)
    total = jnp.sum(expo, axis=-1)
    summed = jnp.einsum(
        "qhk,khd->qhd", expo.astype(jnp.bfloat16), values, preferred_element_type=jnp.float32
    )
    return (summed / total[:, :, None]).astype(jnp.bfloat16)


def fetch_panels(key, value, offsets, levels):
    own = jnp.stack([dilate(key, offsets, RATE), dilate(value, offsets, RATE)])
    panels = []
    for level in range(levels):
        panels.append(from_behind(own, "seq", 1 << level))
    return panels


def layer_rows(state, query, key, value, panels, o_weights, first_row, count, place):
    rows = key.shape[0]
    block = min(512, count)
    size = min(block, first_row + count)
    causal = 0 + lax.broadcasted_iota(jnp.int32, (size, rows), 0) >= lax.broadcasted_iota(
        jnp.int32, (size, rows), 1
    )
    keys = [key]
    vals = [value]
    masks = [causal]
    for level, panel in enumerate(panels):
        keys.append(panel[0])
        vals.append(panel[1])
        masks.append(jnp.broadcast_to(place >= 1 << level, (size, panel.shape[1])))
    pieces = attend(
        query,
        jnp.concatenate(keys, axis=0),
        jnp.concatenate(vals, axis=0),
        jnp.concatenate(masks, axis=1),
    )
    mixed = jnp.einsum("qhd,hde->qhe", pieces, o_weights, preferred_element_type=jnp.float32)
    rows_in = state.astype(jnp.float32)
    return (rows_in + mixed.reshape(count, -1)).astype(jnp.bfloat16)


def on_device(slabs, fresh, norm_gain, qkv_proj, o_proj, offsets):
    state = slabs[0]
    rows = state.shape[0]
    is_first = lax.axis_index("section") == 0
    place = lax.axis_index("seq")
    levels = (lax.axis_size("seq") - 1).bit_length()
    output = state
    for tick in range(TICKS):
        query, key, value = prepare(state, norm_gain[0], qkv_proj[0])
        panels = fetch_panels(key, value, offsets[0], levels)
        is_last = tick == TICKS - 1
        output = layer_rows(state, query, key, value, panels, o_proj[0], 0, rows, place)
        if not is_last:
            moved = from_behind(output, "section", 1)
        if not is_last:
            state = jnp.where(is_first, fresh[tick], moved)
    return output[None]


def solution(mesh):
    in_specs = (
        P("section", "seq", None),
        P(None, "seq", None),
        P("section", None),
        P("section", None, None, None, None),
        P("section", None, None, None),
        P("section", None),
    )
    out_specs = P("section", "seq", None)
    return jax.shard_map(
        on_device, mesh=mesh, in_specs=in_specs, out_specs=out_specs, check_vma=False
    )
```

profile of v0, /device:TPU:401, one launch (start us, length us, event | category | flops | bytes accessed | tf_op | source)
XLA Modules:
  0.0 137.8 jit_solution(8427727831040167840)
XLA Ops:
  0.0 1.4 %convert_bitcast_fusion.2 = f32[24,8,16,128]{3,1,2,0:T(8,128)S(1)} fusion(bf16[1,192,2048]{2,1,0:T(8,128)(2,1)} %param.6), kind=kLoop, calls=%fused_computation.15 | loop fusion | flops 393216 | bytes 2359296
  2.2 1.1 convert_bitcast_fusion.1
  3.3 1.9 %slice_bitcast_fusion.26 = (bf16[192,16,128]{2,0,1:T(8,128)(2,1)}, bf16[192,16,128]{2,0,1:T(8,128)(2,1)}, bf16[1,192,16,128]{3,1,0,2:T(8,128)(2,1)S(1)}, bf16[1,192,16,128]{3,1,0,2:T(8,128)(2,1)S(1)}) fusion(bf16[3,192,16,128]{3,1,0,2:T(8,128)(2,1)S(1)} %convert_bitcast_fusion.1), kind=kLoop, calls=%fused_computation.96 | loop fusion | bytes 4718592 | tf_op jit(solution)/shard_map/squeeze | solution.py:31
  5.3 1.1 multiply_reduce_fusion.3
  6.4 3.7 %collective-permute-start = (bf16[2,12,16,128]{3,1,2,0:T(8,128)(2,1)S(1)}, bf16[2,12,16,128]{3,1,2,0:T(8,128)(2,1)S(1)}, u32[]{:S(2)}, u32[]{:S(2)}) collective-permute-start(bf16[2,12,16,128]{3,1,2,0:T(8,128)(2,1)S(1)} %pad_maximum_fusion), channel_id=1, source_target_pairs={{0,16},{16,32},{32,48},{48,64},{64,80},{80,96},{96,112},{112,128},... | collective-permute-start | bytes 294920 | tf_op jit(solution)/shard_map/ppermute | solution.py:19
  10.1 3.1 %collective-permute-start.1 = (bf16[2,12,16,128]{3,1,2,0:T(8,128)(2,1)S(1)}, bf16[2,12,16,128]{3,1,2,0:T(8,128)(2,1)S(1)}, u32[]{:S(2)}, u32[]{:S(2)}) collective-permute-start(bf16[2,12,16,128]{3,1,2,0:T(8,128)(2,1)S(1)} %pad_maximum_fusion), channel_id=1, source_target_pairs={{0,32},{16,48},{32,64},{48,80},{64,96},{80,112},{96,128},{112,144}... | collective-permute-start | bytes 294920 | tf_op jit(solution)/shard_map/ppermute | solution.py:19
  13.2 4.1 %collective-permute-start.2 = (bf16[2,12,16,128]{3,1,2,0:T(8,128)(2,1)S(1)}, bf16[2,12,16,128]{3,1,2,0:T(8,128)(2,1)S(1)}, u32[]{:S(2)}, u32[]{:S(2)}) collective-permute-start(bf16[2,12,16,128]{3,1,2,0:T(8,128)(2,1)S(1)} %pad_maximum_fusion), channel_id=1, source_target_pairs={{0,64},{16,80},{32,96},{48,112},{64,128},{80,144},{96,160},{112,17... | collective-permute-start | bytes 294920 | tf_op jit(solution)/shard_map/ppermute | solution.py:19
  17.3 2.0 %collective-permute-start.3 = (bf16[2,12,16,128]{3,1,2,0:T(8,128)(2,1)S(1)}, bf16[2,12,16,128]{3,1,2,0:T(8,128)(2,1)S(1)}, u32[]{:S(2)}, u32[]{:S(2)}) collective-permute-start(bf16[2,12,16,128]{3,1,2,0:T(8,128)(2,1)S(1)} %pad_maximum_fusion), channel_id=1, source_target_pairs={{0,128},{16,144},{32,160},{48,176},{64,192},{80,208},{96,224},{112... | collective-permute-start | bytes 294920 | tf_op jit(solution)/shard_map/ppermute | solution.py:19
  19.3 1.3 collective-permute-start.4
  21.0 0.6 slice_bitcast_fusion.18
  21.6 0.7 slice_bitcast_fusion.17
  22.5 0.7 slice_bitcast_fusion.16
  23.2 2.4 %collective-permute-done.3 = bf16[2,12,16,128]{3,1,2,0:T(8,128)(2,1)S(1)} collective-permute-done((bf16[2,12,16,128]{3,1,2,0:T(8,128)(2,1)S(1)}, bf16[2,12,16,128]{3,1,2,0:T(8,128)(2,1)S(1)}, u32[]{:S(2)}, u32[]{:S(2)}) %collective-permute-start.3) | collective-permute-done | bytes 98336 | tf_op jit(solution)/shard_map/ppermute | solution.py:19
  25.5 0.6 slice_bitcast_fusion.15
  26.2 0.5 collective-permute-done.4
  26.6 0.7 slice_bitcast_fusion.14
  27.3 8.2 %concatenate.18 = bf16[252,16,128]{2,0,1:T(8,128)(2,1)S(1)} concatenate(bf16[192,16,128]{2,0,1:T(8,128)(2,1)} %get-tuple-element.15, bf16[12,16,128]{2,0,1:T(8,128)(2,1)} %get-tuple-element.37, bf16[12,16,128]{2,0,1:T(8,128)(2,1)} %get-tuple-element.35, bf16[12,16,128]{2,0,1:T(8,128)(2,1)} %get-tuple-element.33, bf16[12,16,128]{2,0,1:T(8,128)(2,1)} %get-tuple-element.31, ...), dimensions={0} | concatenate | bytes 2064384 | tf_op jit(solution)/shard_map/concatenate | solution.py:80
  35.5 2.1 %fusion.4 = (f32[192,16]{0,1:T(8,128)S(1)}, f32[16,252,192]{1,2,0:T(8,128)S(1)}) fusion(pred[192,252]{1,0:T(8,128)(4,1)S(1)} %concatenate.17, bf16[252,16,128]{2,0,1:T(8,128)(2,1)S(1)} %concatenate.18, bf16[3,192,16,128]{3,1,0,2:T(8,128)(2,1)} %copy-done.3), kind=kOutput, calls=%fused_computation.8 | convolution fusion | flops 200500224 | bytes 4975872 | tf_op jit(solution)/shard_map/qhd,khd->qhk/dot_general | solution.py:45
  37.7 1.6 %copy-done.2 = f32[16,252,192]{1,2,0:T(8,128)} copy-done((f32[16,252,192]{1,2,0:T(8,128)}, f32[16,252,192]{1,2,0:T(8,128)S(1)}, u32[]{:S(2)}) %copy-start.2) | copy-done | bytes 3096600
  39.3 2.1 %fusion = f32[192,16]{0,1:T(8,128)} fusion(f32[16,252,192]{1,2,0:T(8,128)S(1)} %get-tuple-element.40, f32[192,16]{0,1:T(8,128)S(1)} %get-tuple-element.39, pred[192,252]{1,0:T(8,128)(4,1)S(1)} %concatenate.17), kind=kLoop, calls=%fused_computation.4 | loop fusion | flops 3093504 | bytes 3169536 | tf_op jit(solution)/shard_map/reduce_sum | solution.py:49
  41.4 7.7 %concatenate.16 = bf16[252,16,128]{2,0,1:T(8,128)(2,1)} concatenate(bf16[192,16,128]{2,0,1:T(8,128)(2,1)S(1)} %copy-done.6, bf16[12,16,128]{2,0,1:T(8,128)(2,1)S(1)} %get-tuple-element.38, bf16[12,16,128]{2,0,1:T(8,128)(2,1)S(1)} %copy-done.9, bf16[12,16,128]{2,0,1:T(8,128)(2,1)S(1)} %copy-done.11, bf16[12,16,128]{2,0,1:T(8,128)(2,1)S(1)} %copy-done.13, ...), dimensions={0} | concatenate | bytes 2064384 | tf_op jit(solution)/shard_map/concatenate | solution.py:81
  49.1 4.7 %convolution_bitcast_fusion.1 = f32[16,24,8,128]{3,2,1,0:T(8,128)} fusion(bf16[252,16,128]{2,0,1:T(8,128)(2,1)} %concatenate.16, f32[16,252,192]{1,2,0:T(8,128)} %copy-done.2, f32[192,16]{0,1:T(8,128)S(1)} %get-tuple-element.39, pred[192,252]{1,0:T(8,128)(4,1)S(1)} %concatenate.17, f32[192,16]{0,1:T(8,128)} %fusion, bf16[1,16,128,128]{3,2,1,0:T(8,128)(2,1)} %param.10), kind=kOutput, calls=%fused_computation.43 | convolution fusion | flops 302727168 | bytes 6298880 | tf_op jit(solution)/shard_map/qhd,hde->qhe/dot_general | solution.py:84
  53.8 2.5 %fusion.9 = bf16[192,2048]{1,0:T(8,128)(2,1)} fusion(bf16[1,192,2048]{2,1,0:T(8,128)(2,1)S(1)} %copy-done.5, f32[16,24,8,128]{3,2,1,0:T(8,128)} %convolution_bitcast_fusion.1), kind=kLoop, calls=%fused_computation.20 | loop fusion | flops 1179648 | bytes 3145728 | tf_op jit(solution)/shard_map/convert_element_type | solution.py:86
  56.4 2.6 %collective-permute-start.5 = (bf16[192,2048]{1,0:T(8,128)(2,1)}, bf16[192,2048]{1,0:T(8,128)(2,1)}, u32[]{:S(2)}, u32[]{:S(2)}) collective-permute-start(bf16[192,2048]{1,0:T(8,128)(2,1)} %fusion.9), channel_id=1, source_target_pairs={{0,1},{1,2},{2,3},{3,4},{4,5},{5,6},{6,7},{7,8},{8,9},{9,10},{10,1... | collective-permute-start | bytes 2359304 | tf_op jit(solution)/shard_map/ppermute | solution.py:19
  59.0 17.7 %collective-permute-done.5 = bf16[192,2048]{1,0:T(8,128)(2,1)} collective-permute-done((bf16[192,2048]{1,0:T(8,128)(2,1)}, bf16[192,2048]{1,0:T(8,128)(2,1)}, u32[]{:S(2)}, u32[]{:S(2)}) %collective-permute-start.5) | collective-permute-done | bytes 786464 | tf_op jit(solution)/shard_map/ppermute | solution.py:19
  76.7 1.5 %fusion.10 = (f32[192]{0:T(256)S(1)}, bf16[192,2048]{1,0:T(8,128)(2,1)S(1)}) fusion(bf16[192,2048]{1,0:T(8,128)(2,1)} %collective-permute-done.5, bf16[1,192,2048]{2,1,0:T(8,128)(2,1)S(1)} %copy-done.8, pred[]{:T(512)S(6)} %eq.12), kind=kLoop, calls=%fused_computation.21 | loop fusion | flops 1572672 | bytes 2360065 | tf_op jit(solution)/shard_map/reduce_sum | solution.py:26
  78.7 0.8 convert_bitcast_fusion
  79.5 1.9 %slice_bitcast_fusion.24 = (bf16[192,16,128]{2,0,1:T(8,128)(2,1)}, bf16[192,16,128]{2,0,1:T(8,128)(2,1)}, bf16[1,192,16,128]{3,1,0,2:T(8,128)(2,1)S(1)}, bf16[1,192,16,128]{3,1,0,2:T(8,128)(2,1)S(1)}) fusion(bf16[3,192,16,128]{3,1,0,2:T(8,128)(2,1)S(1)} %convert_bitcast_fusion), kind=kLoop, calls=%fused_computation.94 | loop fusion | bytes 4718592 | tf_op jit(solution)/shard_map/squeeze | solution.py:31
  81.4 1.1 multiply_reduce_fusion.1
  82.5 8.4 %collective-permute-start.6 = (bf16[2,12,16,128]{3,1,2,0:T(8,128)(2,1)S(1)}, bf16[2,12,16,128]{3,1,2,0:T(8,128)(2,1)S(1)}, u32[]{:S(2)}, u32[]{:S(2)}) collective-permute-start(bf16[2,12,16,128]{3,1,2,0:T(8,128)(2,1)S(1)} %pad_maximum_fusion.1), channel_id=1, source_target_pairs={{0,16},{16,32},{32,48},{48,64},{64,80},{80,96},{96,112},{112,128},... | collective-permute-start | bytes 294920 | tf_op jit(solution)/shard_map/ppermute | solution.py:19
  90.9 1.9 %collective-permute-start.7 = (bf16[2,12,16,128]{3,1,2,0:T(8,128)(2,1)S(1)}, bf16[2,12,16,128]{3,1,2,0:T(8,128)(2,1)S(1)}, u32[]{:S(2)}, u32[]{:S(2)}) collective-permute-start(bf16[2,12,16,128]{3,1,2,0:T(8,128)(2,1)S(1)} %pad_maximum_fusion.1), channel_id=1, source_target_pairs={{0,32},{16,48},{32,64},{48,80},{64,96},{80,112},{96,128},{112,144}... | collective-permute-start | bytes 294920 | tf_op jit(solution)/shard_map/ppermute | solution.py:19
  92.8 2.7 %collective-permute-start.8 = (bf16[2,12,16,128]{3,1,2,0:T(8,128)(2,1)S(1)}, bf16[2,12,16,128]{3,1,2,0:T(8,128)(2,1)S(1)}, u32[]{:S(2)}, u32[]{:S(2)}) collective-permute-start(bf16[2,12,16,128]{3,1,2,0:T(8,128)(2,1)S(1)} %pad_maximum_fusion.1), channel_id=1, source_target_pairs={{0,64},{16,80},{32,96},{48,112},{64,128},{80,144},{96,160},{112,17... | collective-permute-start | bytes 294920 | tf_op jit(solution)/shard_map/ppermute | solution.py:19
  95.5 1.9 %collective-permute-start.9 = (bf16[2,12,16,128]{3,1,2,0:T(8,128)(2,1)S(1)}, bf16[2,12,16,128]{3,1,2,0:T(8,128)(2,1)S(1)}, u32[]{:S(2)}, u32[]{:S(2)}) collective-permute-start(bf16[2,12,16,128]{3,1,2,0:T(8,128)(2,1)S(1)} %pad_maximum_fusion.1), channel_id=1, source_target_pairs={{0,128},{16,144},{32,160},{48,176},{64,192},{80,208},{96,224},{112... | collective-permute-start | bytes 294920 | tf_op jit(solution)/shard_map/ppermute | solution.py:19
  97.4 1.5 %collective-permute-start.10 = (bf16[2,12,16,128]{3,1,2,0:T(8,128)(2,1)S(1)}, bf16[2,12,16,128]{3,1,2,0:T(8,128)(2,1)S(1)}, u32[]{:S(2)}, u32[]{:S(2)}) collective-permute-start(bf16[2,12,16,128]{3,1,2,0:T(8,128)(2,1)S(1)} %pad_maximum_fusion.1), channel_id=1, source_target_pairs={{0,256},{16,272},{32,288},{48,304},{64,320},{80,336},{96,352},{112... | collective-permute-start | bytes 294920 | tf_op jit(solution)/shard_map/ppermute | solution.py:19
  98.9 0.6 slice_bitcast_fusion.8
  99.5 0.7 slice_bitcast_fusion.7
  100.2 1.6 %collective-permute-done.8 = bf16[2,12,16,128]{3,1,2,0:T(8,128)(2,1)S(1)} collective-permute-done((bf16[2,12,16,128]{3,1,2,0:T(8,128)(2,1)S(1)}, bf16[2,12,16,128]{3,1,2,0:T(8,128)(2,1)S(1)}, u32[]{:S(2)}, u32[]{:S(2)}) %collective-permute-start.8) | collective-permute-done | bytes 98336 | tf_op jit(solution)/shard_map/ppermute | solution.py:19
  101.8 0.7 slice_bitcast_fusion.6
  102.4 5.7 %collective-permute-done.9 = bf16[2,12,16,128]{3,1,2,0:T(8,128)(2,1)S(1)} collective-permute-done((bf16[2,12,16,128]{3,1,2,0:T(8,128)(2,1)S(1)}, bf16[2,12,16,128]{3,1,2,0:T(8,128)(2,1)S(1)}, u32[]{:S(2)}, u32[]{:S(2)}) %collective-permute-start.9) | collective-permute-done | bytes 98336 | tf_op jit(solution)/shard_map/ppermute | solution.py:19
  108.1 0.6 slice_bitcast_fusion.5
  108.8 0.7 slice_bitcast_fusion.4
  109.4 8.2 %concatenate.20 = bf16[252,16,128]{2,0,1:T(8,128)(2,1)S(1)} concatenate(bf16[192,16,128]{2,0,1:T(8,128)(2,1)} %get-tuple-element.11, bf16[12,16,128]{2,0,1:T(8,128)(2,1)} %get-tuple-element.27, bf16[12,16,128]{2,0,1:T(8,128)(2,1)} %get-tuple-element.25, bf16[12,16,128]{2,0,1:T(8,128)(2,1)} %get-tuple-element.23, bf16[12,16,128]{2,0,1:T(8,128)(2,1)} %get-tuple-element.21, ...), dimensions={0} | concatenate | bytes 2064384 | tf_op jit(solution)/shard_map/concatenate | solution.py:80
  117.7 2.1 %fusion.5 = (f32[192,16]{0,1:T(8,128)S(1)}, f32[16,252,192]{1,2,0:T(8,128)S(1)}) fusion(pred[192,252]{1,0:T(8,128)(4,1)S(1)} %concatenate.17, bf16[252,16,128]{2,0,1:T(8,128)(2,1)S(1)} %concatenate.20, bf16[3,192,16,128]{3,1,0,2:T(8,128)(2,1)} %copy-done.4), kind=kOutput, calls=%fused_computation.9 | convolution fusion | flops 200500224 | bytes 4975872 | tf_op jit(solution)/shard_map/qhd,khd->qhk/dot_general | solution.py:45
  119.8 1.6 %copy-done.1 = f32[16,252,192]{1,2,0:T(8,128)} copy-done((f32[16,252,192]{1,2,0:T(8,128)}, f32[16,252,192]{1,2,0:T(8,128)S(1)}, u32[]{:S(2)}) %copy-start.1) | copy-done | bytes 3096600
  121.4 1.5 %fusion.2 = f32[192,16]{0,1:T(8,128)S(1)} fusion(f32[16,252,192]{1,2,0:T(8,128)S(1)} %get-tuple-element.42, f32[192,16]{0,1:T(8,128)S(1)} %get-tuple-element.41, pred[192,252]{1,0:T(8,128)(4,1)S(1)} %concatenate.17), kind=kLoop, calls=%fused_computation.6 | loop fusion | flops 3093504 | bytes 3169536 | tf_op jit(solution)/shard_map/reduce_sum | solution.py:49
  123.0 7.7 %concatenate.19 = bf16[252,16,128]{2,0,1:T(8,128)(2,1)} concatenate(bf16[192,16,128]{2,0,1:T(8,128)(2,1)S(1)} %copy-done.7, bf16[12,16,128]{2,0,1:T(8,128)(2,1)S(1)} %get-tuple-element.28, bf16[12,16,128]{2,0,1:T(8,128)(2,1)S(1)} %copy-done.10, bf16[12,16,128]{2,0,1:T(8,128)(2,1)S(1)} %copy-done.12, bf16[12,16,128]{2,0,1:T(8,128)(2,1)S(1)} %copy-done.14, ...), dimensions={0} | concatenate | bytes 2064384 | tf_op jit(solution)/shard_map/concatenate | solution.py:81
  130.7 4.7 %convolution_bitcast_fusion = f32[16,24,8,128]{3,2,1,0:T(8,128)} fusion(bf16[252,16,128]{2,0,1:T(8,128)(2,1)} %concatenate.19, f32[16,252,192]{1,2,0:T(8,128)} %copy-done.1, f32[192,16]{0,1:T(8,128)S(1)} %get-tuple-element.41, pred[192,252]{1,0:T(8,128)(4,1)S(1)} %concatenate.17, f32[192,16]{0,1:T(8,128)S(1)} %fusion.2, bf16[1,16,128,128]{3,2,1,0:T(8,128)(2,1)} %param.10), kind=kOutput, calls=%fused_computation.42 | convolution fusion | flops 302727168 | bytes 6298880 | tf_op jit(solution)/shard_map/qhd,hde->qhe/dot_general | solution.py:84
  135.4 2.5 %fusion.38 = bf16[1,192,2048]{2,1,0:T(8,128)(2,1)} fusion(f32[16,24,8,128]{3,2,1,0:T(8,128)} %convolution_bitcast_fusion, bf16[192,2048]{1,0:T(8,128)(2,1)S(1)} %get-tuple-element.10), kind=kLoop, calls=%fused_computation.47 | loop fusion | flops 1179648 | bytes 3145728 | tf_op jit(solution)/shard_map/broadcast_in_dim | solution.py:105
  (59 shorter events, 2.0 us)
Async XLA Ops:
  0.0 2.2 %copy-start = (bf16[1,3,16,128,128]{4,3,2,1,0:T(8,128)(2,1)S(1)}, bf16[1,3,16,128,128]{4,3,2,1,0:T(8,128)(2,1)}, u32[]{:S(2)}) copy-start(bf16[1,3,16,128,128]{4,3,2,1,0:T(8,128)(2,1)} %param.9) | copy-start | bytes 4718596
  0.0 1.5 %copy-start.5 = (bf16[1,192,2048]{2,1,0:T(8,128)(2,1)S(1)}, bf16[1,192,2048]{2,1,0:T(8,128)(2,1)}, u32[]{:S(2)}) copy-start(bf16[1,192,2048]{2,1,0:T(8,128)(2,1)} %param.6) | copy-start | bytes 2359300
  1.5 0.7 copy-start.17
  3.3 1.9 %copy-start.3 = (bf16[3,192,16,128]{3,1,0,2:T(8,128)(2,1)}, bf16[3,192,16,128]{3,1,0,2:T(8,128)(2,1)S(1)}, u32[]{:S(2)}) copy-start(bf16[3,192,16,128]{3,1,0,2:T(8,128)(2,1)S(1)} %convert_bitcast_fusion.1) | copy-start | bytes 7077892
  3.3 1.9 %copy-start.18 = (s32[1,16]{1,0:T(1,128)S(1)}, s32[1,16]{1,0:T(1,128)}, u32[]{:S(2)}) copy-start(s32[1,16]{1,0:T(1,128)} %param.11) | copy-start | bytes 196
  6.4 14.6 %collective-permute-start = (bf16[2,12,16,128]{3,1,2,0:T(8,128)(2,1)S(1)}, bf16[2,12,16,128]{3,1,2,0:T(8,128)(2,1)S(1)}, u32[]{:S(2)}, u32[]{:S(2)}) collective-permute-start(bf16[2,12,16,128]{3,1,2,0:T(8,128)(2,1)S(1)} %pad_maximum_fusion), channel_id=1, source_target_pairs={{0,16},{16,32},{32,48},{48,64},{64,80},{80,96},{96,112},{112,128},... | collective-permute-start | bytes 294920 | tf_op jit(solution)/shard_map/ppermute | solution.py:19
  10.1 11.5 %collective-permute-start.1 = (bf16[2,12,16,128]{3,1,2,0:T(8,128)(2,1)S(1)}, bf16[2,12,16,128]{3,1,2,0:T(8,128)(2,1)S(1)}, u32[]{:S(2)}, u32[]{:S(2)}) collective-permute-start(bf16[2,12,16,128]{3,1,2,0:T(8,128)(2,1)S(1)} %pad_maximum_fusion), channel_id=1, source_target_pairs={{0,32},{16,48},{32,64},{48,80},{64,96},{80,112},{96,128},{112,144}... | collective-permute-start | bytes 294920 | tf_op jit(solution)/shard_map/ppermute | solution.py:19
  13.2 9.3 %collective-permute-start.2 = (bf16[2,12,16,128]{3,1,2,0:T(8,128)(2,1)S(1)}, bf16[2,12,16,128]{3,1,2,0:T(8,128)(2,1)S(1)}, u32[]{:S(2)}, u32[]{:S(2)}) collective-permute-start(bf16[2,12,16,128]{3,1,2,0:T(8,128)(2,1)S(1)} %pad_maximum_fusion), channel_id=1, source_target_pairs={{0,64},{16,80},{32,96},{48,112},{64,128},{80,144},{96,160},{112,17... | collective-permute-start | bytes 294920 | tf_op jit(solution)/shard_map/ppermute | solution.py:19
  17.3 8.2 %collective-permute-start.3 = (bf16[2,12,16,128]{3,1,2,0:T(8,128)(2,1)S(1)}, bf16[2,12,16,128]{3,1,2,0:T(8,128)(2,1)S(1)}, u32[]{:S(2)}, u32[]{:S(2)}) collective-permute-start(bf16[2,12,16,128]{3,1,2,0:T(8,128)(2,1)S(1)} %pad_maximum_fusion), channel_id=1, source_target_pairs={{0,128},{16,144},{32,160},{48,176},{64,192},{80,208},{96,224},{112... | collective-permute-start | bytes 294920 | tf_op jit(solution)/shard_map/ppermute | solution.py:19
  19.3 7.3 %collective-permute-start.4 = (bf16[2,12,16,128]{3,1,2,0:T(8,128)(2,1)S(1)}, bf16[2,12,16,128]{3,1,2,0:T(8,128)(2,1)S(1)}, u32[]{:S(2)}, u32[]{:S(2)}) collective-permute-start(bf16[2,12,16,128]{3,1,2,0:T(8,128)(2,1)S(1)} %pad_maximum_fusion), channel_id=1, source_target_pairs={{0,256},{16,272},{32,288},{48,304},{64,320},{80,336},{96,352},{112... | collective-permute-start | bytes 294920 | tf_op jit(solution)/shard_map/ppermute | solution.py:19
  37.6 1.7 %copy-start.2 = (f32[16,252,192]{1,2,0:T(8,128)}, f32[16,252,192]{1,2,0:T(8,128)S(1)}, u32[]{:S(2)}) copy-start(f32[16,252,192]{1,2,0:T(8,128)S(1)} %get-tuple-element.40) | copy-start | bytes 9289732
  37.6 3.7 %copy-start.6 = (bf16[192,16,128]{2,0,1:T(8,128)(2,1)S(1)}, bf16[192,16,128]{2,0,1:T(8,128)(2,1)}, u32[]{:S(2)}) copy-start(bf16[192,16,128]{2,0,1:T(8,128)(2,1)} %get-tuple-element.16) | copy-start | bytes 2359300
  37.6 3.7 %copy-start.9 = (bf16[12,16,128]{2,0,1:T(8,128)(2,1)S(1)}, bf16[12,16,128]{2,0,1:T(8,128)(2,1)}, u32[]{:S(2)}) copy-start(bf16[12,16,128]{2,0,1:T(8,128)(2,1)} %get-tuple-element.36) | copy-start | bytes 147460
  37.7 3.7 %copy-start.11 = (bf16[12,16,128]{2,0,1:T(8,128)(2,1)S(1)}, bf16[12,16,128]{2,0,1:T(8,128)(2,1)}, u32[]{:S(2)}) copy-start(bf16[12,16,128]{2,0,1:T(8,128)(2,1)} %get-tuple-element.34) | copy-start | bytes 147460
  37.7 3.7 %copy-start.13 = (bf16[12,16,128]{2,0,1:T(8,128)(2,1)S(1)}, bf16[12,16,128]{2,0,1:T(8,128)(2,1)}, u32[]{:S(2)}) copy-start(bf16[12,16,128]{2,0,1:T(8,128)(2,1)} %get-tuple-element.32) | copy-start | bytes 147460
  37.7 3.7 %copy-start.15 = (bf16[12,16,128]{2,0,1:T(8,128)(2,1)S(1)}, bf16[12,16,128]{2,0,1:T(8,128)(2,1)}, u32[]{:S(2)}) copy-start(bf16[12,16,128]{2,0,1:T(8,128)(2,1)} %get-tuple-element.30) | copy-start | bytes 147460
  53.8 22.9 %copy-start.8 = (bf16[1,192,2048]{2,1,0:T(8,128)(2,1)S(1)}, bf16[1,192,2048]{2,1,0:T(8,128)(2,1)}, u32[]{:S(2)}) copy-start(bf16[1,192,2048]{2,1,0:T(8,128)(2,1)} %param.7) | copy-start | bytes 2359300
  56.4 20.3 %collective-permute-start.5 = (bf16[192,2048]{1,0:T(8,128)(2,1)}, bf16[192,2048]{1,0:T(8,128)(2,1)}, u32[]{:S(2)}, u32[]{:S(2)}) collective-permute-start(bf16[192,2048]{1,0:T(8,128)(2,1)} %fusion.9), channel_id=1, source_target_pairs={{0,1},{1,2},{2,3},{3,4},{4,5},{5,6},{6,7},{7,8},{8,9},{9,10},{10,1... | collective-permute-start | bytes 2359304 | tf_op jit(solution)/shard_map/ppermute | solution.py:19
  79.5 1.9 %copy-start.4 = (bf16[3,192,16,128]{3,1,0,2:T(8,128)(2,1)}, bf16[3,192,16,128]{3,1,0,2:T(8,128)(2,1)S(1)}, u32[]{:S(2)}) copy-start(bf16[3,192,16,128]{3,1,0,2:T(8,128)(2,1)S(1)} %convert_bitcast_fusion) | copy-start | bytes 7077892
  82.5 16.4 %collective-permute-start.6 = (bf16[2,12,16,128]{3,1,2,0:T(8,128)(2,1)S(1)}, bf16[2,12,16,128]{3,1,2,0:T(8,128)(2,1)S(1)}, u32[]{:S(2)}, u32[]{:S(2)}) collective-permute-start(bf16[2,12,16,128]{3,1,2,0:T(8,128)(2,1)S(1)} %pad_maximum_fusion.1), channel_id=1, source_target_pairs={{0,16},{16,32},{32,48},{48,64},{64,80},{80,96},{96,112},{112,128},... | collective-permute-start | bytes 294920 | tf_op jit(solution)/shard_map/ppermute | solution.py:19
  90.9 8.7 %collective-permute-start.7 = (bf16[2,12,16,128]{3,1,2,0:T(8,128)(2,1)S(1)}, bf16[2,12,16,128]{3,1,2,0:T(8,128)(2,1)S(1)}, u32[]{:S(2)}, u32[]{:S(2)}) collective-permute-start(bf16[2,12,16,128]{3,1,2,0:T(8,128)(2,1)S(1)} %pad_maximum_fusion.1), channel_id=1, source_target_pairs={{0,32},{16,48},{32,64},{48,80},{64,96},{80,112},{96,128},{112,144}... | collective-permute-start | bytes 294920 | tf_op jit(solution)/shard_map/ppermute | solution.py:19
  92.8 9.0 %collective-permute-start.8 = (bf16[2,12,16,128]{3,1,2,0:T(8,128)(2,1)S(1)}, bf16[2,12,16,128]{3,1,2,0:T(8,128)(2,1)S(1)}, u32[]{:S(2)}, u32[]{:S(2)}) collective-permute-start(bf16[2,12,16,128]{3,1,2,0:T(8,128)(2,1)S(1)} %pad_maximum_fusion.1), channel_id=1, source_target_pairs={{0,64},{16,80},{32,96},{48,112},{64,128},{80,144},{96,160},{112,17... | collective-permute-start | bytes 294920 | tf_op jit(solution)/shard_map/ppermute | solution.py:19
  95.5 12.6 %collective-permute-start.9 = (bf16[2,12,16,128]{3,1,2,0:T(8,128)(2,1)S(1)}, bf16[2,12,16,128]{3,1,2,0:T(8,128)(2,1)S(1)}, u32[]{:S(2)}, u32[]{:S(2)}) collective-permute-start(bf16[2,12,16,128]{3,1,2,0:T(8,128)(2,1)S(1)} %pad_maximum_fusion.1), channel_id=1, source_target_pairs={{0,128},{16,144},{32,160},{48,176},{64,192},{80,208},{96,224},{112... | collective-permute-start | bytes 294920 | tf_op jit(solution)/shard_map/ppermute | solution.py:19
  97.4 11.4 %collective-permute-start.10 = (bf16[2,12,16,128]{3,1,2,0:T(8,128)(2,1)S(1)}, bf16[2,12,16,128]{3,1,2,0:T(8,128)(2,1)S(1)}, u32[]{:S(2)}, u32[]{:S(2)}) collective-permute-start(bf16[2,12,16,128]{3,1,2,0:T(8,128)(2,1)S(1)} %pad_maximum_fusion.1), channel_id=1, source_target_pairs={{0,256},{16,272},{32,288},{48,304},{64,320},{80,336},{96,352},{112... | collective-permute-start | bytes 294920 | tf_op jit(solution)/shard_map/ppermute | solution.py:19
  119.8 1.7 %copy-start.1 = (f32[16,252,192]{1,2,0:T(8,128)}, f32[16,252,192]{1,2,0:T(8,128)S(1)}, u32[]{:S(2)}) copy-start(f32[16,252,192]{1,2,0:T(8,128)S(1)} %get-tuple-element.42) | copy-start | bytes 9289732
  119.8 3.1 %copy-start.7 = (bf16[192,16,128]{2,0,1:T(8,128)(2,1)S(1)}, bf16[192,16,128]{2,0,1:T(8,128)(2,1)}, u32[]{:S(2)}) copy-start(bf16[192,16,128]{2,0,1:T(8,128)(2,1)} %get-tuple-element.12) | copy-start | bytes 2359300
  119.8 3.1 %copy-start.10 = (bf16[12,16,128]{2,0,1:T(8,128)(2,1)S(1)}, bf16[12,16,128]{2,0,1:T(8,128)(2,1)}, u32[]{:S(2)}) copy-start(bf16[12,16,128]{2,0,1:T(8,128)(2,1)} %get-tuple-element.26) | copy-start | bytes 147460
  119.8 3.1 %copy-start.12 = (bf16[12,16,128]{2,0,1:T(8,128)(2,1)S(1)}, bf16[12,16,128]{2,0,1:T(8,128)(2,1)}, u32[]{:S(2)}) copy-start(bf16[12,16,128]{2,0,1:T(8,128)(2,1)} %get-tuple-element.24) | copy-start | bytes 147460
  119.8 3.1 %copy-start.14 = (bf16[12,16,128]{2,0,1:T(8,128)(2,1)S(1)}, bf16[12,16,128]{2,0,1:T(8,128)(2,1)}, u32[]{:S(2)}) copy-start(bf16[12,16,128]{2,0,1:T(8,128)(2,1)} %get-tuple-element.22) | copy-start | bytes 147460
  119.8 3.1 %copy-start.16 = (bf16[12,16,128]{2,0,1:T(8,128)(2,1)S(1)}, bf16[12,16,128]{2,0,1:T(8,128)(2,1)}, u32[]{:S(2)}) copy-start(bf16[12,16,128]{2,0,1:T(8,128)(2,1)} %get-tuple-element.20) | copy-start | bytes 147460
where the time goes:
time: 139 us; the launch traced here: 138 us
  local copies, waits for them, and re-layouts  46.3 us (33%)
  starting transfers between devices  33.2 us (24%)
  waiting for transfers between devices  28 us (20%)
  matrix products  15.5 us (11%)
  other arithmetic  14.4 us (10%)
    ppermute x11, starting transfers between devices, from_behind(): lax.ppermute(value, axis, [(source, source + steps) for source in range(i...  33.2 us
    ppermute x11, waiting for transfers between devices, from_behind(): lax.ppermute(value, axis, [(source, source + steps) for source in range(i...  28 us
    concatenate x2, local copies, waits for them, and re-layouts, layer_rows(): jnp.concatenate(keys, axis=0)  16.5 us
    concatenate x2, local copies, waits for them, and re-layouts, layer_rows(): jnp.concatenate(vals, axis=0)  15.5 us
    dot_general x2, matrix products, layer_rows(): jnp.einsum('qhd,hde->qhe', pieces, o_weights, preferred_element_type=jnp....  9.38 us
    squeeze x10, local copies, waits for them, and re-layouts, layer_rows(): keys.append(panel[0])  6.48 us
    dot_general x2, matrix products, attend(): jnp.einsum('qhd,khd->qhk', queries, keys, preferred_element_type=jnp.floa...  4.22 us
    unnamed x40, local copies, waits for them, and re-layouts  3.95 us
  transfers between devices with their start and end apart: 11, of which 6 were waited for; matrix products, arithmetic and copies ran while one was open for 4% of the time, Pallas kernels for 0%

commit v1 on v0

v1 whole, which is shorter than its diff:
```python
import functools
import math

import jax
import jax.numpy as jnp
from jax import lax
from jax.experimental import pallas as pl
from jax.experimental.pallas import tpu as pltpu
from jax.sharding import PartitionSpec as P

RATE = 16
HEADS = 16
DIM = 128
PACK = 8
SLOTS = 5
PAD = 16

eps = 1e-06
neg_big = -1e30
f32 = jnp.float32
bf16 = jnp.bfloat16

SMEM = pl.BlockSpec(memory_space=pltpu.SMEM)
VMEM = pl.BlockSpec(memory_space=pltpu.VMEM)


def inverse_rms(squares, width):
    return lax.rsqrt(squares * (1.0 / width) + eps)


def pick_panel(wide_ref, inv_ref, gain_ref, offsets_ref, panel_ref):
    count = wide_ref.shape[1] // RATE
    for head in range(HEADS):
        cols = slice(head * DIM, (head + 1) * DIM)
        where = pl.ds(offsets_ref[head], count, stride=RATE)
        picked = wide_ref[head, where, :] * inv_ref[where, :] * gain_ref[:, cols].astype(f32)
        panel_ref[:, cols] = jnp.concatenate(
            [picked, jnp.zeros((PAD - count, DIM), f32)], axis=0
        ).astype(bf16)


def norm_kernel(offsets_ref, state_ref, gain_ref, panel_ref, inv_ref, ahead_ref, wide_ref):
    width = state_ref.shape[1]
    ahead_ref[:, :width] = gain_ref[...]
    lane = lax.broadcasted_iota(jnp.int32, (1, DIM), 1)
    phases = jnp.zeros((1, DIM), jnp.int32)
    for head in range(HEADS):
        phases = jnp.where(lane == head, offsets_ref[head], phases)
    ahead_ref[:, width:] = phases.astype(f32).astype(bf16)
    squares = None
    for head in range(HEADS):
        cols = slice(head * DIM, (head + 1) * DIM)
        values = state_ref[:, cols].astype(f32)
        wide_ref[head] = values
        squares = values * values if squares is None else squares + values * values
    inverse = inverse_rms(jnp.sum(squares, axis=-1, keepdims=True), width)
    inv_ref[...] = jnp.broadcast_to(inverse, inv_ref.shape)
    pick_panel(wide_ref, inv_ref, gain_ref, offsets_ref, panel_ref)


def norm_panel(offsets, state, gain):
    rows, width = state.shape
    return pl.pallas_call(
        norm_kernel,
        out_shape=(
            jax.ShapeDtypeStruct((PAD, width), bf16),
            jax.ShapeDtypeStruct((rows, DIM), f32),
            jax.ShapeDtypeStruct((1, width + DIM), bf16),
        ),
        in_specs=[SMEM, VMEM, VMEM],
        out_specs=(VMEM, VMEM, VMEM),
        scratch_shapes=[pltpu.VMEM((HEADS, rows, DIM), f32)],
        cost_estimate=pl.CostEstimate(flops=2000000, bytes_accessed=1000000, transcendentals=0),
        name="norm_panel",
    )(offsets, state, gain)


def prepare_attention(place, chip_ref, first_ref, second_ref, swapped_ref, bias_ref, packed_ref, count):
    rows = bias_ref.shape[0]
    keys = bias_ref.shape[1]
    core = lax.rem(place, 2)
    other = 1 - core
    slots = [
        jnp.where(core == 0, first_ref[1], chip_ref[0]),
        first_ref[core],
        second_ref[core],
        swapped_ref[other, 0],
        swapped_ref[other, 1],
    ]
    for slot, panel in enumerate(slots):
        packed_ref[slot * count : (slot + 1) * count, :] = panel[:count].astype(f32)
    packed_ref[SLOTS * count :, :] = jnp.zeros(
        (packed_ref.shape[0] - SLOTS * count, packed_ref.shape[1]), f32
    )
    even, odd = (1, 2, 4, 8, 16), (1, 8, 16, 2, 4)
    row = lax.broadcasted_iota(jnp.int32, (rows, keys), 0)
    col = lax.broadcasted_iota(jnp.int32, (rows, keys), 1)
    allowed = (col < rows) & (col <= row)
    for slot in range(SLOTS):
        distance = jnp.where(core == 0, even[slot], odd[slot])
        start = jnp.where(place >= distance, rows + slot * count, keys)
        allowed = allowed | ((col >= start) & (col < rows + (slot + 1) * count))
    bias_ref[...] = jnp.where(allowed, 0.0, neg_big).astype(f32)


def some_heads(states, inverse, gains, queries, keys, values, outs, panels, bias):
    scale = math.log2(math.e) / math.sqrt(DIM)
    wide = [state.astype(f32) for state in states]
    normed = [(w * inverse * gain.astype(f32)).astype(bf16) for w, gain in zip(wide, gains)]
    both = [jnp.concatenate([n, panel.astype(bf16)], axis=0) for n, panel in zip(normed, panels)]
    query = [jnp.dot(n, w, preferred_element_type=f32).astype(bf16) for n, w in zip(normed, queries)]
    pair = [
        jnp.dot(rows, jnp.concatenate([k, v], axis=1), preferred_element_type=f32).astype(bf16)
        for rows, k, v in zip(both, keys, values)
    ]
    scores = [
        lax.dot_general(q, p[:, :DIM], (((1,), (1,)), ((), ())), preferred_element_type=f32)
        for q, p in zip(query, pair)
    ]
    scores = [s * scale + bias for s in scores]
    expo = [jnp.exp2(s - jnp.max(s, axis=-1, keepdims=True)) for s in scores]
    total = [jnp.sum(e, axis=-1, keepdims=True) for e in expo]
    summed = [
        jnp.dot(e.astype(bf16), p[:, DIM:], preferred_element_type=f32) for e, p in zip(expo, pair)
    ]
    attended = [(m * (1.0 / t)).astype(bf16) for m, t in zip(summed, total)]
    mixed = [jnp.dot(a, w, preferred_element_type=f32) for a, w in zip(attended, outs)]
    return [(w + m).astype(bf16) for w, m in zip(wide, mixed)]


def first_kernel(
    place_ref, offsets_ref,
    state_ref, inv_ref, gain_ref, qkv_ref, o_ref, chip_ref, first_ref, second_ref, swapped_ref, gain_next_ref,
    out_ref, panel_ref,
    bias_ref, packed_ref, wide_ref, squares_ref, inv_next_ref,
):
    step = pl.program_id(0)
    rows = state_ref.shape[0]
    count = rows // RATE

    @pl.when(step == 0)
    def _():
        prepare_attention(
            place_ref[0], chip_ref, first_ref, second_ref, swapped_ref, bias_ref, packed_ref, count
        )

    inverse, bias = inv_ref[...], bias_ref[...]
    squares = jnp.zeros((rows, DIM), f32)
    local_cols = [slice(local * DIM, (local + 1) * DIM) for local in range(PACK)]
    there = [pl.ds(pl.multiple_of((step * PACK + local) * DIM, DIM), DIM) for local in range(PACK)]
    results = some_heads(
        [state_ref[:, cols] for cols in local_cols], inverse, [gain_ref[:, cols] for cols in local_cols],
        [qkv_ref[0, i] for i in range(PACK)], [qkv_ref[1, i] for i in range(PACK)], [qkv_ref[2, i] for i in range(PACK)],
        [o_ref[i] for i in range(PACK)], [packed_ref[:, at] for at in there], bias,
    )
    for local, result in enumerate(results):
        out_ref[:, local_cols[local]] = result
        values = result.astype(f32)
        wide_ref[step * PACK + local] = values
        squares = squares + values * values
    squares_ref[...] = jnp.where(step == 0, squares, squares_ref[...] + squares)

    @pl.when(step == pl.num_programs(0) - 1)
    def _():
        total = jnp.sum(squares_ref[...], axis=-1, keepdims=True)
        inv_next_ref[...] = jnp.broadcast_to(inverse_rms(total, HEADS * DIM), inv_next_ref.shape)
        pick_panel(wide_ref, inv_next_ref, gain_next_ref, offsets_ref, panel_ref)


def attention_specs(rows, width):
    return [
        pl.BlockSpec((1, PACK * DIM), lambda i: (0, i)),
        pl.BlockSpec((3, PACK, DIM, DIM), lambda i: (0, i, 0, 0)),
        pl.BlockSpec((PACK, DIM, DIM), lambda i: (i, 0, 0)),
        pl.BlockSpec((2, PAD, width), lambda i: (0, 0, 0)),
        pl.BlockSpec((2, PAD, width), lambda i: (0, 0, 0)),
        pl.BlockSpec((2, PAD, width), lambda i: (0, 0, 0)),
        pl.BlockSpec((2, 2, PAD, width), lambda i: (0, 0, 0, 0)),
    ]


def first_layer(place, offsets_next, state, inv, gain, qkv, o_weights, fetched, gain_next):
    rows, width = state.shape
    keys = 256
    return pl.pallas_call(
        first_kernel,
        grid=(HEADS // PACK,),
        out_shape=(
            jax.ShapeDtypeStruct((rows, width), bf16),
            jax.ShapeDtypeStruct((PAD, width), bf16),
        ),
        in_specs=[
            SMEM,
            SMEM,
            pl.BlockSpec((rows, PACK * DIM), lambda i: (0, i)),
            pl.BlockSpec((rows, DIM), lambda i: (0, 0)),
            *attention_specs(rows, width),
            pl.BlockSpec((1, width), lambda i: (0, 0)),
        ],
        out_specs=(
            pl.BlockSpec((rows, PACK * DIM), lambda i: (0, i)),
            pl.BlockSpec((PAD, width), lambda i: (0, 0)),
        ),
        scratch_shapes=[
            pltpu.VMEM((rows, keys), f32),
            pltpu.VMEM((keys - rows, width), f32),
            pltpu.VMEM((HEADS, rows, DIM), f32),
            pltpu.VMEM((rows, DIM), f32),
            pltpu.VMEM((rows, DIM), f32),
        ],
        compiler_params=pltpu.CompilerParams(vmem_limit_bytes=60 << 20),
        cost_estimate=pl.CostEstimate(flops=800000000, bytes_accessed=5000000, transcendentals=800000),
        name="first_layer",
    )(place, offsets_next, state, inv, gain, qkv, o_weights, *fetched, gain_next)


def last_kernel(
    place_ref, first_section_ref,
    moved_ref, fresh_ref, gain_ref, qkv_ref, o_ref, chip_ref, first_ref, second_ref, swapped_ref,
    out_ref,
    bias_ref, packed_ref, state_ref, inv_ref,
):
    step = pl.program_id(0)
    rows, width = moved_ref.shape
    count = rows // RATE

    @pl.when(step == 0)
    def _():
        prepare_attention(
            place_ref[0], chip_ref, first_ref, second_ref, swapped_ref, bias_ref, packed_ref, count
        )
        is_first = first_section_ref[0] == 1
        squares = None
        for head in range(HEADS):
            cols = slice(head * DIM, (head + 1) * DIM)
            values = jnp.where(is_first, fresh_ref[:, cols], moved_ref[:, cols])
            state_ref[:, cols] = values
            values = values.astype(f32)
            squares = values * values if squares is None else squares + values * values
        inverse = inverse_rms(jnp.sum(squares, axis=-1, keepdims=True), width)
        inv_ref[...] = jnp.broadcast_to(inverse, inv_ref.shape)

    inverse, bias = inv_ref[...], bias_ref[...]
    local_cols = [slice(local * DIM, (local + 1) * DIM) for local in range(PACK)]
    there = [pl.ds(pl.multiple_of((step * PACK + local) * DIM, DIM), DIM) for local in range(PACK)]
    results = some_heads(
        [state_ref[:, at] for at in there], inverse, [gain_ref[:, cols] for cols in local_cols],
        [qkv_ref[0, i] for i in range(PACK)], [qkv_ref[1, i] for i in range(PACK)], [qkv_ref[2, i] for i in range(PACK)],
        [o_ref[i] for i in range(PACK)], [packed_ref[:, at] for at in there], bias,
    )
    for local, result in enumerate(results):
        out_ref[:, local_cols[local]] = result


def last_layer(place, first_section, moved, fresh, gain, qkv, o_weights, fetched):
    rows, width = moved.shape
    keys = 256
    return pl.pallas_call(
        last_kernel,
        grid=(HEADS // PACK,),
        out_shape=jax.ShapeDtypeStruct((rows, width), bf16),
        in_specs=[
            SMEM,
            SMEM,
            pl.BlockSpec((rows, width), lambda i: (0, 0)),
            pl.BlockSpec((rows, width), lambda i: (0, 0)),
            *attention_specs(rows, width),
        ],
        out_specs=pl.BlockSpec((rows, PACK * DIM), lambda i: (0, i)),
        scratch_shapes=[
            pltpu.VMEM((rows, keys), f32),
            pltpu.VMEM((keys - rows, width), f32),
            pltpu.VMEM((rows, width), bf16),
            pltpu.VMEM((rows, DIM), f32),
        ],
        compiler_params=pltpu.CompilerParams(vmem_limit_bytes=60 << 20),
        cost_estimate=pl.CostEstimate(flops=800000000, bytes_accessed=5000000, transcendentals=800000),
        name="last_layer",
    )(place, first_section, moved, fresh, gain, qkv, o_weights, *fetched)


def shifted(value, axis, steps):
    count = lax.axis_size(axis)
    first, last = max(0, -steps), min(count, count - steps)
    return lax.ppermute(value, axis, [(source, source + steps) for source in range(first, last)])


def by_core(value, even_steps, odd_steps):
    chips = lax.axis_size("seq") // 2
    pairs = [(2 * c, 2 * (c + even_steps)) for c in range(chips - even_steps)]
    pairs += [(2 * c + 1, 2 * (c + odd_steps) + 1) for c in range(chips - odd_steps)]
    return lax.ppermute(value, "seq", pairs)


def fetch(panel, core):
    count = lax.axis_size("seq")
    cores = [[chip, chip + 1] for chip in range(0, count, 2)]
    chip = lax.all_gather(panel, "seq", axis=0, axis_index_groups=cores)
    first = by_core(chip, 1, 4)
    second = by_core(chip, 2, 8)
    mine = jnp.stack(
        [
            lax.dynamic_index_in_dim(first, 1 - core, 0, keepdims=False),
            lax.dynamic_index_in_dim(second, 1 - core, 0, keepdims=False),
        ]
    )
    swapped = lax.all_gather(mine, "seq", axis=0, axis_index_groups=cores)
    return chip, first, second, swapped


def on_device(slabs, fresh, norm_gain, qkv_proj, o_proj, offsets):
    place = lax.axis_index("seq").astype(jnp.int32)
    section = lax.axis_index("section")
    core = lax.rem(place, 2)
    here = place.reshape(1)
    is_first = (section == 0).astype(jnp.int32)
    state, entering = slabs[0], fresh[0]
    gain, qkv, o_weights = norm_gain, qkv_proj[0], o_proj[0]

    panel, inv, ahead = norm_panel(offsets[0], state, gain)
    fetched = fetch(panel, core)
    ahead = shifted(ahead, "section", -1)
    gain_next = ahead[:, : HEADS * DIM]
    offsets_next = ahead[0, HEADS * DIM : HEADS * DIM + HEADS].astype(jnp.int32)
    output, panel_next = first_layer(
        here, offsets_next, state, inv, gain, qkv, o_weights, fetched, gain_next
    )
    entering_panel, _, _ = norm_panel(offsets[0], entering, gain)
    moved_panel = shifted(panel_next, "section", 1)
    moved = shifted(output, "section", 1)
    panel = jnp.where(is_first == 1, entering_panel, moved_panel)
    fetched = fetch(panel, core)
    result = last_layer(here, is_first.reshape(1), moved, entering, gain, qkv, o_weights, fetched)
    return result[None]


def solution(mesh):
    in_specs = (
        P("section", "seq", None),
        P(None, "seq", None),
        P("section", None),
        P("section", None, None, None, None),
        P("section", None, None, None),
        P("section", None),
    )
    out_specs = P("section", "seq", None)
    return jax.shard_map(
        on_device, mesh=mesh, in_specs=in_specs, out_specs=out_specs, check_vma=False
    )
```

time: 139 us -> 72.4 us (0.52)
  the two profiles are of different devices: /device:TPU:401 before, /device:TPU:385 now
where the time goes in v1:
time: 72.4 us; the launch traced here: 72 us
  starting transfers between devices  24.6 us (34%)
  waiting for transfers between devices  19.1 us (26%)
  Pallas kernels  15.1 us (21%)
  blocking collectives  10.9 us (15%)
  local copies, waits for them, and re-layouts  1.56 us (2%)
    ppermute x4, starting transfers between devices, by_core(): return lax.ppermute(value, 'seq', pairs)  17 us
    ppermute x3, waiting for transfers between devices, shifted(): lax.ppermute(value, axis, [(source, source + steps) for source in range(f...  16.4 us
    ppermute x3, starting transfers between devices, shifted(): lax.ppermute(value, axis, [(source, source + steps) for source in range(f...  7.67 us
    all_gather x2, blocking collectives, fetch(): chip = lax.all_gather(panel, 'seq', axis=0, axis_index_groups=cores)  5.78 us
    pallas_call x1, Pallas kernels, last_layer(): pl.pallas_call(last_kernel, grid=(HEADS // PACK,), out_shape=jax.ShapeDty...  5.54 us
    pallas_call x1, Pallas kernels, first_layer(): pl.pallas_call(first_kernel, grid=(HEADS // PACK,), out_shape=(jax.ShapeD...  5.3 us
    all_gather x2, blocking collectives, fetch(): swapped = lax.all_gather(mine, 'seq', axis=0, axis_index_groups=cores)  5.12 us
    pallas_call x2, Pallas kernels, norm_panel(): pl.pallas_call(norm_kernel, out_shape=(jax.ShapeDtypeStruct((PAD, width),...  4.29 us
  transfers between devices with their start and end apart: 7, of which 4 were waited for; matrix products, arithmetic and copies ran while one was open for 2% of the time, Pallas kernels for 3%

profile of v1, /device:TPU:385, one launch (start us, length us, event | category | flops | bytes accessed | tf_op | source)
XLA Modules:
  0.0 72.0 jit_solution(11830142729929974122)
XLA Ops:
  0.0 2.1 %norm_panel.2 = (bf16[16,2048]{1,0:T(8,128)(2,1)}, f32[192,128]{1,0:T(8,128)}, bf16[1,2176]{1,0:T(2,128)(2,1)}) custom-call(s32[16]{0:T(128)} %bitcast.33, bf16[192,2048]{1,0:T(8,128)(2,1)} %bitcast.19, bf16[1,2048]{1,0:T(2,128)(2,1)} %gain_ref.7), custom_call_target="tpu_custom_call" | custom-call | flops 2000000 | bytes 1000000 | tf_op jit(solution)/shard_map/norm_panel/pallas_call | solution.py:63
  2.1 3.8 %collective-permute-start = (bf16[1,2176]{1,0:T(2,128)(2,1)}, bf16[1,2176]{1,0:T(2,128)(2,1)S(1)}, u32[]{:S(2)}, u32[]{:S(2)}) collective-permute-start(bf16[1,2176]{1,0:T(2,128)(2,1)} %get-tuple-element.11), channel_id=1, source_target_pairs={{1,0},{2,1},{3,2},{4,3},{5,4},{6,5},{7,6},{8,7},{9,8},{10,9},{11,1... | collective-permute-start | bytes 13064 | tf_op jit(solution)/shard_map/ppermute | solution.py:285
  6.0 2.7 %all-gather = bf16[32,2048]{1,0:T(8,128)(2,1)S(1)} all-gather(bf16[16,2048]{1,0:T(8,128)(2,1)} %get-tuple-element.13), channel_id=2, replica_groups={{0,16},{32,48},{64,80},{96,112},{128,144},{160,176},{192,208},{224,240}..., dimensions={0}, use_global_device_ids=true | all-gather | bytes 196608 | tf_op jit(solution)/shard_map/all_gather | solution.py:298
  8.7 0.0 copy-start.1
  8.7 3.2 %collective-permute-start.1 = (bf16[2,16,2048]{2,1,0:T(8,128)(2,1)S(1)}, bf16[2,16,2048]{2,1,0:T(8,128)(2,1)S(1)}, u32[]{:S(2)}, u32[]{:S(2)}) collective-permute-start(bf16[2,16,2048]{2,1,0:T(8,128)(2,1)S(1)} %bitcast.27), channel_id=1, source_target_pairs={{0,32},{32,64},{64,96},{96,128},{128,160},{160,192},{192,224},{224... | collective-permute-start | bytes 393224 | tf_op jit(solution)/shard_map/ppermute | solution.py:292
  11.9 4.5 %collective-permute-start.2 = (bf16[2,16,2048]{2,1,0:T(8,128)(2,1)S(1)}, bf16[2,16,2048]{2,1,0:T(8,128)(2,1)S(1)}, u32[]{:S(2)}, u32[]{:S(2)}) collective-permute-start(bf16[2,16,2048]{2,1,0:T(8,128)(2,1)S(1)} %bitcast.28), channel_id=1, source_target_pairs={{0,64},{32,96},{64,128},{96,160},{128,192},{160,224},{192,256},{22... | collective-permute-start | bytes 393224 | tf_op jit(solution)/shard_map/ppermute | solution.py:292
  16.5 0.0 collective-permute-done
  16.5 0.6 slice.9.gain_next_ref
  17.1 0.5 fusion.offsets_ref
  17.6 0.8 %collective-permute-done.2.second_ref = bf16[2,16,2048]{2,1,0:T(8,128)(2,1)S(1)} collective-permute-done((bf16[2,16,2048]{2,1,0:T(8,128)(2,1)S(1)}, bf16[2,16,2048]{2,1,0:T(8,128)(2,1)S(1)}, u32[]{:S(2)}, u32[]{:S(2)}) %collective-permute-start.2) | collective-permute-done | bytes 131104 | tf_op jit(solution)/shard_map/ppermute | solution.py:292
  18.4 0.0 copy-start.4
  18.4 0.0 collective-permute-done.1.first_ref
  18.4 0.0 copy-start.3
  18.4 3.0 %all-gather.1 = bf16[4,16,2048]{2,1,0:T(8,128)(2,1)} all-gather(bf16[2,16,2048]{2,1,0:T(8,128)(2,1)S(1)} %pad_maximum_fusion), channel_id=3, replica_groups={{0,16},{32,48},{64,80},{96,112},{128,144},{160,176},{192,208},{224,240}..., dimensions={0}, use_global_device_ids=true | all-gather | bytes 393216 | tf_op jit(solution)/shard_map/all_gather | solution.py:307
  21.4 0.0 copy-done.1
  21.4 0.0 copy-done.4
  21.4 0.0 copy-done.3
  21.4 5.3 %first_layer.1 = (bf16[192,2048]{1,0:T(8,128)(2,1)}, bf16[16,2048]{1,0:T(8,128)(2,1)}) custom-call(s32[1]{0:T(128)} %bitcast.place_ref, s32[16]{0:T(128)} %fusion.offsets_ref, bf16[192,2048]{1,0:T(8,128)(2,1)} %bitcast.20, f32[192,128]{1,0:T(8,128)} %get-tuple-element.12.inv_ref, bf16[1,2048]{1,0:T(2,128)(2,1)} %gain_ref.7, ...), custom_call_target="tpu_custom_call" | custom-call | flops 800000000 | bytes 5000000 | tf_op jit(solution)/shard_map/first_layer/pallas_call | solution.py:185
  26.7 1.9 %collective-permute-start.4 = (bf16[16,2048]{1,0:T(8,128)(2,1)}, bf16[16,2048]{1,0:T(8,128)(2,1)S(1)}, u32[]{:S(2)}, u32[]{:S(2)}) collective-permute-start(bf16[16,2048]{1,0:T(8,128)(2,1)} %get-tuple-element.16), channel_id=1, source_target_pairs={{0,1},{1,2},{2,3},{3,4},{4,5},{5,6},{6,7},{7,8},{8,9},{9,10},{10,1... | collective-permute-start | bytes 196616 | tf_op jit(solution)/shard_map/ppermute | solution.py:285
  28.7 2.1 %norm_panel.3 = (bf16[16,2048]{1,0:T(8,128)(2,1)}, f32[192,128]{1,0:T(8,128)}, bf16[1,2176]{1,0:T(2,128)(2,1)}) custom-call(s32[16]{0:T(128)} %bitcast.34, bf16[192,2048]{1,0:T(8,128)(2,1)} %bitcast.21, bf16[1,2048]{1,0:T(2,128)(2,1)} %gain_ref.7), custom_call_target="tpu_custom_call" | custom-call | flops 2000000 | bytes 1000000 | tf_op jit(solution)/shard_map/norm_panel/pallas_call | solution.py:63
  30.8 2.3 %collective-permute-done.4 = bf16[16,2048]{1,0:T(8,128)(2,1)S(1)} collective-permute-done((bf16[16,2048]{1,0:T(8,128)(2,1)}, bf16[16,2048]{1,0:T(8,128)(2,1)S(1)}, u32[]{:S(2)}, u32[]{:S(2)}) %collective-permute-start.4) | collective-permute-done | bytes 65568 | tf_op jit(solution)/shard_map/ppermute | solution.py:285
  33.2 3.1 %all-gather.2 = bf16[32,2048]{1,0:T(8,128)(2,1)S(1)} all-gather(bf16[16,2048]{1,0:T(8,128)(2,1)S(1)} %broadcast_select_fusion), channel_id=4, replica_groups={{0,16},{32,48},{64,80},{96,112},{128,144},{160,176},{192,208},{224,240}..., dimensions={0}, use_global_device_ids=true | all-gather | bytes 196608 | tf_op jit(solution)/shard_map/all_gather | solution.py:298
  36.3 0.0 copy-start.2
  36.3 6.9 %collective-permute-start.6 = (bf16[2,16,2048]{2,1,0:T(8,128)(2,1)S(1)}, bf16[2,16,2048]{2,1,0:T(8,128)(2,1)S(1)}, u32[]{:S(2)}, u32[]{:S(2)}) collective-permute-start(bf16[2,16,2048]{2,1,0:T(8,128)(2,1)S(1)} %bitcast.30), channel_id=1, source_target_pairs={{0,64},{32,96},{64,128},{96,160},{128,192},{160,224},{192,256},{22... | collective-permute-start | bytes 393224 | tf_op jit(solution)/shard_map/ppermute | solution.py:292
  43.2 1.9 %collective-permute-start.3 = (bf16[192,2048]{1,0:T(8,128)(2,1)}, bf16[192,2048]{1,0:T(8,128)(2,1)S(1)}, u32[]{:S(2)}, u32[]{:S(2)}) collective-permute-start(bf16[192,2048]{1,0:T(8,128)(2,1)} %get-tuple-element.14), channel_id=1, source_target_pairs={{0,1},{1,2},{2,3},{3,4},{4,5},{5,6},{6,7},{7,8},{8,9},{9,10},{10,1... | collective-permute-start | bytes 2359304 | tf_op jit(solution)/shard_map/ppermute | solution.py:285
  45.1 2.3 %collective-permute-start.5 = (bf16[2,16,2048]{2,1,0:T(8,128)(2,1)S(1)}, bf16[2,16,2048]{2,1,0:T(8,128)(2,1)S(1)}, u32[]{:S(2)}, u32[]{:S(2)}) collective-permute-start(bf16[2,16,2048]{2,1,0:T(8,128)(2,1)S(1)} %bitcast.31), channel_id=1, source_target_pairs={{0,32},{32,64},{64,96},{96,128},{128,160},{160,192},{192,224},{224... | collective-permute-start | bytes 393224 | tf_op jit(solution)/shard_map/ppermute | solution.py:292
  47.4 0.0 collective-permute-done.6.second_ref
  47.5 0.0 copy-start.5
  47.5 1.9 %collective-permute-done.5.first_ref = bf16[2,16,2048]{2,1,0:T(8,128)(2,1)S(1)} collective-permute-done((bf16[2,16,2048]{2,1,0:T(8,128)(2,1)S(1)}, bf16[2,16,2048]{2,1,0:T(8,128)(2,1)S(1)}, u32[]{:S(2)}, u32[]{:S(2)}) %collective-permute-start.5) | collective-permute-done | bytes 131104 | tf_op jit(solution)/shard_map/ppermute | solution.py:292
  49.4 0.0 copy-start.6
  49.4 2.1 %all-gather.3 = bf16[4,16,2048]{2,1,0:T(8,128)(2,1)} all-gather(bf16[2,16,2048]{2,1,0:T(8,128)(2,1)S(1)} %pad_maximum_fusion.1), channel_id=5, replica_groups={{0,16},{32,48},{64,80},{96,112},{128,144},{160,176},{192,208},{224,240}..., dimensions={0}, use_global_device_ids=true | all-gather | bytes 393216 | tf_op jit(solution)/shard_map/all_gather | solution.py:307
  51.5 14.0 %collective-permute-done.3.moved_ref = bf16[192,2048]{1,0:T(8,128)(2,1)S(1)} collective-permute-done((bf16[192,2048]{1,0:T(8,128)(2,1)}, bf16[192,2048]{1,0:T(8,128)(2,1)S(1)}, u32[]{:S(2)}, u32[]{:S(2)}) %collective-permute-start.3) | collective-permute-done | bytes 786464 | tf_op jit(solution)/shard_map/ppermute | solution.py:285
  65.5 0.0 copy-start
  65.5 0.0 copy-done.2
  65.5 0.0 copy-done.5
  65.5 0.0 copy-done.6
  65.5 0.9 %copy-done = bf16[192,2048]{1,0:T(8,128)(2,1)} copy-done((bf16[192,2048]{1,0:T(8,128)(2,1)}, bf16[192,2048]{1,0:T(8,128)(2,1)S(1)}, u32[]{:S(2)}) %copy-start) | copy-done | bytes 786456
  66.4 5.5 %last_layer.1 = bf16[192,2048]{1,0:T(8,128)(2,1)} custom-call(s32[1]{0:T(128)} %bitcast.place_ref, s32[1]{0:T(128)} %bitcast.1.first_section_ref, bf16[192,2048]{1,0:T(8,128)(2,1)} %copy-done, bf16[192,2048]{1,0:T(8,128)(2,1)} %bitcast.22, bf16[1,2048]{1,0:T(2,128)(2,1)} %gain_ref.7, bf16[3,16,128,128]{3,2,1,0:T(8,128)(2,1)} %bitcast.18, ...), custom_call_target="tpu_custom_call" | custom-call | flops 800000000 | bytes 5000000 | tf_op jit(solution)/shard_map/last_layer/pallas_call | solution.py:258
  (7 shorter events, 0.1 us)
Async XLA Ops:
  2.1 14.3 %collective-permute-start = (bf16[1,2176]{1,0:T(2,128)(2,1)}, bf16[1,2176]{1,0:T(2,128)(2,1)S(1)}, u32[]{:S(2)}, u32[]{:S(2)}) collective-permute-start(bf16[1,2176]{1,0:T(2,128)(2,1)} %get-tuple-element.11), channel_id=1, source_target_pairs={{1,0},{2,1},{3,2},{4,3},{5,4},{6,5},{7,6},{8,7},{9,8},{10,9},{11,1... | collective-permute-start | bytes 13064 | tf_op jit(solution)/shard_map/ppermute | solution.py:285
  8.7 12.7 %copy-start.1 = (bf16[32,2048]{1,0:T(8,128)(2,1)}, bf16[32,2048]{1,0:T(8,128)(2,1)S(1)}, u32[]{:S(2)}) copy-start(bf16[32,2048]{1,0:T(8,128)(2,1)S(1)} %all-gather) | copy-start | bytes 393220
  8.7 9.7 %collective-permute-start.1 = (bf16[2,16,2048]{2,1,0:T(8,128)(2,1)S(1)}, bf16[2,16,2048]{2,1,0:T(8,128)(2,1)S(1)}, u32[]{:S(2)}, u32[]{:S(2)}) collective-permute-start(bf16[2,16,2048]{2,1,0:T(8,128)(2,1)S(1)} %bitcast.27), channel_id=1, source_target_pairs={{0,32},{32,64},{64,96},{96,128},{128,160},{160,192},{192,224},{224... | collective-permute-start | bytes 393224 | tf_op jit(solution)/shard_map/ppermute | solution.py:292
  11.9 6.5 %collective-permute-start.2 = (bf16[2,16,2048]{2,1,0:T(8,128)(2,1)S(1)}, bf16[2,16,2048]{2,1,0:T(8,128)(2,1)S(1)}, u32[]{:S(2)}, u32[]{:S(2)}) collective-permute-start(bf16[2,16,2048]{2,1,0:T(8,128)(2,1)S(1)} %bitcast.28), channel_id=1, source_target_pairs={{0,64},{32,96},{64,128},{96,160},{128,192},{160,224},{192,256},{22... | collective-permute-start | bytes 393224 | tf_op jit(solution)/shard_map/ppermute | solution.py:292
  18.4 3.1 %copy-start.4 = (bf16[2,16,2048]{2,1,0:T(8,128)(2,1)}, bf16[2,16,2048]{2,1,0:T(8,128)(2,1)S(1)}, u32[]{:S(2)}) copy-start(bf16[2,16,2048]{2,1,0:T(8,128)(2,1)S(1)} %collective-permute-done.2.second_ref) | copy-start | bytes 393220
  18.4 3.1 %copy-start.3 = (bf16[2,16,2048]{2,1,0:T(8,128)(2,1)}, bf16[2,16,2048]{2,1,0:T(8,128)(2,1)S(1)}, u32[]{:S(2)}) copy-start(bf16[2,16,2048]{2,1,0:T(8,128)(2,1)S(1)} %collective-permute-done.1.first_ref) | copy-start | bytes 393220
  26.7 6.4 %collective-permute-start.4 = (bf16[16,2048]{1,0:T(8,128)(2,1)}, bf16[16,2048]{1,0:T(8,128)(2,1)S(1)}, u32[]{:S(2)}, u32[]{:S(2)}) collective-permute-start(bf16[16,2048]{1,0:T(8,128)(2,1)} %get-tuple-element.16), channel_id=1, source_target_pairs={{0,1},{1,2},{2,3},{3,4},{4,5},{5,6},{6,7},{7,8},{8,9},{9,10},{10,1... | collective-permute-start | bytes 196616 | tf_op jit(solution)/shard_map/ppermute | solution.py:285
  36.3 29.3 %copy-start.2 = (bf16[32,2048]{1,0:T(8,128)(2,1)}, bf16[32,2048]{1,0:T(8,128)(2,1)S(1)}, u32[]{:S(2)}) copy-start(bf16[32,2048]{1,0:T(8,128)(2,1)S(1)} %all-gather.2) | copy-start | bytes 393220
  36.3 11.2 %collective-permute-start.6 = (bf16[2,16,2048]{2,1,0:T(8,128)(2,1)S(1)}, bf16[2,16,2048]{2,1,0:T(8,128)(2,1)S(1)}, u32[]{:S(2)}, u32[]{:S(2)}) collective-permute-start(bf16[2,16,2048]{2,1,0:T(8,128)(2,1)S(1)} %bitcast.30), channel_id=1, source_target_pairs={{0,64},{32,96},{64,128},{96,160},{128,192},{160,224},{192,256},{22... | collective-permute-start | bytes 393224 | tf_op jit(solution)/shard_map/ppermute | solution.py:292
  43.2 22.3 %collective-permute-start.3 = (bf16[192,2048]{1,0:T(8,128)(2,1)}, bf16[192,2048]{1,0:T(8,128)(2,1)S(1)}, u32[]{:S(2)}, u32[]{:S(2)}) collective-permute-start(bf16[192,2048]{1,0:T(8,128)(2,1)} %get-tuple-element.14), channel_id=1, source_target_pairs={{0,1},{1,2},{2,3},{3,4},{4,5},{5,6},{6,7},{7,8},{8,9},{9,10},{10,1... | collective-permute-start | bytes 2359304 | tf_op jit(solution)/shard_map/ppermute | solution.py:285
  45.1 4.2 %collective-permute-start.5 = (bf16[2,16,2048]{2,1,0:T(8,128)(2,1)S(1)}, bf16[2,16,2048]{2,1,0:T(8,128)(2,1)S(1)}, u32[]{:S(2)}, u32[]{:S(2)}) collective-permute-start(bf16[2,16,2048]{2,1,0:T(8,128)(2,1)S(1)} %bitcast.31), channel_id=1, source_target_pairs={{0,32},{32,64},{64,96},{96,128},{128,160},{160,192},{192,224},{224... | collective-permute-start | bytes 393224 | tf_op jit(solution)/shard_map/ppermute | solution.py:292
  47.5 18.1 %copy-start.5 = (bf16[2,16,2048]{2,1,0:T(8,128)(2,1)}, bf16[2,16,2048]{2,1,0:T(8,128)(2,1)S(1)}, u32[]{:S(2)}) copy-start(bf16[2,16,2048]{2,1,0:T(8,128)(2,1)S(1)} %collective-permute-done.6.second_ref) | copy-start | bytes 393220
  49.4 16.2 %copy-start.6 = (bf16[2,16,2048]{2,1,0:T(8,128)(2,1)}, bf16[2,16,2048]{2,1,0:T(8,128)(2,1)S(1)}, u32[]{:S(2)}) copy-start(bf16[2,16,2048]{2,1,0:T(8,128)(2,1)S(1)} %collective-permute-done.5.first_ref) | copy-start | bytes 393220
  65.5 0.9 %copy-start = (bf16[192,2048]{1,0:T(8,128)(2,1)}, bf16[192,2048]{1,0:T(8,128)(2,1)S(1)}, u32[]{:S(2)}) copy-start(bf16[192,2048]{1,0:T(8,128)(2,1)S(1)} %collective-permute-done.3.moved_ref) | copy-start | bytes 2359300

commit v2 on v1

--- a/solution.py
+++ b/solution.py
@@ -13,6 +13,7 @@
 DIM = 128
 PACK = 8
 SLOTS = 5
+KEYS = 256
 PAD = 16
 
 eps = 1e-06
@@ -22,6 +23,7 @@
 
 SMEM = pl.BlockSpec(memory_space=pltpu.SMEM)
 VMEM = pl.BlockSpec(memory_space=pltpu.VMEM)
+ANY = pl.BlockSpec(memory_space=pl.ANY)
 
 
 def inverse_rms(squares, width):
@@ -75,10 +77,8 @@
     )(offsets, state, gain)
 
 
-def prepare_attention(place, chip_ref, first_ref, second_ref, swapped_ref, bias_ref, packed_ref, count):
-    rows = bias_ref.shape[0]
-    keys = bias_ref.shape[1]
-    core = lax.rem(place, 2)
+def pack_panels(core, chip_ref, first_ref, second_ref, swapped_ref, packed_ref, count):
+    width = packed_ref.shape[1]
     other = 1 - core
     slots = [
         jnp.where(core == 0, first_ref[1], chip_ref[0]),
@@ -89,9 +89,12 @@
     ]
     for slot, panel in enumerate(slots):
         packed_ref[slot * count : (slot + 1) * count, :] = panel[:count].astype(f32)
-    packed_ref[SLOTS * count :, :] = jnp.zeros(
-        (packed_ref.shape[0] - SLOTS * count, packed_ref.shape[1]), f32
-    )
+    packed_ref[SLOTS * count :, :] = jnp.zeros((packed_ref.shape[0] - SLOTS * count, width), f32)
+
+
+def write_bias(place, bias_ref, count):
+    rows, keys = bias_ref.shape
+    core = lax.rem(place, 2)
     even, odd = (1, 2, 4, 8, 16), (1, 8, 16, 2, 4)
     row = lax.broadcasted_iota(jnp.int32, (rows, keys), 0)
     col = lax.broadcasted_iota(jnp.int32, (rows, keys), 1)
@@ -101,6 +104,50 @@
         start = jnp.where(place >= distance, rows + slot * count, keys)
         allowed = allowed | ((col >= start) & (col < rows + (slot + 1) * count))
     bias_ref[...] = jnp.where(allowed, 0.0, neg_big).astype(f32)
+
+
+def entering_kernel(place_ref, is_first_ref, offsets_ref, fresh_ref, gain_ref, panel_ref, bias_ref, state_ref, wide_ref, inv_ref, sem):
+    write_bias(place_ref[0], bias_ref, wide_ref.shape[1] // RATE)
+
+    @pl.when(is_first_ref[0] == 1)
+    def _():
+        copy = pltpu.make_async_copy(fresh_ref, state_ref, sem)
+        copy.start()
+        copy.wait()
+        squares = None
+        for head in range(HEADS):
+            values = state_ref[:, head * DIM : (head + 1) * DIM].astype(f32)
+            wide_ref[head] = values
+            squares = values * values if squares is None else squares + values * values
+        inverse = inverse_rms(jnp.sum(squares, axis=-1, keepdims=True), HEADS * DIM)
+        inv_ref[...] = jnp.broadcast_to(inverse, inv_ref.shape)
+        pick_panel(wide_ref, inv_ref, gain_ref, offsets_ref, panel_ref)
+
+    @pl.when(is_first_ref[0] == 0)
+    def _():
+        panel_ref[...] = jnp.zeros(panel_ref.shape, panel_ref.dtype)
+
+
+def entering_panel(place, is_first, offsets, fresh, gain):
+    rows, width = fresh.shape
+    return pl.pallas_call(
+        entering_kernel,
+        out_shape=(
+            jax.ShapeDtypeStruct((PAD, width), bf16),
+            jax.ShapeDtypeStruct((rows, KEYS), f32),
+        ),
+        in_specs=[SMEM, SMEM, SMEM, ANY, VMEM],
+        out_specs=(VMEM, VMEM),
+        scratch_shapes=[
+            pltpu.VMEM((rows, width), bf16),
+            pltpu.VMEM((HEADS, rows, DIM), f32),
+            pltpu.VMEM((rows, DIM), f32),
+            pltpu.SemaphoreType.DMA,
+        ],
+        compiler_params=pltpu.CompilerParams(vmem_limit_bytes=60 << 20),
+        cost_estimate=pl.CostEstimate(flops=2000000, bytes_accessed=1000000, transcendentals=0),
+        name="entering_panel",
+    )(place, is_first, offsets, fresh, gain)
 
 
 def some_heads(states, inverse, gains, queries, keys, values, outs, panels, bias):
@@ -130,9 +177,9 @@
 
 def first_kernel(
     place_ref, offsets_ref,
-    state_ref, inv_ref, gain_ref, qkv_ref, o_ref, chip_ref, first_ref, second_ref, swapped_ref, gain_next_ref,
+    state_ref, inv_ref, bias_ref, gain_ref, qkv_ref, o_ref, chip_ref, first_ref, second_ref, swapped_ref, gain_next_ref,
     out_ref, panel_ref,
-    bias_ref, packed_ref, wide_ref, squares_ref, inv_next_ref,
+    packed_ref, wide_ref, squares_ref, inv_next_ref,
 ):
     step = pl.program_id(0)
     rows = state_ref.shape[0]
@@ -140,8 +187,8 @@
 
     @pl.when(step == 0)
     def _():
-        prepare_attention(
-            place_ref[0], chip_ref, first_ref, second_ref, swapped_ref, bias_ref, packed_ref, count
+        pack_panels(
+            lax.rem(place_ref[0], 2), chip_ref, first_ref, second_ref, swapped_ref, packed_ref, count
         )
 
     inverse, bias = inv_ref[...], bias_ref[...]
@@ -179,9 +226,8 @@
     ]
 
 
-def first_layer(place, offsets_next, state, inv, gain, qkv, o_weights, fetched, gain_next):
+def first_layer(place, offsets_next, state, inv, gain, bias, qkv, o_weights, fetched, gain_next):
     rows, width = state.shape
-    keys = 256
     return pl.pallas_call(
         first_kernel,
         grid=(HEADS // PACK,),
@@ -194,6 +240,7 @@
             SMEM,
             pl.BlockSpec((rows, PACK * DIM), lambda i: (0, i)),
             pl.BlockSpec((rows, DIM), lambda i: (0, 0)),
+            pl.BlockSpec((rows, KEYS), lambda i: (0, 0)),
             *attention_specs(rows, width),
             pl.BlockSpec((1, width), lambda i: (0, 0)),
         ],
@@ -202,8 +249,7 @@
             pl.BlockSpec((PAD, width), lambda i: (0, 0)),
         ),
         scratch_shapes=[
-            pltpu.VMEM((rows, keys), f32),
-            pltpu.VMEM((keys - rows, width), f32),
+            pltpu.VMEM((KEYS - rows, width), f32),
             pltpu.VMEM((HEADS, rows, DIM), f32),
             pltpu.VMEM((rows, DIM), f32),
             pltpu.VMEM((rows, DIM), f32),
@@ -211,14 +257,14 @@
         compiler_params=pltpu.CompilerParams(vmem_limit_bytes=60 << 20),
         cost_estimate=pl.CostEstimate(flops=800000000, bytes_accessed=5000000, transcendentals=800000),
         name="first_layer",
-    )(place, offsets_next, state, inv, gain, qkv, o_weights, *fetched, gain_next)
+    )(place, offsets_next, state, inv, bias, gain, qkv, o_weights, *fetched, gain_next)
 
 
 def last_kernel(
-    place_ref, first_section_ref,
-    moved_ref, fresh_ref, gain_ref, qkv_ref, o_ref, chip_ref, first_ref, second_ref, swapped_ref,
+    place_ref, is_first_ref,
+    moved_ref, fresh_ref, bias_ref, gain_ref, qkv_ref, o_ref, chip_ref, first_ref, second_ref, swapped_ref,
     out_ref,
-    bias_ref, packed_ref, state_ref, inv_ref,
+    packed_ref, state_ref, inv_ref, sem,
 ):
     step = pl.program_id(0)
     rows, width = moved_ref.shape
@@ -226,16 +272,23 @@
 
     @pl.when(step == 0)
     def _():
-        prepare_attention(
-            place_ref[0], chip_ref, first_ref, second_ref, swapped_ref, bias_ref, packed_ref, count
+        pack_panels(
+            lax.rem(place_ref[0], 2), chip_ref, first_ref, second_ref, swapped_ref, packed_ref, count
         )
-        is_first = first_section_ref[0] == 1
+
+        @pl.when(is_first_ref[0] == 1)
+        def _():
+            copy = pltpu.make_async_copy(fresh_ref, state_ref, sem)
+            copy.start()
+            copy.wait()
+
+        @pl.when(is_first_ref[0] == 0)
+        def _():
+            state_ref[...] = moved_ref[...]
+
         squares = None
         for head in range(HEADS):
-            cols = slice(head * DIM, (head + 1) * DIM)
-            values = jnp.where(is_first, fresh_ref[:, cols], moved_ref[:, cols])
-            state_ref[:, cols] = values
-            values = values.astype(f32)
+            values = state_ref[:, head * DIM : (head + 1) * DIM].astype(f32)
             squares = values * values if squares is None else squares + values * values
         inverse = inverse_rms(jnp.sum(squares, axis=-1, keepdims=True), width)
         inv_ref[...] = jnp.broadcast_to(inverse, inv_ref.shape)
@@ -252,9 +305,8 @@
         out_ref[:, local_cols[local]] = result
 
 
-def last_layer(place, first_section, moved, fresh, gain, qkv, o_weights, fetched):
+def last_layer(place, is_first, moved, fresh, gain, bias, qkv, o_weights, fetched):
     rows, width = moved.shape
-    keys = 256
     return pl.pallas_call(
         last_kernel,
         grid=(HEADS // PACK,),
@@ -263,20 +315,21 @@
             SMEM,
             SMEM,
             pl.BlockSpec((rows, width), lambda i: (0, 0)),
-            pl.BlockSpec((rows, width), lambda i: (0, 0)),
+            ANY,
+            pl.BlockSpec((rows, KEYS), lambda i: (0, 0)),
             *attention_specs(rows, width),
         ],
         out_specs=pl.BlockSpec((rows, PACK * DIM), lambda i: (0, i)),
         scratch_shapes=[
-            pltpu.VMEM((rows, keys), f32),
-            pltpu.VMEM((keys - rows, width), f32),
+            pltpu.VMEM((KEYS - rows, width), f32),
             pltpu.VMEM((rows, width), bf16),
             pltpu.VMEM((rows, DIM), f32),
+            pltpu.SemaphoreType.DMA,
         ],
-        compiler_params=pltpu.CompilerParams(vmem_limit_bytes=60 << 20),
+        compiler_params=pltpu.CompilerParams(vmem_limit_bytes=48 << 20),
         cost_estimate=pl.CostEstimate(flops=800000000, bytes_accessed=5000000, transcendentals=800000),
         name="last_layer",
-    )(place, first_section, moved, fresh, gain, qkv, o_weights, *fetched)
+    )(place, is_first, moved, fresh, bias, gain, qkv, o_weights, *fetched)
 
 
 def shifted(value, axis, steps):
@@ -322,15 +375,17 @@
     ahead = shifted(ahead, "section", -1)
     gain_next = ahead[:, : HEADS * DIM]
     offsets_next = ahead[0, HEADS * DIM : HEADS * DIM + HEADS].astype(jnp.int32)
+    own_panel, bias = entering_panel(here, is_first.reshape(1), offsets[0], entering, gain)
     output, panel_next = first_layer(
-        here, offsets_next, state, inv, gain, qkv, o_weights, fetched, gain_next
-    )
-    entering_panel, _, _ = norm_panel(offsets[0], entering, gain)
+        here, offsets_next, state, inv, gain, bias, qkv, o_weights, fetched, gain_next
+    )
     moved_panel = shifted(panel_next, "section", 1)
     moved = shifted(output, "section", 1)
-    panel = jnp.where(is_first == 1, entering_panel, moved_panel)
-    fetched = fetch(panel, core)
-    result = last_layer(here, is_first.reshape(1), moved, entering, gain, qkv, o_weights, fetched)
+    panel = jnp.where(is_first == 1, own_panel, moved_panel)
+    fetched = lax.fori_loop(
+        0, 1 + jnp.minimum(offsets[0, 0], 0), lambda _, previous: fetch(panel, core), fetched
+    )
+    result = last_layer(here, is_first.reshape(1), moved, entering, gain, bias, qkv, o_weights, fetched)
     return result[None]
 
 

time: 72.4 us -> 60.1 us (0.83)
  the two profiles are of different devices: /device:TPU:385 before, /device:TPU:401 now
where the time goes in v2:
time: 60.1 us; the launch traced here: 59.2 us
  starting transfers between devices  16.3 us (27%)
  Pallas kernels  14 us (23%)
  blocking collectives  13.9 us (23%)
  waiting for transfers between devices  13.4 us (22%)
  local copies, waits for them, and re-layouts  0.68 us (1%)
  other arithmetic  0.62 us (1%)
    ppermute x4, waiting for transfers between devices, by_core(): return lax.ppermute(value, 'seq', pairs)  10.7 us
    ppermute x4, starting transfers between devices, by_core(): return lax.ppermute(value, 'seq', pairs)  8.38 us
    all_gather x2, blocking collectives, fetch(): swapped = lax.all_gather(mine, 'seq', axis=0, axis_index_groups=cores)  8 us
    ppermute x3, starting transfers between devices, shifted(): lax.ppermute(value, axis, [(source, source + steps) for source in range(f...  7.92 us
    all_gather x2, blocking collectives, fetch(): chip = lax.all_gather(panel, 'seq', axis=0, axis_index_groups=cores)  5.92 us
    pallas_call x1, Pallas kernels, first_layer(): pl.pallas_call(first_kernel, grid=(HEADS // PACK,), out_shape=(jax.ShapeD...  5.21 us
    pallas_call x1, Pallas kernels, last_layer(): pl.pallas_call(last_kernel, grid=(HEADS // PACK,), out_shape=jax.ShapeDty...  5.11 us
    ppermute x3, waiting for transfers between devices, shifted(): lax.ppermute(value, axis, [(source, source + steps) for source in range(f...  2.74 us
  transfers between devices with their start and end apart: 7, of which 6 were waited for; matrix products, arithmetic and copies ran while one was open for 2% of the time, Pallas kernels for 3%

profile of v2, /device:TPU:401, one launch (start us, length us, event | category | flops | bytes accessed | tf_op | source)
XLA Modules:
  0.0 59.2 jit_solution(13397739538501607027)
XLA Ops:
  0.0 2.1 %norm_panel.1 = (bf16[16,2048]{1,0:T(8,128)(2,1)}, f32[192,128]{1,0:T(8,128)}, bf16[1,2176]{1,0:T(2,128)(2,1)}) custom-call(s32[16]{0:T(128)} %bitcast.41, bf16[192,2048]{1,0:T(8,128)(2,1)} %bitcast.29, bf16[1,2048]{1,0:T(2,128)(2,1)} %gain_ref.7), custom_call_target="tpu_custom_call" | custom-call | flops 2000000 | bytes 1000000 | tf_op jit(solution)/shard_map/norm_panel/pallas_call | solution.py:65
  2.1 3.8 %collective-permute-start.2 = (bf16[1,2176]{1,0:T(2,128)(2,1)}, bf16[1,2176]{1,0:T(2,128)(2,1)S(1)}, u32[]{:S(2)}, u32[]{:S(2)}) collective-permute-start(bf16[1,2176]{1,0:T(2,128)(2,1)} %get-tuple-element.104), channel_id=1, source_target_pairs={{1,0},{2,1},{3,2},{4,3},{5,4},{6,5},{7,6},{8,7},{9,8},{10,9},{11,1... | collective-permute-start | bytes 13064 | tf_op jit(solution)/shard_map/ppermute | solution.py:338
  6.0 2.7 %all-gather.2 = bf16[32,2048]{1,0:T(8,128)(2,1)S(1)} all-gather(bf16[16,2048]{1,0:T(8,128)(2,1)} %get-tuple-element.107), channel_id=4, replica_groups={{0,16},{32,48},{64,80},{96,112},{128,144},{160,176},{192,208},{224,240}..., dimensions={0}, use_global_device_ids=true | all-gather | bytes 196608 | tf_op jit(solution)/shard_map/all_gather | solution.py:351
  8.7 0.0 copy-start.10
  8.7 1.3 %collective-permute-start.4 = (bf16[2,16,2048]{2,1,0:T(8,128)(2,1)S(1)}, bf16[2,16,2048]{2,1,0:T(8,128)(2,1)S(1)}, u32[]{:S(2)}, u32[]{:S(2)}) collective-permute-start(bf16[2,16,2048]{2,1,0:T(8,128)(2,1)S(1)} %bitcast.34), channel_id=1, source_target_pairs={{0,64},{32,96},{64,128},{96,160},{128,192},{160,224},{192,256},{22... | collective-permute-start | bytes 393224 | tf_op jit(solution)/shard_map/ppermute | solution.py:345
  10.0 2.9 %collective-permute-start.3 = (bf16[2,16,2048]{2,1,0:T(8,128)(2,1)S(1)}, bf16[2,16,2048]{2,1,0:T(8,128)(2,1)S(1)}, u32[]{:S(2)}, u32[]{:S(2)}) collective-permute-start(bf16[2,16,2048]{2,1,0:T(8,128)(2,1)S(1)} %bitcast.35), channel_id=1, source_target_pairs={{0,32},{32,64},{64,96},{96,128},{128,160},{160,192},{192,224},{224... | collective-permute-start | bytes 393224 | tf_op jit(solution)/shard_map/ppermute | solution.py:345
  12.9 1.5 %entering_panel.1 = (bf16[16,2048]{1,0:T(8,128)(2,1)}, f32[192,256]{1,0:T(8,128)}) custom-call(s32[1]{0:T(128)} %bitcast.2.place_ref, s32[1]{0:T(128)} %bitcast.3.is_first_ref, s32[16]{0:T(128)} %bitcast.42, bf16[192,2048]{1,0:T(8,128)(2,1)} %bitcast.25, bf16[1,2048]{1,0:T(2,128)(2,1)} %gain_ref.7), custom_call_target="tpu_custom_call" | custom-call | flops 2000000 | bytes 1000000 | tf_op jit(solution)/shard_map/entering_panel/pallas_call | solution.py:133
  14.4 0.0 collective-permute-done.2
  14.5 0.6 %slice.13.gain_next_ref = bf16[1,2048]{1,0:T(2,128)(2,1)} slice(bf16[1,2176]{1,0:T(2,128)(2,1)S(1)} %collective-permute-done.2), slice={[0:1], [0:2048]} | slice | bytes 8192 | tf_op jit(solution)/shard_map/slice | solution.py:376
  15.1 0.6 fusion.offsets_ref
  15.6 0.3 collective-permute-done.4.second_ref
  15.9 0.0 copy-start.5
  15.9 2.8 %collective-permute-done.3.first_ref = bf16[2,16,2048]{2,1,0:T(8,128)(2,1)S(1)} collective-permute-done((bf16[2,16,2048]{2,1,0:T(8,128)(2,1)S(1)}, bf16[2,16,2048]{2,1,0:T(8,128)(2,1)S(1)}, u32[]{:S(2)}, u32[]{:S(2)}) %collective-permute-start.3) | collective-permute-done | bytes 131104 | tf_op jit(solution)/shard_map/ppermute | solution.py:345
  18.7 0.0 copy-start.7
  18.8 5.9 %all-gather.3 = bf16[4,16,2048]{2,1,0:T(8,128)(2,1)S(1)} all-gather(bf16[2,16,2048]{2,1,0:T(8,128)(2,1)S(1)} %pad_maximum_fusion.1), channel_id=5, replica_groups={{0,16},{32,48},{64,80},{96,112},{128,144},{160,176},{192,208},{224,240}..., dimensions={0}, use_global_device_ids=true | all-gather | bytes 393216 | tf_op jit(solution)/shard_map/all_gather | solution.py:360
  24.6 0.0 copy-start.9
  24.6 0.0 copy-start.13
  24.6 0.0 copy-start.12
  24.6 0.0 copy-start
  24.6 5.2 %first_layer.1 = (bf16[192,2048]{1,0:T(8,128)(2,1)}, bf16[16,2048]{1,0:T(8,128)(2,1)}) custom-call(s32[1]{0:T(128)} %bitcast.2.place_ref, s32[16]{0:T(128)} %fusion.offsets_ref, bf16[192,2048]{1,0:T(8,128)(2,1)} %bitcast.30, f32[192,128]{1,0:T(8,128)} %get-tuple-element.105.inv_ref, f32[192,256]{1,0:T(8,128)} %get-tuple-element.106.bias_ref, ...), custom_call_target="tpu_custom_call" | custom-call | flops 800000000 | bytes 5000000 | tf_op jit(solution)/shard_map/first_layer/pallas_call | solution.py:231
  29.9 0.0 copy-done.10
  29.9 0.0 copy-done.5
  29.9 0.0 copy-done.7
  29.9 0.0 copy-done.9
  29.9 1.9 %collective-permute-start.6 = (bf16[16,2048]{1,0:T(8,128)(2,1)}, bf16[16,2048]{1,0:T(8,128)(2,1)S(1)}, u32[]{:S(2)}, u32[]{:S(2)}) collective-permute-start(bf16[16,2048]{1,0:T(8,128)(2,1)} %get-tuple-element.110), channel_id=1, source_target_pairs={{0,1},{1,2},{2,3},{3,4},{4,5},{5,6},{6,7},{7,8},{8,9},{9,10},{10,1... | collective-permute-start | bytes 196616 | tf_op jit(solution)/shard_map/ppermute | solution.py:338
  31.8 0.0 copy-done.13
  31.9 2.2 %collective-permute-start.5 = (bf16[192,2048]{1,0:T(8,128)(2,1)}, bf16[192,2048]{1,0:T(8,128)(2,1)}, u32[]{:S(2)}, u32[]{:S(2)}) collective-permute-start(bf16[192,2048]{1,0:T(8,128)(2,1)} %get-tuple-element.108), channel_id=1, source_target_pairs={{0,1},{1,2},{2,3},{3,4},{4,5},{5,6},{6,7},{7,8},{8,9},{9,10},{10,1... | collective-permute-start | bytes 2359304 | tf_op jit(solution)/shard_map/ppermute | solution.py:338
  34.0 2.3 %collective-permute-done.6 = bf16[16,2048]{1,0:T(8,128)(2,1)S(1)} collective-permute-done((bf16[16,2048]{1,0:T(8,128)(2,1)}, bf16[16,2048]{1,0:T(8,128)(2,1)S(1)}, u32[]{:S(2)}, u32[]{:S(2)}) %collective-permute-start.6) | collective-permute-done | bytes 65568 | tf_op jit(solution)/shard_map/ppermute | solution.py:338
  36.3 0.0 copy-done.12
  36.3 0.0 copy-start.1
  36.4 0.0 copy-start.4
  36.4 17.2 %while.18 = (s32[]{:T(128)}, bf16[2,16,2048]{2,1,0:T(8,128)(2,1)}, bf16[2,16,2048]{2,1,0:T(8,128)(2,1)}, bf16[2,16,2048]{2,1,0:T(8,128)(2,1)}, bf16[2,2,16,2048]...) while((s32[]{:T(128)}, bf16[2,16,2048]{2,1,0:T(8,128)(2,1)}, ...), condition=%wide.region_1.2_spmd, body=%wide.region_0.1_spmd.sunk | while | flops 65538 | bytes 3735817 | solution.py:385
  36.4 3.2 %all-gather.6 = bf16[32,2048]{1,0:T(8,128)(2,1)S(1)} all-gather(bf16[16,2048]{1,0:T(8,128)(2,1)S(1)} %get-tuple-element.197), channel_id=2, replica_groups={{0,16},{32,48},{64,80},{96,112},{128,144},{160,176},{192,208},{224,240}..., dimensions={0}, use_global_device_ids=true | all-gather | bytes 196608 | tf_op jit(solution)/shard_map/while/body/all_gather | solution.py:351
  39.6 1.3 %collective-permute-start.1 = (bf16[2,16,2048]{2,1,0:T(8,128)(2,1)S(1)}, bf16[2,16,2048]{2,1,0:T(8,128)(2,1)S(1)}, u32[]{:S(2)}, u32[]{:S(2)}) collective-permute-start(bf16[2,16,2048]{2,1,0:T(8,128)(2,1)S(1)} %bitcast.38), channel_id=1, source_target_pairs={{0,64},{32,96},{64,128},{96,160},{128,192},{160,224},{192,256},{22... | collective-permute-start | bytes 393224 | tf_op jit(solution)/shard_map/while/body/ppermute | solution.py:345
  40.9 2.9 %collective-permute-start = (bf16[2,16,2048]{2,1,0:T(8,128)(2,1)S(1)}, bf16[2,16,2048]{2,1,0:T(8,128)(2,1)S(1)}, u32[]{:S(2)}, u32[]{:S(2)}) collective-permute-start(bf16[2,16,2048]{2,1,0:T(8,128)(2,1)S(1)} %bitcast.39), channel_id=1, source_target_pairs={{0,32},{32,64},{64,96},{96,128},{128,160},{160,192},{192,224},{224... | collective-permute-start | bytes 393224 | tf_op jit(solution)/shard_map/while/body/ppermute | solution.py:345
  43.8 3.4 %collective-permute-done.1 = bf16[2,16,2048]{2,1,0:T(8,128)(2,1)S(1)} collective-permute-done((bf16[2,16,2048]{2,1,0:T(8,128)(2,1)S(1)}, bf16[2,16,2048]{2,1,0:T(8,128)(2,1)S(1)}, u32[]{:S(2)}, u32[]{:S(2)}) %collective-permute-start.1) | collective-permute-done | bytes 131104 | tf_op jit(solution)/shard_map/while/body/ppermute | solution.py:345
  47.2 4.2 %collective-permute-done = bf16[2,16,2048]{2,1,0:T(8,128)(2,1)S(1)} collective-permute-done((bf16[2,16,2048]{2,1,0:T(8,128)(2,1)S(1)}, bf16[2,16,2048]{2,1,0:T(8,128)(2,1)S(1)}, u32[]{:S(2)}, u32[]{:S(2)}) %collective-permute-start) | collective-permute-done | bytes 131104 | tf_op jit(solution)/shard_map/while/body/ppermute | solution.py:345
  51.4 2.1 %all-gather.7 = bf16[4,16,2048]{2,1,0:T(8,128)(2,1)} all-gather(bf16[2,16,2048]{2,1,0:T(8,128)(2,1)S(1)} %pad_maximum_fusion.3), channel_id=3, replica_groups={{0,16},{32,48},{64,80},{96,112},{128,144},{160,176},{192,208},{224,240}..., dimensions={0}, use_global_device_ids=true | all-gather | bytes 393216 | tf_op jit(solution)/shard_map/while/body/all_gather | solution.py:360
  53.6 0.0 copy-done.11
  53.6 0.0 copy-done.6
  53.6 0.0 copy-done.8
  53.6 0.5 collective-permute-done.5.moved_ref
  54.0 0.0 copy-done
  54.0 0.0 copy-done.3
  54.1 0.0 copy-done.2
  54.1 0.0 copy-done.1
  54.1 0.0 copy-done.4
  54.1 5.1 %last_layer.1 = bf16[192,2048]{1,0:T(8,128)(2,1)} custom-call(s32[1]{0:T(128)} %bitcast.2.place_ref, s32[1]{0:T(128)} %bitcast.3.is_first_ref, bf16[192,2048]{1,0:T(8,128)(2,1)} %collective-permute-done.5.moved_ref, bf16[192,2048]{1,0:T(8,128)(2,1)S(1)} %bitcast.26, f32[192,256]{1,0:T(8,128)S(1)} %copy-done.3, bf16[1,2048]{1,0:T(2,128)(2,1)S(1)} %copy-done.4, ...), custom_call_target="tpu_custom_call" | custom-call | flops 800000000 | bytes 5000000 | tf_op jit(solution)/shard_map/last_layer/pallas_call | solution.py:310
  (12 shorter events, 0.1 us)
Async XLA Ops:
  2.1 12.3 %collective-permute-start.2 = (bf16[1,2176]{1,0:T(2,128)(2,1)}, bf16[1,2176]{1,0:T(2,128)(2,1)S(1)}, u32[]{:S(2)}, u32[]{:S(2)}) collective-permute-start(bf16[1,2176]{1,0:T(2,128)(2,1)} %get-tuple-element.104), channel_id=1, source_target_pairs={{1,0},{2,1},{3,2},{4,3},{5,4},{6,5},{7,6},{8,7},{9,8},{10,9},{11,1... | collective-permute-start | bytes 13064 | tf_op jit(solution)/shard_map/ppermute | solution.py:338
  8.7 21.2 %copy-start.10 = (bf16[32,2048]{1,0:T(8,128)(2,1)}, bf16[32,2048]{1,0:T(8,128)(2,1)S(1)}, u32[]{:S(2)}) copy-start(bf16[32,2048]{1,0:T(8,128)(2,1)S(1)} %all-gather.2) | copy-start | bytes 393220
  8.7 7.2 %collective-permute-start.4 = (bf16[2,16,2048]{2,1,0:T(8,128)(2,1)S(1)}, bf16[2,16,2048]{2,1,0:T(8,128)(2,1)S(1)}, u32[]{:S(2)}, u32[]{:S(2)}) collective-permute-start(bf16[2,16,2048]{2,1,0:T(8,128)(2,1)S(1)} %bitcast.34), channel_id=1, source_target_pairs={{0,64},{32,96},{64,128},{96,160},{128,192},{160,224},{192,256},{22... | collective-permute-start | bytes 393224 | tf_op jit(solution)/shard_map/ppermute | solution.py:345
  10.0 8.7 %collective-permute-start.3 = (bf16[2,16,2048]{2,1,0:T(8,128)(2,1)S(1)}, bf16[2,16,2048]{2,1,0:T(8,128)(2,1)S(1)}, u32[]{:S(2)}, u32[]{:S(2)}) collective-permute-start(bf16[2,16,2048]{2,1,0:T(8,128)(2,1)S(1)} %bitcast.35), channel_id=1, source_target_pairs={{0,32},{32,64},{64,96},{96,128},{128,160},{160,192},{192,224},{224... | collective-permute-start | bytes 393224 | tf_op jit(solution)/shard_map/ppermute | solution.py:345
  15.9 13.9 %copy-start.5 = (bf16[2,16,2048]{2,1,0:T(8,128)(2,1)}, bf16[2,16,2048]{2,1,0:T(8,128)(2,1)S(1)}, u32[]{:S(2)}) copy-start(bf16[2,16,2048]{2,1,0:T(8,128)(2,1)S(1)} %collective-permute-done.4.second_ref) | copy-start | bytes 393220
  18.7 11.2 %copy-start.7 = (bf16[2,16,2048]{2,1,0:T(8,128)(2,1)}, bf16[2,16,2048]{2,1,0:T(8,128)(2,1)S(1)}, u32[]{:S(2)}) copy-start(bf16[2,16,2048]{2,1,0:T(8,128)(2,1)S(1)} %collective-permute-done.3.first_ref) | copy-start | bytes 393220
  24.6 5.3 %copy-start.9 = (bf16[4,16,2048]{2,1,0:T(8,128)(2,1)}, bf16[4,16,2048]{2,1,0:T(8,128)(2,1)S(1)}, u32[]{:S(2)}) copy-start(bf16[4,16,2048]{2,1,0:T(8,128)(2,1)S(1)} %all-gather.3) | copy-start | bytes 786436
  24.6 7.2 %copy-start.13 = (s32[1,16]{1,0:T(1,128)S(1)}, s32[1,16]{1,0:T(1,128)}, u32[]{:S(2)}) copy-start(s32[1,16]{1,0:T(1,128)} %param.13) | copy-start | bytes 196
  24.6 11.7 %copy-start.12 = (bf16[16,2048]{1,0:T(8,128)(2,1)S(1)}, bf16[16,2048]{1,0:T(8,128)(2,1)}, u32[]{:S(2)}) copy-start(bf16[16,2048]{1,0:T(8,128)(2,1)} %get-tuple-element.109) | copy-start | bytes 196612
  24.6 29.4 %copy-start = (bf16[1,3,16,128,128]{4,3,2,1,0:T(8,128)(2,1)S(1)}, bf16[1,3,16,128,128]{4,3,2,1,0:T(8,128)(2,1)}, u32[]{:S(2)}) copy-start(bf16[1,3,16,128,128]{4,3,2,1,0:T(8,128)(2,1)} %param.11) | copy-start | bytes 4718596
  24.6 29.4 %copy-start.3 = (f32[192,256]{1,0:T(8,128)S(1)}, f32[192,256]{1,0:T(8,128)}, u32[]{:S(2)}) copy-start(f32[192,256]{1,0:T(8,128)} %get-tuple-element.106.bias_ref) | copy-start | bytes 589828
  29.9 6.4 %collective-permute-start.6 = (bf16[16,2048]{1,0:T(8,128)(2,1)}, bf16[16,2048]{1,0:T(8,128)(2,1)S(1)}, u32[]{:S(2)}, u32[]{:S(2)}) collective-permute-start(bf16[16,2048]{1,0:T(8,128)(2,1)} %get-tuple-element.110), channel_id=1, source_target_pairs={{0,1},{1,2},{2,3},{3,4},{4,5},{5,6},{6,7},{7,8},{8,9},{9,10},{10,1... | collective-permute-start | bytes 196616 | tf_op jit(solution)/shard_map/ppermute | solution.py:338
  31.9 22.2 %collective-permute-start.5 = (bf16[192,2048]{1,0:T(8,128)(2,1)}, bf16[192,2048]{1,0:T(8,128)(2,1)}, u32[]{:S(2)}, u32[]{:S(2)}) collective-permute-start(bf16[192,2048]{1,0:T(8,128)(2,1)} %get-tuple-element.108), channel_id=1, source_target_pairs={{0,1},{1,2},{2,3},{3,4},{4,5},{5,6},{6,7},{7,8},{8,9},{9,10},{10,1... | collective-permute-start | bytes 2359304 | tf_op jit(solution)/shard_map/ppermute | solution.py:338
  36.3 17.7 %copy-start.2 = (bf16[1,16,128,128]{3,2,1,0:T(8,128)(2,1)S(1)}, bf16[1,16,128,128]{3,2,1,0:T(8,128)(2,1)}, u32[]{:S(2)}) copy-start(bf16[1,16,128,128]{3,2,1,0:T(8,128)(2,1)} %param.12) | copy-start | bytes 1572868
  36.3 17.7 %copy-start.1 = (bf16[1,192,2048]{2,1,0:T(8,128)(2,1)S(1)}, bf16[1,192,2048]{2,1,0:T(8,128)(2,1)}, u32[]{:S(2)}) copy-start(bf16[1,192,2048]{2,1,0:T(8,128)(2,1)} %param.9) | copy-start | bytes 2359300
  36.4 17.7 %copy-start.4 = (bf16[1,2048]{1,0:T(2,128)(2,1)S(1)}, bf16[1,2048]{1,0:T(2,128)(2,1)}, u32[]{:S(2)}) copy-start(bf16[1,2048]{1,0:T(2,128)(2,1)} %gain_ref.7) | copy-start | bytes 12292
  39.6 14.0 %copy-start.11 = (bf16[32,2048]{1,0:T(8,128)(2,1)}, bf16[32,2048]{1,0:T(8,128)(2,1)S(1)}, u32[]{:S(2)}) copy-start(bf16[32,2048]{1,0:T(8,128)(2,1)S(1)} %all-gather.6) | copy-start | bytes 393220 | tf_op jit(solution)/shard_map/while
  39.6 7.6 %collective-permute-start.1 = (bf16[2,16,2048]{2,1,0:T(8,128)(2,1)S(1)}, bf16[2,16,2048]{2,1,0:T(8,128)(2,1)S(1)}, u32[]{:S(2)}, u32[]{:S(2)}) collective-permute-start(bf16[2,16,2048]{2,1,0:T(8,128)(2,1)S(1)} %bitcast.38), channel_id=1, source_target_pairs={{0,64},{32,96},{64,128},{96,160},{128,192},{160,224},{192,256},{22... | collective-permute-start | bytes 393224 | tf_op jit(solution)/shard_map/while/body/ppermute | solution.py:345
  40.9 10.5 %collective-permute-start = (bf16[2,16,2048]{2,1,0:T(8,128)(2,1)S(1)}, bf16[2,16,2048]{2,1,0:T(8,128)(2,1)S(1)}, u32[]{:S(2)}, u32[]{:S(2)}) collective-permute-start(bf16[2,16,2048]{2,1,0:T(8,128)(2,1)S(1)} %bitcast.39), channel_id=1, source_target_pairs={{0,32},{32,64},{64,96},{96,128},{128,160},{160,192},{192,224},{224... | collective-permute-start | bytes 393224 | tf_op jit(solution)/shard_map/while/body/ppermute | solution.py:345
  47.2 6.4 %copy-start.6 = (bf16[2,16,2048]{2,1,0:T(8,128)(2,1)}, bf16[2,16,2048]{2,1,0:T(8,128)(2,1)S(1)}, u32[]{:S(2)}) copy-start(bf16[2,16,2048]{2,1,0:T(8,128)(2,1)S(1)} %collective-permute-done.1) | copy-start | bytes 393220 | tf_op jit(solution)/shard_map/while
  51.4 2.2 %copy-start.8 = (bf16[2,16,2048]{2,1,0:T(8,128)(2,1)}, bf16[2,16,2048]{2,1,0:T(8,128)(2,1)S(1)}, u32[]{:S(2)}) copy-start(bf16[2,16,2048]{2,1,0:T(8,128)(2,1)S(1)} %collective-permute-done) | copy-start | bytes 393220 | tf_op jit(solution)/shard_map/while

commit v3 on v2

--- a/solution.py
+++ b/solution.py
@@ -30,11 +30,11 @@
     return lax.rsqrt(squares * (1.0 / width) + eps)
 
 
-def pick_panel(wide_ref, inv_ref, gain_ref, offsets_ref, panel_ref):
+def pick_panel(wide_ref, inv_ref, gain_ref, offset_of, panel_ref):
     count = wide_ref.shape[1] // RATE
     for head in range(HEADS):
         cols = slice(head * DIM, (head + 1) * DIM)
-        where = pl.ds(offsets_ref[head], count, stride=RATE)
+        where = pl.ds(offset_of(head), count, stride=RATE)
         picked = wide_ref[head, where, :] * inv_ref[where, :] * gain_ref[:, cols].astype(f32)
         panel_ref[:, cols] = jnp.concatenate(
             [picked, jnp.zeros((PAD - count, DIM), f32)], axis=0
@@ -57,7 +57,7 @@
         squares = values * values if squares is None else squares + values * values
     inverse = inverse_rms(jnp.sum(squares, axis=-1, keepdims=True), width)
     inv_ref[...] = jnp.broadcast_to(inverse, inv_ref.shape)
-    pick_panel(wide_ref, inv_ref, gain_ref, offsets_ref, panel_ref)
+    pick_panel(wide_ref, inv_ref, gain_ref, lambda head: offsets_ref[head], panel_ref)
 
 
 def norm_panel(offsets, state, gain):
@@ -121,7 +121,7 @@
             squares = values * values if squares is None else squares + values * values
         inverse = inverse_rms(jnp.sum(squares, axis=-1, keepdims=True), HEADS * DIM)
         inv_ref[...] = jnp.broadcast_to(inverse, inv_ref.shape)
-        pick_panel(wide_ref, inv_ref, gain_ref, offsets_ref, panel_ref)
+        pick_panel(wide_ref, inv_ref, gain_ref, lambda head: offsets_ref[head], panel_ref)
 
     @pl.when(is_first_ref[0] == 0)
     def _():
@@ -176,10 +176,10 @@
 
 
 def first_kernel(
-    place_ref, offsets_ref,
+    place_ref,
     state_ref, inv_ref, bias_ref, gain_ref, qkv_ref, o_ref, chip_ref, first_ref, second_ref, swapped_ref, gain_next_ref,
     out_ref, panel_ref,
-    packed_ref, wide_ref, squares_ref, inv_next_ref,
+    packed_ref, wide_ref, squares_ref, inv_next_ref, phases_ref, phases_smem, sem,
 ):
     step = pl.program_id(0)
     rows = state_ref.shape[0]
@@ -187,6 +187,8 @@
 
     @pl.when(step == 0)
     def _():
+        phases_ref[...] = gain_next_ref[:, HEADS * DIM :].astype(f32).astype(jnp.int32)
+        pltpu.make_async_copy(phases_ref, phases_smem, sem).start()
         pack_panels(
             lax.rem(place_ref[0], 2), chip_ref, first_ref, second_ref, swapped_ref, packed_ref, count
         )
@@ -211,7 +213,8 @@
     def _():
         total = jnp.sum(squares_ref[...], axis=-1, keepdims=True)
         inv_next_ref[...] = jnp.broadcast_to(inverse_rms(total, HEADS * DIM), inv_next_ref.shape)
-        pick_panel(wide_ref, inv_next_ref, gain_next_ref, offsets_ref, panel_ref)
+        pltpu.make_async_copy(phases_ref, phases_smem, sem).wait()
+        pick_panel(wide_ref, inv_next_ref, gain_next_ref, lambda head: phases_smem[0, head], panel_ref)
 
 
 def attention_specs(rows, width):
@@ -226,7 +229,7 @@
     ]
 
 
-def first_layer(place, offsets_next, state, inv, gain, bias, qkv, o_weights, fetched, gain_next):
+def first_layer(place, state, inv, gain, bias, qkv, o_weights, fetched, gain_next):
     rows, width = state.shape
     return pl.pallas_call(
         first_kernel,
@@ -237,12 +240,11 @@
         ),
         in_specs=[
             SMEM,
-            SMEM,
             pl.BlockSpec((rows, PACK * DIM), lambda i: (0, i)),
             pl.BlockSpec((rows, DIM), lambda i: (0, 0)),
             pl.BlockSpec((rows, KEYS), lambda i: (0, 0)),
             *attention_specs(rows, width),
-            pl.BlockSpec((1, width), lambda i: (0, 0)),
+            pl.BlockSpec((1, width + DIM), lambda i: (0, 0)),
         ],
         out_specs=(
             pl.BlockSpec((rows, PACK * DIM), lambda i: (0, i)),
@@ -253,78 +255,77 @@
             pltpu.VMEM((HEADS, rows, DIM), f32),
             pltpu.VMEM((rows, DIM), f32),
             pltpu.VMEM((rows, DIM), f32),
+            pltpu.VMEM((1, DIM), jnp.int32),
+            pltpu.SMEM((1, DIM), jnp.int32),
+            pltpu.SemaphoreType.DMA,
         ],
         compiler_params=pltpu.CompilerParams(vmem_limit_bytes=60 << 20),
         cost_estimate=pl.CostEstimate(flops=800000000, bytes_accessed=5000000, transcendentals=800000),
         name="first_layer",
-    )(place, offsets_next, state, inv, bias, gain, qkv, o_weights, *fetched, gain_next)
+    )(place, state, inv, bias, gain, qkv, o_weights, *fetched, gain_next)
 
 
 def last_kernel(
     place_ref, is_first_ref,
     moved_ref, fresh_ref, bias_ref, gain_ref, qkv_ref, o_ref, chip_ref, first_ref, second_ref, swapped_ref,
     out_ref,
-    packed_ref, state_ref, inv_ref, sem,
+    packed_ref, state_ref, out_buf, sem, out_sems,
 ):
-    step = pl.program_id(0)
     rows, width = moved_ref.shape
-    count = rows // RATE
-
-    @pl.when(step == 0)
-    def _():
-        pack_panels(
-            lax.rem(place_ref[0], 2), chip_ref, first_ref, second_ref, swapped_ref, packed_ref, count
+
+    @pl.when(is_first_ref[0] == 1)
+    def _():
+        copy = pltpu.make_async_copy(fresh_ref, state_ref, sem)
+        copy.start()
+        copy.wait()
+
+    @pl.when(is_first_ref[0] == 0)
+    def _():
+        state_ref[...] = moved_ref[...]
+
+    pack_panels(
+        lax.rem(place_ref[0], 2), chip_ref, first_ref, second_ref, swapped_ref, packed_ref, rows // RATE
+    )
+    squares = None
+    for head in range(HEADS):
+        values = state_ref[:, head * DIM : (head + 1) * DIM].astype(f32)
+        squares = values * values if squares is None else squares + values * values
+    inverse = jnp.broadcast_to(
+        inverse_rms(jnp.sum(squares, axis=-1, keepdims=True), width), (rows, DIM)
+    )
+    bias = bias_ref[...]
+    outs = []
+    for group in range(HEADS // PACK):
+        heads = range(group * PACK, (group + 1) * PACK)
+        cols = [slice(head * DIM, (head + 1) * DIM) for head in heads]
+        results = some_heads(
+            [state_ref[:, c] for c in cols], inverse, [gain_ref[:, c] for c in cols],
+            [qkv_ref[0, h] for h in heads], [qkv_ref[1, h] for h in heads], [qkv_ref[2, h] for h in heads],
+            [o_ref[h] for h in heads], [packed_ref[:, c] for c in cols], bias,
         )
-
-        @pl.when(is_first_ref[0] == 1)
-        def _():
-            copy = pltpu.make_async_copy(fresh_ref, state_ref, sem)
-            copy.start()
-            copy.wait()
-
-        @pl.when(is_first_ref[0] == 0)
-        def _():
-            state_ref[...] = moved_ref[...]
-
-        squares = None
-        for head in range(HEADS):
-            values = state_ref[:, head * DIM : (head + 1) * DIM].astype(f32)
-            squares = values * values if squares is None else squares + values * values
-        inverse = inverse_rms(jnp.sum(squares, axis=-1, keepdims=True), width)
-        inv_ref[...] = jnp.broadcast_to(inverse, inv_ref.shape)
-
-    inverse, bias = inv_ref[...], bias_ref[...]
-    local_cols = [slice(local * DIM, (local + 1) * DIM) for local in range(PACK)]
-    there = [pl.ds(pl.multiple_of((step * PACK + local) * DIM, DIM), DIM) for local in range(PACK)]
-    results = some_heads(
-        [state_ref[:, at] for at in there], inverse, [gain_ref[:, cols] for cols in local_cols],
-        [qkv_ref[0, i] for i in range(PACK)], [qkv_ref[1, i] for i in range(PACK)], [qkv_ref[2, i] for i in range(PACK)],
-        [o_ref[i] for i in range(PACK)], [packed_ref[:, at] for at in there], bias,
-    )
-    for local, result in enumerate(results):
-        out_ref[:, local_cols[local]] = result
+        for c, result in zip(cols, results):
+            out_buf[:, c] = result
+        block = slice(group * PACK * DIM, (group + 1) * PACK * DIM)
+        out = pltpu.make_async_copy(out_buf.at[:, block], out_ref.at[:, block], out_sems.at[group])
+        out.start()
+        outs.append(out)
+    for out in outs:
+        out.wait()
 
 
 def last_layer(place, is_first, moved, fresh, gain, bias, qkv, o_weights, fetched):
     rows, width = moved.shape
     return pl.pallas_call(
         last_kernel,
-        grid=(HEADS // PACK,),
         out_shape=jax.ShapeDtypeStruct((rows, width), bf16),
-        in_specs=[
-            SMEM,
-            SMEM,
-            pl.BlockSpec((rows, width), lambda i: (0, 0)),
-            ANY,
-            pl.BlockSpec((rows, KEYS), lambda i: (0, 0)),
-            *attention_specs(rows, width),
-        ],
-        out_specs=pl.BlockSpec((rows, PACK * DIM), lambda i: (0, i)),
+        in_specs=[SMEM, SMEM, VMEM, ANY, *[VMEM] * 8],
+        out_specs=ANY,
         scratch_shapes=[
             pltpu.VMEM((KEYS - rows, width), f32),
             pltpu.VMEM((rows, width), bf16),
-            pltpu.VMEM((rows, DIM), f32),
+            pltpu.VMEM((rows, width), bf16),
             pltpu.SemaphoreType.DMA,
+            pltpu.SemaphoreType.DMA((HEADS // PACK,)),
         ],
         compiler_params=pltpu.CompilerParams(vmem_limit_bytes=48 << 20),
         cost_estimate=pl.CostEstimate(flops=800000000, bytes_accessed=5000000, transcendentals=800000),
@@ -345,7 +346,7 @@
     return lax.ppermute(value, "seq", pairs)
 
 
-def fetch(panel, core):
+def fetch(panel, core, beside=None):
     count = lax.axis_size("seq")
     cores = [[chip, chip + 1] for chip in range(0, count, 2)]
     chip = lax.all_gather(panel, "seq", axis=0, axis_index_groups=cores)
@@ -357,8 +358,10 @@
             lax.dynamic_index_in_dim(second, 1 - core, 0, keepdims=False),
         ]
     )
+    if beside is not None:
+        mine, beside = lax.optimization_barrier((mine, beside))
     swapped = lax.all_gather(mine, "seq", axis=0, axis_index_groups=cores)
-    return chip, first, second, swapped
+    return (chip, first, second, swapped) if beside is None else ((chip, first, second, swapped), beside)
 
 
 def on_device(slabs, fresh, norm_gain, qkv_proj, o_proj, offsets):
@@ -371,13 +374,10 @@
     gain, qkv, o_weights = norm_gain, qkv_proj[0], o_proj[0]
 
     panel, inv, ahead = norm_panel(offsets[0], state, gain)
-    fetched = fetch(panel, core)
-    ahead = shifted(ahead, "section", -1)
-    gain_next = ahead[:, : HEADS * DIM]
-    offsets_next = ahead[0, HEADS * DIM : HEADS * DIM + HEADS].astype(jnp.int32)
+    fetched, ahead = fetch(panel, core, shifted(ahead, "section", -1))
     own_panel, bias = entering_panel(here, is_first.reshape(1), offsets[0], entering, gain)
     output, panel_next = first_layer(
-        here, offsets_next, state, inv, gain, bias, qkv, o_weights, fetched, gain_next
+        here, state, inv, gain, bias, qkv, o_weights, fetched, ahead
     )
     moved_panel = shifted(panel_next, "section", 1)
     moved = shifted(output, "section", 1)

time: 60.1 us -> 57.4 us (0.955)
  the two profiles are of different devices: /device:TPU:401 before, /device:TPU:134 now
where the time goes in v3:
time: 57.4 us; the launch traced here: 57 us
  starting transfers between devices  25.4 us (44%)
  Pallas kernels  13.6 us (24%)
  waiting for transfers between devices  9.27 us (16%)
  blocking collectives  8.24 us (14%)
    ppermute x4, starting transfers between devices, by_core(): return lax.ppermute(value, 'seq', pairs)  15.7 us
    ppermute x3, starting transfers between devices, shifted(): lax.ppermute(value, axis, [(source, source + steps) for source in range(f...  9.67 us
    ppermute x3, waiting for transfers between devices, shifted(): lax.ppermute(value, axis, [(source, source + steps) for source in range(f...  6.77 us
    pallas_call x1, Pallas kernels, first_layer(): pl.pallas_call(first_kernel, grid=(HEADS // PACK,), out_shape=(jax.ShapeD...  5.23 us
    pallas_call x1, Pallas kernels, last_layer(): pl.pallas_call(last_kernel, out_shape=jax.ShapeDtypeStruct((rows, width),...  4.74 us
    all_gather x2, blocking collectives, fetch(): chip = lax.all_gather(panel, 'seq', axis=0, axis_index_groups=cores)  4.13 us
    all_gather x2, blocking collectives, fetch(): swapped = lax.all_gather(mine, 'seq', axis=0, axis_index_groups=cores)  4.11 us
    ppermute x4, waiting for transfers between devices, by_core(): return lax.ppermute(value, 'seq', pairs)  2.49 us
  transfers between devices with their start and end apart: 7, of which 4 were waited for; matrix products, arithmetic and copies ran while one was open for 0% of the time, Pallas kernels for 3%

profile of v3, /device:TPU:134, one launch (start us, length us, event | category | flops | bytes accessed | tf_op | source)
XLA Modules:
  0.0 57.0 jit_solution(4974486087054451452)
XLA Ops:
  0.0 2.1 %norm_panel.1 = (bf16[16,2048]{1,0:T(8,128)(2,1)}, f32[192,128]{1,0:T(8,128)}, bf16[1,2176]{1,0:T(2,128)(2,1)}) custom-call(s32[16]{0:T(128)} %bitcast.36, bf16[192,2048]{1,0:T(8,128)(2,1)} %bitcast.24, bf16[1,2048]{1,0:T(2,128)(2,1)} %gain_ref.7), custom_call_target="tpu_custom_call" | custom-call | flops 2000000 | bytes 1000000 | tf_op jit(solution)/shard_map/norm_panel/pallas_call | solution.py:65
  2.1 2.1 %all-gather.2 = bf16[32,2048]{1,0:T(8,128)(2,1)S(1)} all-gather(bf16[16,2048]{1,0:T(8,128)(2,1)} %get-tuple-element.108), channel_id=4, replica_groups={{0,16},{32,48},{64,80},{96,112},{128,144},{160,176},{192,208},{224,240}..., dimensions={0}, use_global_device_ids=true | all-gather | bytes 196608 | tf_op jit(solution)/shard_map/all_gather | solution.py:352
  4.2 0.0 copy-start.10
  4.2 4.3 %collective-permute-start.3 = (bf16[2,16,2048]{2,1,0:T(8,128)(2,1)S(1)}, bf16[2,16,2048]{2,1,0:T(8,128)(2,1)S(1)}, u32[]{:S(2)}, u32[]{:S(2)}) collective-permute-start(bf16[2,16,2048]{2,1,0:T(8,128)(2,1)S(1)} %bitcast.29), channel_id=1, source_target_pairs={{0,64},{32,96},{64,128},{96,160},{128,192},{160,224},{192,256},{22... | collective-permute-start | bytes 393224 | tf_op jit(solution)/shard_map/ppermute | solution.py:346
  8.6 4.0 %collective-permute-start.2 = (bf16[2,16,2048]{2,1,0:T(8,128)(2,1)S(1)}, bf16[2,16,2048]{2,1,0:T(8,128)(2,1)S(1)}, u32[]{:S(2)}, u32[]{:S(2)}) collective-permute-start(bf16[2,16,2048]{2,1,0:T(8,128)(2,1)S(1)} %bitcast.30), channel_id=1, source_target_pairs={{0,32},{32,64},{64,96},{96,128},{128,160},{160,192},{192,224},{224... | collective-permute-start | bytes 393224 | tf_op jit(solution)/shard_map/ppermute | solution.py:346
  12.6 2.0 %collective-permute-start.4 = (bf16[1,2176]{1,0:T(2,128)(2,1)}, bf16[1,2176]{1,0:T(2,128)(2,1)S(1)}, u32[]{:S(2)}, u32[]{:S(2)}) collective-permute-start(bf16[1,2176]{1,0:T(2,128)(2,1)} %get-tuple-element.109), channel_id=1, source_target_pairs={{1,0},{2,1},{3,2},{4,3},{5,4},{6,5},{7,6},{8,7},{9,8},{10,9},{11,1... | collective-permute-start | bytes 13064 | tf_op jit(solution)/shard_map/ppermute | solution.py:339
  14.6 1.5 %entering_panel.1 = (bf16[16,2048]{1,0:T(8,128)(2,1)}, f32[192,256]{1,0:T(8,128)}) custom-call(s32[1]{0:T(128)} %bitcast.2.place_ref, s32[1]{0:T(128)} %bitcast.3.is_first_ref, s32[16]{0:T(128)} %bitcast.37, bf16[192,2048]{1,0:T(8,128)(2,1)} %bitcast.20, bf16[1,2048]{1,0:T(2,128)(2,1)} %gain_ref.7), custom_call_target="tpu_custom_call" | custom-call | flops 2000000 | bytes 1000000 | tf_op jit(solution)/shard_map/entering_panel/pallas_call | solution.py:133
  16.1 0.0 collective-permute-done.3.second_ref
  16.1 0.0 copy-start.5
  16.2 0.0 collective-permute-done.2.first_ref
  16.2 0.0 copy-start.7
  16.2 2.1 %collective-permute-done.4.gain_next_ref = bf16[1,2176]{1,0:T(2,128)(2,1)S(1)} collective-permute-done((bf16[1,2176]{1,0:T(2,128)(2,1)}, bf16[1,2176]{1,0:T(2,128)(2,1)S(1)}, u32[]{:S(2)}, u32[]{:S(2)}) %collective-permute-start.4) | collective-permute-done | bytes 4384 | tf_op jit(solution)/shard_map/ppermute | solution.py:339
  18.3 0.0 copy-start.13
  18.3 2.0 %all-gather.3 = bf16[4,16,2048]{2,1,0:T(8,128)(2,1)S(1)} all-gather(bf16[2,16,2048]{2,1,0:T(8,128)(2,1)S(1)} %pad_maximum_fusion.1), channel_id=5, replica_groups={{0,16},{32,48},{64,80},{96,112},{128,144},{160,176},{192,208},{224,240}..., dimensions={0}, use_global_device_ids=true | all-gather | bytes 393216 | tf_op jit(solution)/shard_map/all_gather | solution.py:363
  20.3 0.0 copy-start.9
  20.3 0.0 copy-done.13
  20.3 0.0 copy-start
  20.4 0.0 copy-start.3
  20.4 5.2 %first_layer.1 = (bf16[192,2048]{1,0:T(8,128)(2,1)}, bf16[16,2048]{1,0:T(8,128)(2,1)}) custom-call(s32[1]{0:T(128)} %bitcast.2.place_ref, bf16[192,2048]{1,0:T(8,128)(2,1)} %bitcast.25, f32[192,128]{1,0:T(8,128)} %get-tuple-element.106.inv_ref, f32[192,256]{1,0:T(8,128)} %get-tuple-element.107.bias_ref, bf16[1,2048]{1,0:T(2,128)(2,1)} %gain_ref.7, ...), custom_call_target="tpu_custom_call" | custom-call | flops 800000000 | bytes 5000000 | tf_op jit(solution)/shard_map/first_layer/pallas_call | solution.py:234
  25.6 0.0 copy-done.10
  25.6 0.0 copy-done.5
  25.6 0.0 copy-done.7
  25.6 0.0 copy-done.9
  25.6 3.8 %collective-permute-start.6 = (bf16[16,2048]{1,0:T(8,128)(2,1)}, bf16[16,2048]{1,0:T(8,128)(2,1)S(1)}, u32[]{:S(2)}, u32[]{:S(2)}) collective-permute-start(bf16[16,2048]{1,0:T(8,128)(2,1)} %get-tuple-element.114), channel_id=1, source_target_pairs={{0,1},{1,2},{2,3},{3,4},{4,5},{5,6},{6,7},{7,8},{8,9},{9,10},{10,1... | collective-permute-start | bytes 196616 | tf_op jit(solution)/shard_map/ppermute | solution.py:339
  29.5 0.0 copy-done.14
  29.5 3.8 %collective-permute-start.5 = (bf16[192,2048]{1,0:T(8,128)(2,1)}, bf16[192,2048]{1,0:T(8,128)(2,1)}, u32[]{:S(2)}, u32[]{:S(2)}) collective-permute-start(bf16[192,2048]{1,0:T(8,128)(2,1)} %get-tuple-element.112), channel_id=1, source_target_pairs={{0,1},{1,2},{2,3},{3,4},{4,5},{5,6},{6,7},{7,8},{8,9},{9,10},{10,1... | collective-permute-start | bytes 2359304 | tf_op jit(solution)/shard_map/ppermute | solution.py:339
  33.4 0.0 collective-permute-done.6
  33.4 0.0 copy-done.12
  33.4 0.0 copy-start.2
  33.4 0.0 copy-start.1
  33.4 0.0 copy-start.4
  33.4 14.2 %while.18 = (s32[]{:T(128)}, bf16[2,16,2048]{2,1,0:T(8,128)(2,1)}, bf16[2,16,2048]{2,1,0:T(8,128)(2,1)}, bf16[2,16,2048]{2,1,0:T(8,128)(2,1)}, bf16[2,2,16,2048]...) while((s32[]{:T(128)}, bf16[2,16,2048]{2,1,0:T(8,128)(2,1)}, ...), condition=%wide.region_1.2_spmd, body=%wide.region_0.1_spmd.sunk | while | flops 65538 | bytes 3735817 | solution.py:385
  33.5 2.0 %all-gather.6 = bf16[32,2048]{1,0:T(8,128)(2,1)S(1)} all-gather(bf16[16,2048]{1,0:T(8,128)(2,1)S(1)} %get-tuple-element.201), channel_id=2, replica_groups={{0,16},{32,48},{64,80},{96,112},{128,144},{160,176},{192,208},{224,240}..., dimensions={0}, use_global_device_ids=true | all-gather | bytes 196608 | tf_op jit(solution)/shard_map/while/body/all_gather | solution.py:352
  35.5 2.8 %collective-permute-start.1 = (bf16[2,16,2048]{2,1,0:T(8,128)(2,1)S(1)}, bf16[2,16,2048]{2,1,0:T(8,128)(2,1)S(1)}, u32[]{:S(2)}, u32[]{:S(2)}) collective-permute-start(bf16[2,16,2048]{2,1,0:T(8,128)(2,1)S(1)} %bitcast.33), channel_id=1, source_target_pairs={{0,64},{32,96},{64,128},{96,160},{128,192},{160,224},{192,256},{22... | collective-permute-start | bytes 393224 | tf_op jit(solution)/shard_map/while/body/ppermute | solution.py:346
  38.3 4.6 %collective-permute-start = (bf16[2,16,2048]{2,1,0:T(8,128)(2,1)S(1)}, bf16[2,16,2048]{2,1,0:T(8,128)(2,1)S(1)}, u32[]{:S(2)}, u32[]{:S(2)}) collective-permute-start(bf16[2,16,2048]{2,1,0:T(8,128)(2,1)S(1)} %bitcast.34), channel_id=1, source_target_pairs={{0,32},{32,64},{64,96},{96,128},{128,160},{160,192},{192,224},{224... | collective-permute-start | bytes 393224 | tf_op jit(solution)/shard_map/while/body/ppermute | solution.py:346
  42.9 0.9 %collective-permute-done.1 = bf16[2,16,2048]{2,1,0:T(8,128)(2,1)S(1)} collective-permute-done((bf16[2,16,2048]{2,1,0:T(8,128)(2,1)S(1)}, bf16[2,16,2048]{2,1,0:T(8,128)(2,1)S(1)}, u32[]{:S(2)}, u32[]{:S(2)}) %collective-permute-start.1) | collective-permute-done | bytes 131104 | tf_op jit(solution)/shard_map/while/body/ppermute | solution.py:346
  43.9 1.6 %collective-permute-done = bf16[2,16,2048]{2,1,0:T(8,128)(2,1)S(1)} collective-permute-done((bf16[2,16,2048]{2,1,0:T(8,128)(2,1)S(1)}, bf16[2,16,2048]{2,1,0:T(8,128)(2,1)S(1)}, u32[]{:S(2)}, u32[]{:S(2)}) %collective-permute-start) | collective-permute-done | bytes 131104 | tf_op jit(solution)/shard_map/while/body/ppermute | solution.py:346
  45.5 2.1 %all-gather.7 = bf16[4,16,2048]{2,1,0:T(8,128)(2,1)} all-gather(bf16[2,16,2048]{2,1,0:T(8,128)(2,1)S(1)} %pad_maximum_fusion.3), channel_id=3, replica_groups={{0,16},{32,48},{64,80},{96,112},{128,144},{160,176},{192,208},{224,240}..., dimensions={0}, use_global_device_ids=true | all-gather | bytes 393216 | tf_op jit(solution)/shard_map/while/body/all_gather | solution.py:363
  47.6 0.0 copy-done.11
  47.6 0.0 copy-done.6
  47.6 0.0 copy-done.8
  47.6 4.7 %collective-permute-done.5.moved_ref = bf16[192,2048]{1,0:T(8,128)(2,1)} collective-permute-done((bf16[192,2048]{1,0:T(8,128)(2,1)}, bf16[192,2048]{1,0:T(8,128)(2,1)}, u32[]{:S(2)}, u32[]{:S(2)}) %collective-permute-start.5) | collective-permute-done | bytes 786464 | tf_op jit(solution)/shard_map/ppermute | solution.py:339
  52.3 0.0 copy-done
  52.3 0.0 copy-done.3
  52.3 0.0 copy-done.2
  52.3 0.0 copy-done.1
  52.3 0.0 copy-done.4
  52.3 4.7 %last_layer.1 = bf16[192,2048]{1,0:T(8,128)(2,1)} custom-call(s32[1]{0:T(128)} %bitcast.2.place_ref, s32[1]{0:T(128)} %bitcast.3.is_first_ref, bf16[192,2048]{1,0:T(8,128)(2,1)} %collective-permute-done.5.moved_ref, bf16[192,2048]{1,0:T(8,128)(2,1)S(1)} %bitcast.21, f32[192,256]{1,0:T(8,128)S(1)} %copy-done.3, bf16[1,2048]{1,0:T(2,128)(2,1)S(1)} %copy-done.4, ...), custom_call_target="tpu_custom_call" | custom-call | flops 800000000 | bytes 5000000 | tf_op jit(solution)/shard_map/last_layer/pallas_call | solution.py:318
  (12 shorter events, 0.1 us)
Async XLA Ops:
  4.2 21.4 %copy-start.10 = (bf16[32,2048]{1,0:T(8,128)(2,1)}, bf16[32,2048]{1,0:T(8,128)(2,1)S(1)}, u32[]{:S(2)}) copy-start(bf16[32,2048]{1,0:T(8,128)(2,1)S(1)} %all-gather.2) | copy-start | bytes 393220
  4.2 11.9 %collective-permute-start.3 = (bf16[2,16,2048]{2,1,0:T(8,128)(2,1)S(1)}, bf16[2,16,2048]{2,1,0:T(8,128)(2,1)S(1)}, u32[]{:S(2)}, u32[]{:S(2)}) collective-permute-start(bf16[2,16,2048]{2,1,0:T(8,128)(2,1)S(1)} %bitcast.29), channel_id=1, source_target_pairs={{0,64},{32,96},{64,128},{96,160},{128,192},{160,224},{192,256},{22... | collective-permute-start | bytes 393224 | tf_op jit(solution)/shard_map/ppermute | solution.py:346
  8.6 7.6 %collective-permute-start.2 = (bf16[2,16,2048]{2,1,0:T(8,128)(2,1)S(1)}, bf16[2,16,2048]{2,1,0:T(8,128)(2,1)S(1)}, u32[]{:S(2)}, u32[]{:S(2)}) collective-permute-start(bf16[2,16,2048]{2,1,0:T(8,128)(2,1)S(1)} %bitcast.30), channel_id=1, source_target_pairs={{0,32},{32,64},{64,96},{96,128},{128,160},{160,192},{192,224},{224... | collective-permute-start | bytes 393224 | tf_op jit(solution)/shard_map/ppermute | solution.py:346
  12.6 5.8 %collective-permute-start.4 = (bf16[1,2176]{1,0:T(2,128)(2,1)}, bf16[1,2176]{1,0:T(2,128)(2,1)S(1)}, u32[]{:S(2)}, u32[]{:S(2)}) collective-permute-start(bf16[1,2176]{1,0:T(2,128)(2,1)} %get-tuple-element.109), channel_id=1, source_target_pairs={{1,0},{2,1},{3,2},{4,3},{5,4},{6,5},{7,6},{8,7},{9,8},{10,9},{11,1... | collective-permute-start | bytes 13064 | tf_op jit(solution)/shard_map/ppermute | solution.py:339
  16.1 9.5 %copy-start.5 = (bf16[2,16,2048]{2,1,0:T(8,128)(2,1)}, bf16[2,16,2048]{2,1,0:T(8,128)(2,1)S(1)}, u32[]{:S(2)}) copy-start(bf16[2,16,2048]{2,1,0:T(8,128)(2,1)S(1)} %collective-permute-done.3.second_ref) | copy-start | bytes 393220
  16.2 9.4 %copy-start.7 = (bf16[2,16,2048]{2,1,0:T(8,128)(2,1)}, bf16[2,16,2048]{2,1,0:T(8,128)(2,1)S(1)}, u32[]{:S(2)}) copy-start(bf16[2,16,2048]{2,1,0:T(8,128)(2,1)S(1)} %collective-permute-done.2.first_ref) | copy-start | bytes 393220
  18.3 2.0 %copy-start.13 = (bf16[1,2176]{1,0:T(2,128)(2,1)}, bf16[1,2176]{1,0:T(2,128)(2,1)S(1)}, u32[]{:S(2)}) copy-start(bf16[1,2176]{1,0:T(2,128)(2,1)S(1)} %collective-permute-done.4.gain_next_ref) | copy-start | bytes 13060
  20.3 5.3 %copy-start.9 = (bf16[4,16,2048]{2,1,0:T(8,128)(2,1)}, bf16[4,16,2048]{2,1,0:T(8,128)(2,1)S(1)}, u32[]{:S(2)}) copy-start(bf16[4,16,2048]{2,1,0:T(8,128)(2,1)S(1)} %all-gather.3) | copy-start | bytes 786436
  20.3 9.1 %copy-start.14 = (s32[1,16]{1,0:T(1,128)S(1)}, s32[1,16]{1,0:T(1,128)}, u32[]{:S(2)}) copy-start(s32[1,16]{1,0:T(1,128)} %param.13) | copy-start | bytes 196
  20.3 13.0 %copy-start.12 = (bf16[16,2048]{1,0:T(8,128)(2,1)S(1)}, bf16[16,2048]{1,0:T(8,128)(2,1)}, u32[]{:S(2)}) copy-start(bf16[16,2048]{1,0:T(8,128)(2,1)} %get-tuple-element.113) | copy-start | bytes 196612
  20.3 31.9 %copy-start = (bf16[1,3,16,128,128]{4,3,2,1,0:T(8,128)(2,1)S(1)}, bf16[1,3,16,128,128]{4,3,2,1,0:T(8,128)(2,1)}, u32[]{:S(2)}) copy-start(bf16[1,3,16,128,128]{4,3,2,1,0:T(8,128)(2,1)} %param.11) | copy-start | bytes 4718596
  20.4 31.9 %copy-start.3 = (f32[192,256]{1,0:T(8,128)S(1)}, f32[192,256]{1,0:T(8,128)}, u32[]{:S(2)}) copy-start(f32[192,256]{1,0:T(8,128)} %get-tuple-element.107.bias_ref) | copy-start | bytes 589828
  25.6 7.7 %collective-permute-start.6 = (bf16[16,2048]{1,0:T(8,128)(2,1)}, bf16[16,2048]{1,0:T(8,128)(2,1)S(1)}, u32[]{:S(2)}, u32[]{:S(2)}) collective-permute-start(bf16[16,2048]{1,0:T(8,128)(2,1)} %get-tuple-element.114), channel_id=1, source_target_pairs={{0,1},{1,2},{2,3},{3,4},{4,5},{5,6},{6,7},{7,8},{8,9},{9,10},{10,1... | collective-permute-start | bytes 196616 | tf_op jit(solution)/shard_map/ppermute | solution.py:339
  29.5 22.7 %collective-permute-start.5 = (bf16[192,2048]{1,0:T(8,128)(2,1)}, bf16[192,2048]{1,0:T(8,128)(2,1)}, u32[]{:S(2)}, u32[]{:S(2)}) collective-permute-start(bf16[192,2048]{1,0:T(8,128)(2,1)} %get-tuple-element.112), channel_id=1, source_target_pairs={{0,1},{1,2},{2,3},{3,4},{4,5},{5,6},{6,7},{7,8},{8,9},{9,10},{10,1... | collective-permute-start | bytes 2359304 | tf_op jit(solution)/shard_map/ppermute | solution.py:339
  33.4 18.9 %copy-start.2 = (bf16[1,16,128,128]{3,2,1,0:T(8,128)(2,1)S(1)}, bf16[1,16,128,128]{3,2,1,0:T(8,128)(2,1)}, u32[]{:S(2)}) copy-start(bf16[1,16,128,128]{3,2,1,0:T(8,128)(2,1)} %param.12) | copy-start | bytes 1572868
  33.4 18.9 %copy-start.1 = (bf16[1,192,2048]{2,1,0:T(8,128)(2,1)S(1)}, bf16[1,192,2048]{2,1,0:T(8,128)(2,1)}, u32[]{:S(2)}) copy-start(bf16[1,192,2048]{2,1,0:T(8,128)(2,1)} %param.9) | copy-start | bytes 2359300
  33.4 18.9 %copy-start.4 = (bf16[1,2048]{1,0:T(2,128)(2,1)S(1)}, bf16[1,2048]{1,0:T(2,128)(2,1)}, u32[]{:S(2)}) copy-start(bf16[1,2048]{1,0:T(2,128)(2,1)} %gain_ref.7) | copy-start | bytes 12292
  35.5 12.1 %copy-start.11 = (bf16[32,2048]{1,0:T(8,128)(2,1)}, bf16[32,2048]{1,0:T(8,128)(2,1)S(1)}, u32[]{:S(2)}) copy-start(bf16[32,2048]{1,0:T(8,128)(2,1)S(1)} %all-gather.6) | copy-start | bytes 393220 | tf_op jit(solution)/shard_map/while
  35.5 8.4 %collective-permute-start.1 = (bf16[2,16,2048]{2,1,0:T(8,128)(2,1)S(1)}, bf16[2,16,2048]{2,1,0:T(8,128)(2,1)S(1)}, u32[]{:S(2)}, u32[]{:S(2)}) collective-permute-start(bf16[2,16,2048]{2,1,0:T(8,128)(2,1)S(1)} %bitcast.33), channel_id=1, source_target_pairs={{0,64},{32,96},{64,128},{96,160},{128,192},{160,224},{192,256},{22... | collective-permute-start | bytes 393224 | tf_op jit(solution)/shard_map/while/body/ppermute | solution.py:346
  38.3 7.1 %collective-permute-start = (bf16[2,16,2048]{2,1,0:T(8,128)(2,1)S(1)}, bf16[2,16,2048]{2,1,0:T(8,128)(2,1)S(1)}, u32[]{:S(2)}, u32[]{:S(2)}) collective-permute-start(bf16[2,16,2048]{2,1,0:T(8,128)(2,1)S(1)} %bitcast.34), channel_id=1, source_target_pairs={{0,32},{32,64},{64,96},{96,128},{128,160},{160,192},{192,224},{224... | collective-permute-start | bytes 393224 | tf_op jit(solution)/shard_map/while/body/ppermute | solution.py:346
  43.8 3.7 %copy-start.6 = (bf16[2,16,2048]{2,1,0:T(8,128)(2,1)}, bf16[2,16,2048]{2,1,0:T(8,128)(2,1)S(1)}, u32[]{:S(2)}) copy-start(bf16[2,16,2048]{2,1,0:T(8,128)(2,1)S(1)} %collective-permute-done.1) | copy-start | bytes 393220 | tf_op jit(solution)/shard_map/while
  45.4 2.2 %copy-start.8 = (bf16[2,16,2048]{2,1,0:T(8,128)(2,1)}, bf16[2,16,2048]{2,1,0:T(8,128)(2,1)S(1)}, u32[]{:S(2)}) copy-start(bf16[2,16,2048]{2,1,0:T(8,128)(2,1)S(1)} %collective-permute-done) | copy-start | bytes 393220 | tf_op jit(solution)/shard_map/while

commit v4 on v3

--- a/solution.py
+++ b/solution.py
@@ -14,6 +14,7 @@
 PACK = 8
 SLOTS = 5
 KEYS = 256
+PIECES = 4
 PAD = 16
 
 eps = 1e-06
@@ -89,6 +90,34 @@
     ]
     for slot, panel in enumerate(slots):
         packed_ref[slot * count : (slot + 1) * count, :] = panel[:count].astype(f32)
+    packed_ref[SLOTS * count :, :] = jnp.zeros((packed_ref.shape[0] - SLOTS * count, width), f32)
+
+
+def fetch_slots(core, chip_ref, first_ref, second_ref, swapped_ref, slots_ref, sems):
+    other = 1 - core
+    sources = [first_ref.at[core], second_ref.at[core], swapped_ref.at[other, 0], swapped_ref.at[other, 1]]
+    copies = [
+        pltpu.make_async_copy(source, slots_ref.at[1 + slot], sems.at[1 + slot])
+        for slot, source in enumerate(sources)
+    ]
+    for copy in copies:
+        copy.start()
+
+    @pl.when(core == 0)
+    def _():
+        pltpu.make_async_copy(first_ref.at[1], slots_ref.at[0], sems.at[0]).start()
+
+    @pl.when(core == 1)
+    def _():
+        pltpu.make_async_copy(chip_ref.at[0], slots_ref.at[0], sems.at[0]).start()
+
+    return [pltpu.make_async_copy(chip_ref.at[0], slots_ref.at[0], sems.at[0]), *copies]
+
+
+def pack_slots(slots_ref, packed_ref, count):
+    width = packed_ref.shape[1]
+    for slot in range(SLOTS):
+        packed_ref[slot * count : (slot + 1) * count, :] = slots_ref[slot][:count].astype(f32)
     packed_ref[SLOTS * count :, :] = jnp.zeros((packed_ref.shape[0] - SLOTS * count, width), f32)
 
 
@@ -269,30 +298,44 @@
     place_ref, is_first_ref,
     moved_ref, fresh_ref, bias_ref, gain_ref, qkv_ref, o_ref, chip_ref, first_ref, second_ref, swapped_ref,
     out_ref,
-    packed_ref, state_ref, out_buf, sem, out_sems,
+    slots_ref, packed_ref, state_ref, inv_ref, out_buf, slot_sems, sems, out_sems,
 ):
     rows, width = moved_ref.shape
+    step = rows // PIECES
+    blocks = [slice(p * step, (p + 1) * step) for p in range(PIECES)]
+
+    def reads(source):
+        return [
+            pltpu.make_async_copy(source.at[block], state_ref.at[block], sems.at[p])
+            for p, block in enumerate(blocks)
+        ]
+
+    slots = fetch_slots(
+        lax.rem(place_ref[0], 2), chip_ref, first_ref, second_ref, swapped_ref, slots_ref, slot_sems
+    )
 
     @pl.when(is_first_ref[0] == 1)
     def _():
-        copy = pltpu.make_async_copy(fresh_ref, state_ref, sem)
-        copy.start()
+        for copy in reads(fresh_ref):
+            copy.start()
+
+    @pl.when(is_first_ref[0] == 0)
+    def _():
+        for copy in reads(moved_ref):
+            copy.start()
+
+    for copy in slots:
         copy.wait()
-
-    @pl.when(is_first_ref[0] == 0)
-    def _():
-        state_ref[...] = moved_ref[...]
-
-    pack_panels(
-        lax.rem(place_ref[0], 2), chip_ref, first_ref, second_ref, swapped_ref, packed_ref, rows // RATE
-    )
-    squares = None
-    for head in range(HEADS):
-        values = state_ref[:, head * DIM : (head + 1) * DIM].astype(f32)
-        squares = values * values if squares is None else squares + values * values
-    inverse = jnp.broadcast_to(
-        inverse_rms(jnp.sum(squares, axis=-1, keepdims=True), width), (rows, DIM)
-    )
+    pack_slots(slots_ref, packed_ref, rows // RATE)
+    for block, copy in zip(blocks, reads(moved_ref)):
+        copy.wait()
+        squares = None
+        for head in range(HEADS):
+            values = state_ref[block, head * DIM : (head + 1) * DIM].astype(f32)
+            squares = values * values if squares is None else squares + values * values
+        inverse = inverse_rms(jnp.sum(squares, axis=-1, keepdims=True), width)
+        inv_ref[block] = jnp.broadcast_to(inverse, (step, DIM))
+    inverse = inv_ref[...]
     bias = bias_ref[...]
     outs = []
     for group in range(HEADS // PACK):
@@ -318,13 +361,16 @@
     return pl.pallas_call(
         last_kernel,
         out_shape=jax.ShapeDtypeStruct((rows, width), bf16),
-        in_specs=[SMEM, SMEM, VMEM, ANY, *[VMEM] * 8],
+        in_specs=[SMEM, SMEM, ANY, ANY, *[VMEM] * 4, *[ANY] * 4],
         out_specs=ANY,
         scratch_shapes=[
+            pltpu.VMEM((SLOTS, PAD, width), bf16),
             pltpu.VMEM((KEYS - rows, width), f32),
             pltpu.VMEM((rows, width), bf16),
+            pltpu.VMEM((rows, DIM), f32),
             pltpu.VMEM((rows, width), bf16),
-            pltpu.SemaphoreType.DMA,
+            pltpu.SemaphoreType.DMA((SLOTS,)),
+            pltpu.SemaphoreType.DMA((PIECES,)),
             pltpu.SemaphoreType.DMA((HEADS // PACK,)),
         ],
         compiler_params=pltpu.CompilerParams(vmem_limit_bytes=48 << 20),

time: 57.4 us -> 57.4 us (level)
  the two profiles are of different devices: /device:TPU:134 before, /device:TPU:238 now
where the time goes in v4:
time: 57.4 us; the launch traced here: 57 us
  starting transfers between devices  24.2 us (42%)
  Pallas kernels  13.6 us (24%)
  waiting for transfers between devices  10.5 us (18%)
  blocking collectives  8.24 us (14%)
    ppermute x4, starting transfers between devices, by_core(): return lax.ppermute(value, 'seq', pairs)  15.4 us
    ppermute x3, starting transfers between devices, shifted(): lax.ppermute(value, axis, [(source, source + steps) for source in range(f...  8.77 us
    ppermute x3, waiting for transfers between devices, shifted(): lax.ppermute(value, axis, [(source, source + steps) for source in range(f...  7.96 us
    pallas_call x1, Pallas kernels, first_layer(): pl.pallas_call(first_kernel, grid=(HEADS // PACK,), out_shape=(jax.ShapeD...  5.23 us
    pallas_call x1, Pallas kernels, last_layer(): pl.pallas_call(last_kernel, out_shape=jax.ShapeDtypeStruct((rows, width),...  4.74 us
    all_gather x2, blocking collectives, fetch(): chip = lax.all_gather(panel, 'seq', axis=0, axis_index_groups=cores)  4.13 us
    all_gather x2, blocking collectives, fetch(): swapped = lax.all_gather(mine, 'seq', axis=0, axis_index_groups=cores)  4.11 us
    ppermute x4, waiting for transfers between devices, by_core(): return lax.ppermute(value, 'seq', pairs)  2.49 us
  transfers between devices with their start and end apart: 7, of which 4 were waited for; matrix products, arithmetic and copies ran while one was open for 0% of the time, Pallas kernels for 3%

profile of v4, /device:TPU:238, one launch (start us, length us, event | category | flops | bytes accessed | tf_op | source)
XLA Modules:
  0.0 57.0 jit_solution(5020300351593075036)
XLA Ops:
  0.0 2.1 %norm_panel.1 = (bf16[16,2048]{1,0:T(8,128)(2,1)}, f32[192,128]{1,0:T(8,128)}, bf16[1,2176]{1,0:T(2,128)(2,1)}) custom-call(s32[16]{0:T(128)} %bitcast.36, bf16[192,2048]{1,0:T(8,128)(2,1)} %bitcast.24, bf16[1,2048]{1,0:T(2,128)(2,1)} %gain_ref.7), custom_call_target="tpu_custom_call" | custom-call | flops 2000000 | bytes 1000000 | tf_op jit(solution)/shard_map/norm_panel/pallas_call | solution.py:66
  2.1 2.1 %all-gather.2 = bf16[32,2048]{1,0:T(8,128)(2,1)S(1)} all-gather(bf16[16,2048]{1,0:T(8,128)(2,1)} %get-tuple-element.108), channel_id=4, replica_groups={{0,16},{32,48},{64,80},{96,112},{128,144},{160,176},{192,208},{224,240}..., dimensions={0}, use_global_device_ids=true | all-gather | bytes 196608 | tf_op jit(solution)/shard_map/all_gather | solution.py:398
  4.2 0.0 copy-start.10
  4.2 4.3 %collective-permute-start.3 = (bf16[2,16,2048]{2,1,0:T(8,128)(2,1)S(1)}, bf16[2,16,2048]{2,1,0:T(8,128)(2,1)S(1)}, u32[]{:S(2)}, u32[]{:S(2)}) collective-permute-start(bf16[2,16,2048]{2,1,0:T(8,128)(2,1)S(1)} %bitcast.29), channel_id=1, source_target_pairs={{0,64},{32,96},{64,128},{96,160},{128,192},{160,224},{192,256},{22... | collective-permute-start | bytes 393224 | tf_op jit(solution)/shard_map/ppermute | solution.py:392
  8.6 4.0 %collective-permute-start.2 = (bf16[2,16,2048]{2,1,0:T(8,128)(2,1)S(1)}, bf16[2,16,2048]{2,1,0:T(8,128)(2,1)S(1)}, u32[]{:S(2)}, u32[]{:S(2)}) collective-permute-start(bf16[2,16,2048]{2,1,0:T(8,128)(2,1)S(1)} %bitcast.30), channel_id=1, source_target_pairs={{0,32},{32,64},{64,96},{96,128},{128,160},{160,192},{192,224},{224... | collective-permute-start | bytes 393224 | tf_op jit(solution)/shard_map/ppermute | solution.py:392
  12.6 2.0 %collective-permute-start.4 = (bf16[1,2176]{1,0:T(2,128)(2,1)}, bf16[1,2176]{1,0:T(2,128)(2,1)S(1)}, u32[]{:S(2)}, u32[]{:S(2)}) collective-permute-start(bf16[1,2176]{1,0:T(2,128)(2,1)} %get-tuple-element.109), channel_id=1, source_target_pairs={{1,0},{2,1},{3,2},{4,3},{5,4},{6,5},{7,6},{8,7},{9,8},{10,9},{11,1... | collective-permute-start | bytes 13064 | tf_op jit(solution)/shard_map/ppermute | solution.py:385
  14.6 1.5 %entering_panel.1 = (bf16[16,2048]{1,0:T(8,128)(2,1)}, f32[192,256]{1,0:T(8,128)}) custom-call(s32[1]{0:T(128)} %bitcast.2.place_ref, s32[1]{0:T(128)} %bitcast.3.is_first_ref, s32[16]{0:T(128)} %bitcast.37, bf16[192,2048]{1,0:T(8,128)(2,1)} %bitcast.20, bf16[1,2048]{1,0:T(2,128)(2,1)} %gain_ref.7), custom_call_target="tpu_custom_call" | custom-call | flops 2000000 | bytes 1000000 | tf_op jit(solution)/shard_map/entering_panel/pallas_call | solution.py:162
  16.1 0.0 collective-permute-done.3.second_ref
  16.1 0.0 copy-start.5
  16.2 0.0 collective-permute-done.2.first_ref
  16.2 0.0 copy-start.7
  16.2 3.3 %collective-permute-done.4.gain_next_ref = bf16[1,2176]{1,0:T(2,128)(2,1)S(1)} collective-permute-done((bf16[1,2176]{1,0:T(2,128)(2,1)}, bf16[1,2176]{1,0:T(2,128)(2,1)S(1)}, u32[]{:S(2)}, u32[]{:S(2)}) %collective-permute-start.4) | collective-permute-done | bytes 4384 | tf_op jit(solution)/shard_map/ppermute | solution.py:385
  19.6 0.0 copy-start.13
  19.6 2.0 %all-gather.3 = bf16[4,16,2048]{2,1,0:T(8,128)(2,1)S(1)} all-gather(bf16[2,16,2048]{2,1,0:T(8,128)(2,1)S(1)} %pad_maximum_fusion.1), channel_id=5, replica_groups={{0,16},{32,48},{64,80},{96,112},{128,144},{160,176},{192,208},{224,240}..., dimensions={0}, use_global_device_ids=true | all-gather | bytes 393216 | tf_op jit(solution)/shard_map/all_gather | solution.py:409
  21.5 0.0 copy-start.9
  21.5 0.0 copy-done.13
  21.6 0.0 copy-start
  21.6 0.0 copy-start.3
  21.6 5.2 %first_layer.1 = (bf16[192,2048]{1,0:T(8,128)(2,1)}, bf16[16,2048]{1,0:T(8,128)(2,1)}) custom-call(s32[1]{0:T(128)} %bitcast.2.place_ref, bf16[192,2048]{1,0:T(8,128)(2,1)} %bitcast.25, f32[192,128]{1,0:T(8,128)} %get-tuple-element.106.inv_ref, f32[192,256]{1,0:T(8,128)} %get-tuple-element.107.bias_ref, bf16[1,2048]{1,0:T(2,128)(2,1)} %gain_ref.7, ...), custom_call_target="tpu_custom_call" | custom-call | flops 800000000 | bytes 5000000 | tf_op jit(solution)/shard_map/first_layer/pallas_call | solution.py:263
  26.8 0.0 copy-done.10
  26.8 0.0 copy-done.5
  26.8 0.0 copy-done.7
  26.8 0.0 copy-done.9
  26.9 3.8 %collective-permute-start.6 = (bf16[16,2048]{1,0:T(8,128)(2,1)}, bf16[16,2048]{1,0:T(8,128)(2,1)S(1)}, u32[]{:S(2)}, u32[]{:S(2)}) collective-permute-start(bf16[16,2048]{1,0:T(8,128)(2,1)} %get-tuple-element.114), channel_id=1, source_target_pairs={{0,1},{1,2},{2,3},{3,4},{4,5},{5,6},{6,7},{7,8},{8,9},{9,10},{10,1... | collective-permute-start | bytes 196616 | tf_op jit(solution)/shard_map/ppermute | solution.py:385
  30.7 0.0 copy-done.14
  30.7 2.9 %collective-permute-start.5 = (bf16[192,2048]{1,0:T(8,128)(2,1)}, bf16[192,2048]{1,0:T(8,128)(2,1)}, u32[]{:S(2)}, u32[]{:S(2)}) collective-permute-start(bf16[192,2048]{1,0:T(8,128)(2,1)} %get-tuple-element.112), channel_id=1, source_target_pairs={{0,1},{1,2},{2,3},{3,4},{4,5},{5,6},{6,7},{7,8},{8,9},{9,10},{10,1... | collective-permute-start | bytes 2359304 | tf_op jit(solution)/shard_map/ppermute | solution.py:385
  33.7 0.0 collective-permute-done.6
  33.7 0.0 copy-done.12
  33.7 0.0 copy-start.2
  33.7 0.0 copy-start.1
  33.7 0.0 copy-start.4
  33.7 13.9 %while.18 = (s32[]{:T(128)}, bf16[2,16,2048]{2,1,0:T(8,128)(2,1)}, bf16[2,16,2048]{2,1,0:T(8,128)(2,1)}, bf16[2,16,2048]{2,1,0:T(8,128)(2,1)}, bf16[2,2,16,2048]...) while((s32[]{:T(128)}, bf16[2,16,2048]{2,1,0:T(8,128)(2,1)}, ...), condition=%wide.region_1.2_spmd, body=%wide.region_0.1_spmd.sunk | while | flops 65538 | bytes 3735817 | solution.py:431
  33.8 2.0 %all-gather.6 = bf16[32,2048]{1,0:T(8,128)(2,1)S(1)} all-gather(bf16[16,2048]{1,0:T(8,128)(2,1)S(1)} %get-tuple-element.201), channel_id=2, replica_groups={{0,16},{32,48},{64,80},{96,112},{128,144},{160,176},{192,208},{224,240}..., dimensions={0}, use_global_device_ids=true | all-gather | bytes 196608 | tf_op jit(solution)/shard_map/while/body/all_gather | solution.py:398
  35.8 2.5 %collective-permute-start.1 = (bf16[2,16,2048]{2,1,0:T(8,128)(2,1)S(1)}, bf16[2,16,2048]{2,1,0:T(8,128)(2,1)S(1)}, u32[]{:S(2)}, u32[]{:S(2)}) collective-permute-start(bf16[2,16,2048]{2,1,0:T(8,128)(2,1)S(1)} %bitcast.33), channel_id=1, source_target_pairs={{0,64},{32,96},{64,128},{96,160},{128,192},{160,224},{192,256},{22... | collective-permute-start | bytes 393224 | tf_op jit(solution)/shard_map/while/body/ppermute | solution.py:392
  38.3 4.6 %collective-permute-start = (bf16[2,16,2048]{2,1,0:T(8,128)(2,1)S(1)}, bf16[2,16,2048]{2,1,0:T(8,128)(2,1)S(1)}, u32[]{:S(2)}, u32[]{:S(2)}) collective-permute-start(bf16[2,16,2048]{2,1,0:T(8,128)(2,1)S(1)} %bitcast.34), channel_id=1, source_target_pairs={{0,32},{32,64},{64,96},{96,128},{128,160},{160,192},{192,224},{224... | collective-permute-start | bytes 393224 | tf_op jit(solution)/shard_map/while/body/ppermute | solution.py:392
  42.9 1.2 %collective-permute-done.1 = bf16[2,16,2048]{2,1,0:T(8,128)(2,1)S(1)} collective-permute-done((bf16[2,16,2048]{2,1,0:T(8,128)(2,1)S(1)}, bf16[2,16,2048]{2,1,0:T(8,128)(2,1)S(1)}, u32[]{:S(2)}, u32[]{:S(2)}) %collective-permute-start.1) | collective-permute-done | bytes 131104 | tf_op jit(solution)/shard_map/while/body/ppermute | solution.py:392
  44.2 1.3 %collective-permute-done = bf16[2,16,2048]{2,1,0:T(8,128)(2,1)S(1)} collective-permute-done((bf16[2,16,2048]{2,1,0:T(8,128)(2,1)S(1)}, bf16[2,16,2048]{2,1,0:T(8,128)(2,1)S(1)}, u32[]{:S(2)}, u32[]{:S(2)}) %collective-permute-start) | collective-permute-done | bytes 131104 | tf_op jit(solution)/shard_map/while/body/ppermute | solution.py:392
  45.5 2.1 %all-gather.7 = bf16[4,16,2048]{2,1,0:T(8,128)(2,1)} all-gather(bf16[2,16,2048]{2,1,0:T(8,128)(2,1)S(1)} %pad_maximum_fusion.3), channel_id=3, replica_groups={{0,16},{32,48},{64,80},{96,112},{128,144},{160,176},{192,208},{224,240}..., dimensions={0}, use_global_device_ids=true | all-gather | bytes 393216 | tf_op jit(solution)/shard_map/while/body/all_gather | solution.py:409
  47.6 0.0 copy-done.11
  47.6 0.0 copy-done.6
  47.6 0.0 copy-done.8
  47.6 4.6 %collective-permute-done.5.moved_ref = bf16[192,2048]{1,0:T(8,128)(2,1)} collective-permute-done((bf16[192,2048]{1,0:T(8,128)(2,1)}, bf16[192,2048]{1,0:T(8,128)(2,1)}, u32[]{:S(2)}, u32[]{:S(2)}) %collective-permute-start.5) | collective-permute-done | bytes 786464 | tf_op jit(solution)/shard_map/ppermute | solution.py:385
  52.3 0.0 copy-done
  52.3 0.0 copy-done.3
  52.3 0.0 copy-done.2
  52.3 0.0 copy-done.1
  52.3 0.0 copy-done.4
  52.3 4.7 %last_layer.1 = bf16[192,2048]{1,0:T(8,128)(2,1)} custom-call(s32[1]{0:T(128)} %bitcast.2.place_ref, s32[1]{0:T(128)} %bitcast.3.is_first_ref, bf16[192,2048]{1,0:T(8,128)(2,1)} %collective-permute-done.5.moved_ref, bf16[192,2048]{1,0:T(8,128)(2,1)S(1)} %bitcast.21, f32[192,256]{1,0:T(8,128)S(1)} %copy-done.3, bf16[1,2048]{1,0:T(2,128)(2,1)S(1)} %copy-done.4, ...), custom_call_target="tpu_custom_call" | custom-call | flops 800000000 | bytes 5000000 | tf_op jit(solution)/shard_map/last_layer/pallas_call | solution.py:361
  (12 shorter events, 0.1 us)
Async XLA Ops:
  4.2 22.6 %copy-start.10 = (bf16[32,2048]{1,0:T(8,128)(2,1)}, bf16[32,2048]{1,0:T(8,128)(2,1)S(1)}, u32[]{:S(2)}) copy-start(bf16[32,2048]{1,0:T(8,128)(2,1)S(1)} %all-gather.2) | copy-start | bytes 393220
  4.2 11.9 %collective-permute-start.3 = (bf16[2,16,2048]{2,1,0:T(8,128)(2,1)S(1)}, bf16[2,16,2048]{2,1,0:T(8,128)(2,1)S(1)}, u32[]{:S(2)}, u32[]{:S(2)}) collective-permute-start(bf16[2,16,2048]{2,1,0:T(8,128)(2,1)S(1)} %bitcast.29), channel_id=1, source_target_pairs={{0,64},{32,96},{64,128},{96,160},{128,192},{160,224},{192,256},{22... | collective-permute-start | bytes 393224 | tf_op jit(solution)/shard_map/ppermute | solution.py:392
  8.6 7.6 %collective-permute-start.2 = (bf16[2,16,2048]{2,1,0:T(8,128)(2,1)S(1)}, bf16[2,16,2048]{2,1,0:T(8,128)(2,1)S(1)}, u32[]{:S(2)}, u32[]{:S(2)}) collective-permute-start(bf16[2,16,2048]{2,1,0:T(8,128)(2,1)S(1)} %bitcast.30), channel_id=1, source_target_pairs={{0,32},{32,64},{64,96},{96,128},{128,160},{160,192},{192,224},{224... | collective-permute-start | bytes 393224 | tf_op jit(solution)/shard_map/ppermute | solution.py:392
  12.6 7.0 %collective-permute-start.4 = (bf16[1,2176]{1,0:T(2,128)(2,1)}, bf16[1,2176]{1,0:T(2,128)(2,1)S(1)}, u32[]{:S(2)}, u32[]{:S(2)}) collective-permute-start(bf16[1,2176]{1,0:T(2,128)(2,1)} %get-tuple-element.109), channel_id=1, source_target_pairs={{1,0},{2,1},{3,2},{4,3},{5,4},{6,5},{7,6},{8,7},{9,8},{10,9},{11,1... | collective-permute-start | bytes 13064 | tf_op jit(solution)/shard_map/ppermute | solution.py:385
  16.1 10.7 %copy-start.5 = (bf16[2,16,2048]{2,1,0:T(8,128)(2,1)}, bf16[2,16,2048]{2,1,0:T(8,128)(2,1)S(1)}, u32[]{:S(2)}) copy-start(bf16[2,16,2048]{2,1,0:T(8,128)(2,1)S(1)} %collective-permute-done.3.second_ref) | copy-start | bytes 393220
  16.2 10.7 %copy-start.7 = (bf16[2,16,2048]{2,1,0:T(8,128)(2,1)}, bf16[2,16,2048]{2,1,0:T(8,128)(2,1)S(1)}, u32[]{:S(2)}) copy-start(bf16[2,16,2048]{2,1,0:T(8,128)(2,1)S(1)} %collective-permute-done.2.first_ref) | copy-start | bytes 393220
  19.6 2.0 %copy-start.13 = (bf16[1,2176]{1,0:T(2,128)(2,1)}, bf16[1,2176]{1,0:T(2,128)(2,1)S(1)}, u32[]{:S(2)}) copy-start(bf16[1,2176]{1,0:T(2,128)(2,1)S(1)} %collective-permute-done.4.gain_next_ref) | copy-start | bytes 13060
  21.5 5.3 %copy-start.9 = (bf16[4,16,2048]{2,1,0:T(8,128)(2,1)}, bf16[4,16,2048]{2,1,0:T(8,128)(2,1)S(1)}, u32[]{:S(2)}) copy-start(bf16[4,16,2048]{2,1,0:T(8,128)(2,1)S(1)} %all-gather.3) | copy-start | bytes 786436
  21.5 9.1 %copy-start.14 = (s32[1,16]{1,0:T(1,128)S(1)}, s32[1,16]{1,0:T(1,128)}, u32[]{:S(2)}) copy-start(s32[1,16]{1,0:T(1,128)} %param.13) | copy-start | bytes 196
  21.5 12.1 %copy-start.12 = (bf16[16,2048]{1,0:T(8,128)(2,1)S(1)}, bf16[16,2048]{1,0:T(8,128)(2,1)}, u32[]{:S(2)}) copy-start(bf16[16,2048]{1,0:T(8,128)(2,1)} %get-tuple-element.113) | copy-start | bytes 196612
  21.6 30.7 %copy-start = (bf16[1,3,16,128,128]{4,3,2,1,0:T(8,128)(2,1)S(1)}, bf16[1,3,16,128,128]{4,3,2,1,0:T(8,128)(2,1)}, u32[]{:S(2)}) copy-start(bf16[1,3,16,128,128]{4,3,2,1,0:T(8,128)(2,1)} %param.11) | copy-start | bytes 4718596
  21.6 30.7 %copy-start.3 = (f32[192,256]{1,0:T(8,128)S(1)}, f32[192,256]{1,0:T(8,128)}, u32[]{:S(2)}) copy-start(f32[192,256]{1,0:T(8,128)} %get-tuple-element.107.bias_ref) | copy-start | bytes 589828
  26.9 6.8 %collective-permute-start.6 = (bf16[16,2048]{1,0:T(8,128)(2,1)}, bf16[16,2048]{1,0:T(8,128)(2,1)S(1)}, u32[]{:S(2)}, u32[]{:S(2)}) collective-permute-start(bf16[16,2048]{1,0:T(8,128)(2,1)} %get-tuple-element.114), channel_id=1, source_target_pairs={{0,1},{1,2},{2,3},{3,4},{4,5},{5,6},{6,7},{7,8},{8,9},{9,10},{10,1... | collective-permute-start | bytes 196616 | tf_op jit(solution)/shard_map/ppermute | solution.py:385
  30.7 21.5 %collective-permute-start.5 = (bf16[192,2048]{1,0:T(8,128)(2,1)}, bf16[192,2048]{1,0:T(8,128)(2,1)}, u32[]{:S(2)}, u32[]{:S(2)}) collective-permute-start(bf16[192,2048]{1,0:T(8,128)(2,1)} %get-tuple-element.112), channel_id=1, source_target_pairs={{0,1},{1,2},{2,3},{3,4},{4,5},{5,6},{6,7},{7,8},{8,9},{9,10},{10,1... | collective-permute-start | bytes 2359304 | tf_op jit(solution)/shard_map/ppermute | solution.py:385
  33.7 18.6 %copy-start.2 = (bf16[1,16,128,128]{3,2,1,0:T(8,128)(2,1)S(1)}, bf16[1,16,128,128]{3,2,1,0:T(8,128)(2,1)}, u32[]{:S(2)}) copy-start(bf16[1,16,128,128]{3,2,1,0:T(8,128)(2,1)} %param.12) | copy-start | bytes 1572868
  33.7 18.6 %copy-start.1 = (bf16[1,192,2048]{2,1,0:T(8,128)(2,1)S(1)}, bf16[1,192,2048]{2,1,0:T(8,128)(2,1)}, u32[]{:S(2)}) copy-start(bf16[1,192,2048]{2,1,0:T(8,128)(2,1)} %param.9) | copy-start | bytes 2359300
  33.7 18.5 %copy-start.4 = (bf16[1,2048]{1,0:T(2,128)(2,1)S(1)}, bf16[1,2048]{1,0:T(2,128)(2,1)}, u32[]{:S(2)}) copy-start(bf16[1,2048]{1,0:T(2,128)(2,1)} %gain_ref.7) | copy-start | bytes 12292
  35.8 11.8 %copy-start.11 = (bf16[32,2048]{1,0:T(8,128)(2,1)}, bf16[32,2048]{1,0:T(8,128)(2,1)S(1)}, u32[]{:S(2)}) copy-start(bf16[32,2048]{1,0:T(8,128)(2,1)S(1)} %all-gather.6) | copy-start | bytes 393220 | tf_op jit(solution)/shard_map/while
  35.8 8.4 %collective-permute-start.1 = (bf16[2,16,2048]{2,1,0:T(8,128)(2,1)S(1)}, bf16[2,16,2048]{2,1,0:T(8,128)(2,1)S(1)}, u32[]{:S(2)}, u32[]{:S(2)}) collective-permute-start(bf16[2,16,2048]{2,1,0:T(8,128)(2,1)S(1)} %bitcast.33), channel_id=1, source_target_pairs={{0,64},{32,96},{64,128},{96,160},{128,192},{160,224},{192,256},{22... | collective-permute-start | bytes 393224 | tf_op jit(solution)/shard_map/while/body/ppermute | solution.py:392
  38.3 7.1 %collective-permute-start = (bf16[2,16,2048]{2,1,0:T(8,128)(2,1)S(1)}, bf16[2,16,2048]{2,1,0:T(8,128)(2,1)S(1)}, u32[]{:S(2)}, u32[]{:S(2)}) collective-permute-start(bf16[2,16,2048]{2,1,0:T(8,128)(2,1)S(1)} %bitcast.34), channel_id=1, source_target_pairs={{0,32},{32,64},{64,96},{96,128},{128,160},{160,192},{192,224},{224... | collective-permute-start | bytes 393224 | tf_op jit(solution)/shard_map/while/body/ppermute | solution.py:392
  44.2 3.4 %copy-start.6 = (bf16[2,16,2048]{2,1,0:T(8,128)(2,1)}, bf16[2,16,2048]{2,1,0:T(8,128)(2,1)S(1)}, u32[]{:S(2)}) copy-start(bf16[2,16,2048]{2,1,0:T(8,128)(2,1)S(1)} %collective-permute-done.1) | copy-start | bytes 393220 | tf_op jit(solution)/shard_map/while
  45.4 2.2 %copy-start.8 = (bf16[2,16,2048]{2,1,0:T(8,128)(2,1)}, bf16[2,16,2048]{2,1,0:T(8,128)(2,1)S(1)}, u32[]{:S(2)}) copy-start(bf16[2,16,2048]{2,1,0:T(8,128)(2,1)S(1)} %collective-permute-done) | copy-start | bytes 393220 | tf_op jit(solution)/shard_map/while

commit v5 on v4

--- a/solution.py
+++ b/solution.py
@@ -132,7 +132,7 @@
         distance = jnp.where(core == 0, even[slot], odd[slot])
         start = jnp.where(place >= distance, rows + slot * count, keys)
         allowed = allowed | ((col >= start) & (col < rows + (slot + 1) * count))
-    bias_ref[...] = jnp.where(allowed, 0.0, neg_big).astype(f32)
+    bias_ref[...] = jnp.where(allowed, 0.0, neg_big).astype(bf16)
 
 
 def entering_kernel(place_ref, is_first_ref, offsets_ref, fresh_ref, gain_ref, panel_ref, bias_ref, state_ref, wide_ref, inv_ref, sem):
@@ -163,7 +163,7 @@
         entering_kernel,
         out_shape=(
             jax.ShapeDtypeStruct((PAD, width), bf16),
-            jax.ShapeDtypeStruct((rows, KEYS), f32),
+            jax.ShapeDtypeStruct((rows, KEYS), bf16),
         ),
         in_specs=[SMEM, SMEM, SMEM, ANY, VMEM],
         out_specs=(VMEM, VMEM),
@@ -222,7 +222,7 @@
             lax.rem(place_ref[0], 2), chip_ref, first_ref, second_ref, swapped_ref, packed_ref, count
         )
 
-    inverse, bias = inv_ref[...], bias_ref[...]
+    inverse, bias = inv_ref[...], bias_ref[...].astype(f32)
     squares = jnp.zeros((rows, DIM), f32)
     local_cols = [slice(local * DIM, (local + 1) * DIM) for local in range(PACK)]
     there = [pl.ds(pl.multiple_of((step * PACK + local) * DIM, DIM), DIM) for local in range(PACK)]
@@ -336,7 +336,7 @@
         inverse = inverse_rms(jnp.sum(squares, axis=-1, keepdims=True), width)
         inv_ref[block] = jnp.broadcast_to(inverse, (step, DIM))
     inverse = inv_ref[...]
-    bias = bias_ref[...]
+    bias = bias_ref[...].astype(f32)
     outs = []
     for group in range(HEADS // PACK):
         heads = range(group * PACK, (group + 1) * PACK)

time: 57.4 us -> 57.4 us (level)
  the two profiles are of different devices: /device:TPU:238 before, /device:TPU:110 now
where the time goes in v5:
time: 57.4 us; the launch traced here: 57 us
  starting transfers between devices  25.1 us (44%)
  Pallas kernels  13.5 us (24%)
  waiting for transfers between devices  9.58 us (17%)
  blocking collectives  8.24 us (14%)
    ppermute x4, starting transfers between devices, by_core(): return lax.ppermute(value, 'seq', pairs)  15.4 us
    ppermute x3, starting transfers between devices, shifted(): lax.ppermute(value, axis, [(source, source + steps) for source in range(f...  9.67 us
    ppermute x3, waiting for transfers between devices, shifted(): lax.ppermute(value, axis, [(source, source + steps) for source in range(f...  7.09 us
    pallas_call x1, Pallas kernels, first_layer(): pl.pallas_call(first_kernel, grid=(HEADS // PACK,), out_shape=(jax.ShapeD...  5.19 us
    pallas_call x1, Pallas kernels, last_layer(): pl.pallas_call(last_kernel, out_shape=jax.ShapeDtypeStruct((rows, width),...  4.73 us
    all_gather x2, blocking collectives, fetch(): chip = lax.all_gather(panel, 'seq', axis=0, axis_index_groups=cores)  4.13 us
    all_gather x2, blocking collectives, fetch(): swapped = lax.all_gather(mine, 'seq', axis=0, axis_index_groups=cores)  4.11 us
    ppermute x4, waiting for transfers between devices, by_core(): return lax.ppermute(value, 'seq', pairs)  2.49 us
  transfers between devices with their start and end apart: 7, of which 4 were waited for; matrix products, arithmetic and copies ran while one was open for 0% of the time, Pallas kernels for 3%

profile of v5, /device:TPU:110, one launch (start us, length us, event | category | flops | bytes accessed | tf_op | source)
XLA Modules:
  0.0 57.0 jit_solution(16510598221430347654)
XLA Ops:
  0.0 2.1 %norm_panel.1 = (bf16[16,2048]{1,0:T(8,128)(2,1)}, f32[192,128]{1,0:T(8,128)}, bf16[1,2176]{1,0:T(2,128)(2,1)}) custom-call(s32[16]{0:T(128)} %bitcast.36, bf16[192,2048]{1,0:T(8,128)(2,1)} %bitcast.24, bf16[1,2048]{1,0:T(2,128)(2,1)} %gain_ref.7), custom_call_target="tpu_custom_call" | custom-call | flops 2000000 | bytes 1000000 | tf_op jit(solution)/shard_map/norm_panel/pallas_call | solution.py:66
  2.1 2.1 %all-gather.2 = bf16[32,2048]{1,0:T(8,128)(2,1)S(1)} all-gather(bf16[16,2048]{1,0:T(8,128)(2,1)} %get-tuple-element.108), channel_id=4, replica_groups={{0,16},{32,48},{64,80},{96,112},{128,144},{160,176},{192,208},{224,240}..., dimensions={0}, use_global_device_ids=true | all-gather | bytes 196608 | tf_op jit(solution)/shard_map/all_gather | solution.py:398
  4.2 0.0 copy-start.10
  4.2 4.3 %collective-permute-start.3 = (bf16[2,16,2048]{2,1,0:T(8,128)(2,1)S(1)}, bf16[2,16,2048]{2,1,0:T(8,128)(2,1)S(1)}, u32[]{:S(2)}, u32[]{:S(2)}) collective-permute-start(bf16[2,16,2048]{2,1,0:T(8,128)(2,1)S(1)} %bitcast.29), channel_id=1, source_target_pairs={{0,64},{32,96},{64,128},{96,160},{128,192},{160,224},{192,256},{22... | collective-permute-start | bytes 393224 | tf_op jit(solution)/shard_map/ppermute | solution.py:392
  8.6 4.0 %collective-permute-start.2 = (bf16[2,16,2048]{2,1,0:T(8,128)(2,1)S(1)}, bf16[2,16,2048]{2,1,0:T(8,128)(2,1)S(1)}, u32[]{:S(2)}, u32[]{:S(2)}) collective-permute-start(bf16[2,16,2048]{2,1,0:T(8,128)(2,1)S(1)} %bitcast.30), channel_id=1, source_target_pairs={{0,32},{32,64},{64,96},{96,128},{128,160},{160,192},{192,224},{224... | collective-permute-start | bytes 393224 | tf_op jit(solution)/shard_map/ppermute | solution.py:392
  12.6 2.0 %collective-permute-start.4 = (bf16[1,2176]{1,0:T(2,128)(2,1)}, bf16[1,2176]{1,0:T(2,128)(2,1)S(1)}, u32[]{:S(2)}, u32[]{:S(2)}) collective-permute-start(bf16[1,2176]{1,0:T(2,128)(2,1)} %get-tuple-element.109), channel_id=1, source_target_pairs={{1,0},{2,1},{3,2},{4,3},{5,4},{6,5},{7,6},{8,7},{9,8},{10,9},{11,1... | collective-permute-start | bytes 13064 | tf_op jit(solution)/shard_map/ppermute | solution.py:385
  14.6 1.5 %entering_panel.1 = (bf16[16,2048]{1,0:T(8,128)(2,1)}, bf16[192,256]{1,0:T(8,128)(2,1)}) custom-call(s32[1]{0:T(128)} %bitcast.2.place_ref, s32[1]{0:T(128)} %bitcast.3.is_first_ref, s32[16]{0:T(128)} %bitcast.37, bf16[192,2048]{1,0:T(8,128)(2,1)} %bitcast.20, bf16[1,2048]{1,0:T(2,128)(2,1)} %gain_ref.7), custom_call_target="tpu_custom_call" | custom-call | flops 2000000 | bytes 1000000 | tf_op jit(solution)/shard_map/entering_panel/pallas_call | solution.py:162
  16.1 0.0 collective-permute-done.3.second_ref
  16.1 0.0 copy-start.5
  16.1 0.0 collective-permute-done.2.first_ref
  16.2 0.0 copy-start.7
  16.2 3.3 %collective-permute-done.4.gain_next_ref = bf16[1,2176]{1,0:T(2,128)(2,1)S(1)} collective-permute-done((bf16[1,2176]{1,0:T(2,128)(2,1)}, bf16[1,2176]{1,0:T(2,128)(2,1)S(1)}, u32[]{:S(2)}, u32[]{:S(2)}) %collective-permute-start.4) | collective-permute-done | bytes 4384 | tf_op jit(solution)/shard_map/ppermute | solution.py:385
  19.6 0.0 copy-start.13
  19.6 2.0 %all-gather.3 = bf16[4,16,2048]{2,1,0:T(8,128)(2,1)S(1)} all-gather(bf16[2,16,2048]{2,1,0:T(8,128)(2,1)S(1)} %pad_maximum_fusion.1), channel_id=5, replica_groups={{0,16},{32,48},{64,80},{96,112},{128,144},{160,176},{192,208},{224,240}..., dimensions={0}, use_global_device_ids=true | all-gather | bytes 393216 | tf_op jit(solution)/shard_map/all_gather | solution.py:409
  21.5 0.0 copy-start.9
  21.5 0.0 copy-done.13
  21.6 0.0 copy-start
  21.6 0.0 copy-start.3
  21.6 5.2 %first_layer.1 = (bf16[192,2048]{1,0:T(8,128)(2,1)}, bf16[16,2048]{1,0:T(8,128)(2,1)}) custom-call(s32[1]{0:T(128)} %bitcast.2.place_ref, bf16[192,2048]{1,0:T(8,128)(2,1)} %bitcast.25, f32[192,128]{1,0:T(8,128)} %get-tuple-element.106.inv_ref, bf16[192,256]{1,0:T(8,128)(2,1)} %get-tuple-element.107.bias_ref, bf16[1,2048]{1,0:T(2,128)(2,1)} %gain_ref.7, ...), custom_call_target="tpu_custom_call" | custom-call | flops 800000000 | bytes 5000000 | tf_op jit(solution)/shard_map/first_layer/pallas_call | solution.py:263
  26.8 0.0 copy-done.10
  26.8 0.0 copy-done.5
  26.8 0.0 copy-done.7
  26.8 0.0 copy-done.9
  26.8 3.8 %collective-permute-start.6 = (bf16[16,2048]{1,0:T(8,128)(2,1)}, bf16[16,2048]{1,0:T(8,128)(2,1)S(1)}, u32[]{:S(2)}, u32[]{:S(2)}) collective-permute-start(bf16[16,2048]{1,0:T(8,128)(2,1)} %get-tuple-element.114), channel_id=1, source_target_pairs={{0,1},{1,2},{2,3},{3,4},{4,5},{5,6},{6,7},{7,8},{8,9},{9,10},{10,1... | collective-permute-start | bytes 196616 | tf_op jit(solution)/shard_map/ppermute | solution.py:385
  30.7 0.0 copy-done.14
  30.7 3.8 %collective-permute-start.5 = (bf16[192,2048]{1,0:T(8,128)(2,1)}, bf16[192,2048]{1,0:T(8,128)(2,1)}, u32[]{:S(2)}, u32[]{:S(2)}) collective-permute-start(bf16[192,2048]{1,0:T(8,128)(2,1)} %get-tuple-element.112), channel_id=1, source_target_pairs={{0,1},{1,2},{2,3},{3,4},{4,5},{5,6},{6,7},{7,8},{8,9},{9,10},{10,1... | collective-permute-start | bytes 2359304 | tf_op jit(solution)/shard_map/ppermute | solution.py:385
  34.5 0.0 collective-permute-done.6
  34.5 0.0 copy-done.12
  34.6 0.0 copy-start.2
  34.6 0.0 copy-start.1
  34.6 0.0 copy-start.4
  34.6 13.9 %while.18 = (s32[]{:T(128)}, bf16[2,16,2048]{2,1,0:T(8,128)(2,1)}, bf16[2,16,2048]{2,1,0:T(8,128)(2,1)}, bf16[2,16,2048]{2,1,0:T(8,128)(2,1)}, bf16[2,2,16,2048]...) while((s32[]{:T(128)}, bf16[2,16,2048]{2,1,0:T(8,128)(2,1)}, ...), condition=%wide.region_1.2_spmd, body=%wide.region_0.1_spmd.sunk | while | flops 65538 | bytes 3735817 | solution.py:431
  34.6 2.0 %all-gather.6 = bf16[32,2048]{1,0:T(8,128)(2,1)S(1)} all-gather(bf16[16,2048]{1,0:T(8,128)(2,1)S(1)} %get-tuple-element.201), channel_id=2, replica_groups={{0,16},{32,48},{64,80},{96,112},{128,144},{160,176},{192,208},{224,240}..., dimensions={0}, use_global_device_ids=true | all-gather | bytes 196608 | tf_op jit(solution)/shard_map/while/body/all_gather | solution.py:398
  36.7 2.5 %collective-permute-start.1 = (bf16[2,16,2048]{2,1,0:T(8,128)(2,1)S(1)}, bf16[2,16,2048]{2,1,0:T(8,128)(2,1)S(1)}, u32[]{:S(2)}, u32[]{:S(2)}) collective-permute-start(bf16[2,16,2048]{2,1,0:T(8,128)(2,1)S(1)} %bitcast.33), channel_id=1, source_target_pairs={{0,64},{32,96},{64,128},{96,160},{128,192},{160,224},{192,256},{22... | collective-permute-start | bytes 393224 | tf_op jit(solution)/shard_map/while/body/ppermute | solution.py:392
  39.2 4.6 %collective-permute-start = (bf16[2,16,2048]{2,1,0:T(8,128)(2,1)S(1)}, bf16[2,16,2048]{2,1,0:T(8,128)(2,1)S(1)}, u32[]{:S(2)}, u32[]{:S(2)}) collective-permute-start(bf16[2,16,2048]{2,1,0:T(8,128)(2,1)S(1)} %bitcast.34), channel_id=1, source_target_pairs={{0,32},{32,64},{64,96},{96,128},{128,160},{160,192},{192,224},{224... | collective-permute-start | bytes 393224 | tf_op jit(solution)/shard_map/while/body/ppermute | solution.py:392
  43.8 1.2 %collective-permute-done.1 = bf16[2,16,2048]{2,1,0:T(8,128)(2,1)S(1)} collective-permute-done((bf16[2,16,2048]{2,1,0:T(8,128)(2,1)S(1)}, bf16[2,16,2048]{2,1,0:T(8,128)(2,1)S(1)}, u32[]{:S(2)}, u32[]{:S(2)}) %collective-permute-start.1) | collective-permute-done | bytes 131104 | tf_op jit(solution)/shard_map/while/body/ppermute | solution.py:392
  45.0 1.3 %collective-permute-done = bf16[2,16,2048]{2,1,0:T(8,128)(2,1)S(1)} collective-permute-done((bf16[2,16,2048]{2,1,0:T(8,128)(2,1)S(1)}, bf16[2,16,2048]{2,1,0:T(8,128)(2,1)S(1)}, u32[]{:S(2)}, u32[]{:S(2)}) %collective-permute-start) | collective-permute-done | bytes 131104 | tf_op jit(solution)/shard_map/while/body/ppermute | solution.py:392
  46.3 2.1 %all-gather.7 = bf16[4,16,2048]{2,1,0:T(8,128)(2,1)} all-gather(bf16[2,16,2048]{2,1,0:T(8,128)(2,1)S(1)} %pad_maximum_fusion.3), channel_id=3, replica_groups={{0,16},{32,48},{64,80},{96,112},{128,144},{160,176},{192,208},{224,240}..., dimensions={0}, use_global_device_ids=true | all-gather | bytes 393216 | tf_op jit(solution)/shard_map/while/body/all_gather | solution.py:409
  48.5 0.0 copy-done.11
  48.5 0.0 copy-done.6
  48.5 0.0 copy-done.8
  48.5 3.7 %collective-permute-done.5.moved_ref = bf16[192,2048]{1,0:T(8,128)(2,1)} collective-permute-done((bf16[192,2048]{1,0:T(8,128)(2,1)}, bf16[192,2048]{1,0:T(8,128)(2,1)}, u32[]{:S(2)}, u32[]{:S(2)}) %collective-permute-start.5) | collective-permute-done | bytes 786464 | tf_op jit(solution)/shard_map/ppermute | solution.py:385
  52.2 0.0 copy-done
  52.2 0.0 copy-done.3
  52.2 0.0 copy-done.2
  52.2 0.0 copy-done.1
  52.2 0.0 copy-done.4
  52.3 4.7 %last_layer.1 = bf16[192,2048]{1,0:T(8,128)(2,1)} custom-call(s32[1]{0:T(128)} %bitcast.2.place_ref, s32[1]{0:T(128)} %bitcast.3.is_first_ref, bf16[192,2048]{1,0:T(8,128)(2,1)} %collective-permute-done.5.moved_ref, bf16[192,2048]{1,0:T(8,128)(2,1)S(1)} %bitcast.21, bf16[192,256]{1,0:T(8,128)(2,1)S(1)} %copy-done.3, bf16[1,2048]{1,0:T(2,128)(2,1)S(1)} %copy-done.4, ...), custom_call_target="tpu_custom_call" | custom-call | flops 800000000 | bytes 5000000 | tf_op jit(solution)/shard_map/last_layer/pallas_call | solution.py:361
  (12 shorter events, 0.1 us)
Async XLA Ops:
  4.2 22.5 %copy-start.10 = (bf16[32,2048]{1,0:T(8,128)(2,1)}, bf16[32,2048]{1,0:T(8,128)(2,1)S(1)}, u32[]{:S(2)}) copy-start(bf16[32,2048]{1,0:T(8,128)(2,1)S(1)} %all-gather.2) | copy-start | bytes 393220
  4.2 11.9 %collective-permute-start.3 = (bf16[2,16,2048]{2,1,0:T(8,128)(2,1)S(1)}, bf16[2,16,2048]{2,1,0:T(8,128)(2,1)S(1)}, u32[]{:S(2)}, u32[]{:S(2)}) collective-permute-start(bf16[2,16,2048]{2,1,0:T(8,128)(2,1)S(1)} %bitcast.29), channel_id=1, source_target_pairs={{0,64},{32,96},{64,128},{96,160},{128,192},{160,224},{192,256},{22... | collective-permute-start | bytes 393224 | tf_op jit(solution)/shard_map/ppermute | solution.py:392
  8.6 7.6 %collective-permute-start.2 = (bf16[2,16,2048]{2,1,0:T(8,128)(2,1)S(1)}, bf16[2,16,2048]{2,1,0:T(8,128)(2,1)S(1)}, u32[]{:S(2)}, u32[]{:S(2)}) collective-permute-start(bf16[2,16,2048]{2,1,0:T(8,128)(2,1)S(1)} %bitcast.30), channel_id=1, source_target_pairs={{0,32},{32,64},{64,96},{96,128},{128,160},{160,192},{192,224},{224... | collective-permute-start | bytes 393224 | tf_op jit(solution)/shard_map/ppermute | solution.py:392
  12.6 7.0 %collective-permute-start.4 = (bf16[1,2176]{1,0:T(2,128)(2,1)}, bf16[1,2176]{1,0:T(2,128)(2,1)S(1)}, u32[]{:S(2)}, u32[]{:S(2)}) collective-permute-start(bf16[1,2176]{1,0:T(2,128)(2,1)} %get-tuple-element.109), channel_id=1, source_target_pairs={{1,0},{2,1},{3,2},{4,3},{5,4},{6,5},{7,6},{8,7},{9,8},{10,9},{11,1... | collective-permute-start | bytes 13064 | tf_op jit(solution)/shard_map/ppermute | solution.py:385
  16.1 10.7 %copy-start.5 = (bf16[2,16,2048]{2,1,0:T(8,128)(2,1)}, bf16[2,16,2048]{2,1,0:T(8,128)(2,1)S(1)}, u32[]{:S(2)}) copy-start(bf16[2,16,2048]{2,1,0:T(8,128)(2,1)S(1)} %collective-permute-done.3.second_ref) | copy-start | bytes 393220
  16.2 10.6 %copy-start.7 = (bf16[2,16,2048]{2,1,0:T(8,128)(2,1)}, bf16[2,16,2048]{2,1,0:T(8,128)(2,1)S(1)}, u32[]{:S(2)}) copy-start(bf16[2,16,2048]{2,1,0:T(8,128)(2,1)S(1)} %collective-permute-done.2.first_ref) | copy-start | bytes 393220
  19.6 2.0 %copy-start.13 = (bf16[1,2176]{1,0:T(2,128)(2,1)}, bf16[1,2176]{1,0:T(2,128)(2,1)S(1)}, u32[]{:S(2)}) copy-start(bf16[1,2176]{1,0:T(2,128)(2,1)S(1)} %collective-permute-done.4.gain_next_ref) | copy-start | bytes 13060
  21.5 5.3 %copy-start.9 = (bf16[4,16,2048]{2,1,0:T(8,128)(2,1)}, bf16[4,16,2048]{2,1,0:T(8,128)(2,1)S(1)}, u32[]{:S(2)}) copy-start(bf16[4,16,2048]{2,1,0:T(8,128)(2,1)S(1)} %all-gather.3) | copy-start | bytes 786436
  21.5 9.1 %copy-start.14 = (s32[1,16]{1,0:T(1,128)S(1)}, s32[1,16]{1,0:T(1,128)}, u32[]{:S(2)}) copy-start(s32[1,16]{1,0:T(1,128)} %param.13) | copy-start | bytes 196
  21.5 13.0 %copy-start.12 = (bf16[16,2048]{1,0:T(8,128)(2,1)S(1)}, bf16[16,2048]{1,0:T(8,128)(2,1)}, u32[]{:S(2)}) copy-start(bf16[16,2048]{1,0:T(8,128)(2,1)} %get-tuple-element.113) | copy-start | bytes 196612
  21.6 30.7 %copy-start = (bf16[1,3,16,128,128]{4,3,2,1,0:T(8,128)(2,1)S(1)}, bf16[1,3,16,128,128]{4,3,2,1,0:T(8,128)(2,1)}, u32[]{:S(2)}) copy-start(bf16[1,3,16,128,128]{4,3,2,1,0:T(8,128)(2,1)} %param.11) | copy-start | bytes 4718596
  21.6 30.7 %copy-start.3 = (bf16[192,256]{1,0:T(8,128)(2,1)S(1)}, bf16[192,256]{1,0:T(8,128)(2,1)}, u32[]{:S(2)}) copy-start(bf16[192,256]{1,0:T(8,128)(2,1)} %get-tuple-element.107.bias_ref) | copy-start | bytes 294916
  26.8 7.7 %collective-permute-start.6 = (bf16[16,2048]{1,0:T(8,128)(2,1)}, bf16[16,2048]{1,0:T(8,128)(2,1)S(1)}, u32[]{:S(2)}, u32[]{:S(2)}) collective-permute-start(bf16[16,2048]{1,0:T(8,128)(2,1)} %get-tuple-element.114), channel_id=1, source_target_pairs={{0,1},{1,2},{2,3},{3,4},{4,5},{5,6},{6,7},{7,8},{8,9},{9,10},{10,1... | collective-permute-start | bytes 196616 | tf_op jit(solution)/shard_map/ppermute | solution.py:385
  30.7 21.5 %collective-permute-start.5 = (bf16[192,2048]{1,0:T(8,128)(2,1)}, bf16[192,2048]{1,0:T(8,128)(2,1)}, u32[]{:S(2)}, u32[]{:S(2)}) collective-permute-start(bf16[192,2048]{1,0:T(8,128)(2,1)} %get-tuple-element.112), channel_id=1, source_target_pairs={{0,1},{1,2},{2,3},{3,4},{4,5},{5,6},{6,7},{7,8},{8,9},{9,10},{10,1... | collective-permute-start | bytes 2359304 | tf_op jit(solution)/shard_map/ppermute | solution.py:385
  34.6 17.7 %copy-start.2 = (bf16[1,16,128,128]{3,2,1,0:T(8,128)(2,1)S(1)}, bf16[1,16,128,128]{3,2,1,0:T(8,128)(2,1)}, u32[]{:S(2)}) copy-start(bf16[1,16,128,128]{3,2,1,0:T(8,128)(2,1)} %param.12) | copy-start | bytes 1572868
  34.6 17.7 %copy-start.1 = (bf16[1,192,2048]{2,1,0:T(8,128)(2,1)S(1)}, bf16[1,192,2048]{2,1,0:T(8,128)(2,1)}, u32[]{:S(2)}) copy-start(bf16[1,192,2048]{2,1,0:T(8,128)(2,1)} %param.9) | copy-start | bytes 2359300
  34.6 17.7 %copy-start.4 = (bf16[1,2048]{1,0:T(2,128)(2,1)S(1)}, bf16[1,2048]{1,0:T(2,128)(2,1)}, u32[]{:S(2)}) copy-start(bf16[1,2048]{1,0:T(2,128)(2,1)} %gain_ref.7) | copy-start | bytes 12292
  36.7 11.8 %copy-start.11 = (bf16[32,2048]{1,0:T(8,128)(2,1)}, bf16[32,2048]{1,0:T(8,128)(2,1)S(1)}, u32[]{:S(2)}) copy-start(bf16[32,2048]{1,0:T(8,128)(2,1)S(1)} %all-gather.6) | copy-start | bytes 393220 | tf_op jit(solution)/shard_map/while
  36.7 8.4 %collective-permute-start.1 = (bf16[2,16,2048]{2,1,0:T(8,128)(2,1)S(1)}, bf16[2,16,2048]{2,1,0:T(8,128)(2,1)S(1)}, u32[]{:S(2)}, u32[]{:S(2)}) collective-permute-start(bf16[2,16,2048]{2,1,0:T(8,128)(2,1)S(1)} %bitcast.33), channel_id=1, source_target_pairs={{0,64},{32,96},{64,128},{96,160},{128,192},{160,224},{192,256},{22... | collective-permute-start | bytes 393224 | tf_op jit(solution)/shard_map/while/body/ppermute | solution.py:392
  39.2 7.1 %collective-permute-start = (bf16[2,16,2048]{2,1,0:T(8,128)(2,1)S(1)}, bf16[2,16,2048]{2,1,0:T(8,128)(2,1)S(1)}, u32[]{:S(2)}, u32[]{:S(2)}) collective-permute-start(bf16[2,16,2048]{2,1,0:T(8,128)(2,1)S(1)} %bitcast.34), channel_id=1, source_target_pairs={{0,32},{32,64},{64,96},{96,128},{128,160},{160,192},{192,224},{224... | collective-permute-start | bytes 393224 | tf_op jit(solution)/shard_map/while/body/ppermute | solution.py:392
  45.0 3.4 %copy-start.6 = (bf16[2,16,2048]{2,1,0:T(8,128)(2,1)}, bf16[2,16,2048]{2,1,0:T(8,128)(2,1)S(1)}, u32[]{:S(2)}) copy-start(bf16[2,16,2048]{2,1,0:T(8,128)(2,1)S(1)} %collective-permute-done.1) | copy-start | bytes 393220 | tf_op jit(solution)/shard_map/while
  46.3 2.2 %copy-start.8 = (bf16[2,16,2048]{2,1,0:T(8,128)(2,1)}, bf16[2,16,2048]{2,1,0:T(8,128)(2,1)S(1)}, u32[]{:S(2)}) copy-start(bf16[2,16,2048]{2,1,0:T(8,128)(2,1)S(1)} %collective-permute-done) | copy-start | bytes 393220 | tf_op jit(solution)/shard_map/while
